TPU v7x, 32 devices: a whole 2x2x4 slice. The times are simulated.
32 devices in a mesh: fsdp: 4 (over z), context: 2 (over x), tensor: 4 (over y, core).
Axes of the slice: x: 2, y: 2, z: 4, core: 2. Of those that a mesh axis runs over, the one named last changes fastest.
Arguments:
- tokens: bfloat16 [2048, 1024], P(('fsdp', 'context')), may hold values from -6 to 6
- w_query: bfloat16 [1024, 1024], P(('fsdp', 'context'), 'tensor'), may hold values from -0.1875 to 0.1875
- key_projection_weight: bfloat16 [1024, 512], P(('fsdp', 'context'), 'tensor'), may hold values from -0.1875 to 0.1875
- value_projection_weight: bfloat16 [1024, 512], P(('fsdp', 'context'), 'tensor'), may hold values from -0.1875 to 0.1875
- w_out: bfloat16 [1024, 1024], P(('fsdp', 'context'), 'tensor'), may hold values from -0.75 to 0.75
- w_gate: bfloat16 [16, 1024, 512], P(None, ('fsdp', 'context'), 'tensor'), may hold values from -0.1875 to 0.1875
- w_up: bfloat16 [16, 1024, 512], P(None, ('fsdp', 'context'), 'tensor'), may hold values from -0.1875 to 0.1875
- w_down: bfloat16 [16, 1024, 512], P(None, ('fsdp', 'context'), 'tensor'), may hold values from -0.25 to 0.25
- norm_in: bfloat16 [1024], P(('fsdp', 'context')), may hold values from 0.5 to 1.5
- norm_mid: bfloat16 [1024], P(('fsdp', 'context')), may hold values from 0.5 to 1.5
- gate_values: float32 [2048, 8], P(('fsdp', 'context')), may hold values from 0.25 to 1
- routes: int32 [2048, 8], P(('fsdp', 'context')), may hold values from 0 to 15, all different within a row; in each aligned block of 256 rows (0 to 255, 256 to 511, ...) at most 144 rows name the same one
- doc_ids: int32 [4, 512], P('fsdp'), may hold values from 0 to 4, as said below
- cotangent: bfloat16 [2048, 1024], P(('fsdp', 'context')), may hold values from -6 to 6
Outputs:
- output: bfloat16 [2048, 1024], P(('fsdp', 'context'))
- d_tokens: bfloat16 [2048, 1024], P(('fsdp', 'context'))
- d_w_query: float32 [1024, 1024], P(('fsdp', 'context'), 'tensor')
- d_w_key: float32 [1024, 512], P(('fsdp', 'context'), 'tensor')
- d_w_value: float32 [1024, 512], P(('fsdp', 'context'), 'tensor')
- d_w_out: float32 [1024, 1024], P(('fsdp', 'context'), 'tensor')
- d_w_gate: float32 [16, 1024, 512], P(None, ('fsdp', 'context'), 'tensor')
- d_w_up: float32 [16, 1024, 512], P(None, ('fsdp', 'context'), 'tensor')
- d_w_down: float32 [16, 1024, 512], P(None, ('fsdp', 'context'), 'tensor')
- d_norm_in: float32 [1024], P(('fsdp', 'context'))
- d_norm_mid: float32 [1024], P(('fsdp', 'context'))
Inputs may be any that keep to these rules, and one draw needn't show every extreme that they name: `routes`: in each block of 256 rows (the rows of one device) no expert is named by more than 144 rows; each row names 8 different experts. `doc_ids`: along each group the numbers never fall and begin at 0; the tokens 512/2 - 1 and 256 lie in one document; one group, drawn from the seed, is a single document.
All inputs are finite; a program needn't handle non-finite values.
Results may differ from a plain program's by a relative error of at most 0.013.
Values may be sent and summed in bfloat16 or wider, within the bound.
A program may use at most 128 MiB of HBM per device.

v0:
```python
import math

import jax
import jax.numpy as jnp
from jax import lax
from jax.sharding import PartitionSpec as P

HEAD_SIZE = 64
TOP = 8
EXPERTS = 16
CAP = 144


EPSILON = 1e-06
CONTRACT_ROWS = (((0,), (0,)), ((), ()))
CONTRACT_COLUMNS = (((1,), (1,)), ((), ()))


def in_blocks(shard, dim, count):
    dims = shard.shape
    parts = shard.reshape(*dims[:dim], count, dims[dim] // count, *dims[dim + 1 :])
    return jnp.moveaxis(parts, dim, 0)


def sent_and_summed(shard, axis, dim):
    count = lax.axis_size(axis)
    parts = lax.all_to_all(in_blocks(shard, dim, count), axis, 0, 0, tiled=True)
    return jnp.sum(parts.astype(jnp.float32), axis=0)


def side_by_side(arrays, axis, dim, along):
    widths = [math.prod(a.shape[along:]) for a in arrays]
    both = jnp.concatenate(
        [a.reshape(*a.shape[:along], w) for a, w in zip(arrays, widths)], axis=along
    )
    out = sent_and_summed(both, axis, dim)
    parts = jnp.split(out, [sum(widths[:k]) for k in range(1, len(widths))], axis=along)
    return tuple((b.reshape(*out.shape[:along], *a.shape[along:]) for a, b in zip(arrays, parts)))


def rms_scale(values):
    return lax.rsqrt(jnp.mean(values * values, axis=-1, keepdims=True) + EPSILON)


def rotate(values, places, direction):
    head_count = values.shape[-1] // HEAD_SIZE
    shaped = values.reshape(values.shape[0], head_count, HEAD_SIZE)
    half_dim = HEAD_SIZE // 2
    frequency = 1.0 / 10000.0 ** (jnp.arange(half_dim, dtype=jnp.float32) * 2.0 / HEAD_SIZE)
    angles = places.astype(jnp.float32)[:, None, None] * frequency[None, None, :]
    cosine = jnp.cos(angles)
    sine_table = jnp.sin(angles) * direction
    first_half = shaped[..., :half_dim]
    second_half = shaped[..., half_dim:]
    turned = jnp.concatenate(
        [
            first_half * cosine - second_half * sine_table,
            second_half * cosine + first_half * sine_table,
        ],
        axis=-1,
    )
    return turned.reshape(values.shape)


def slot_table(route_rows):
    flat_routes = route_rows.reshape(-1)
    onehot_table = (flat_routes[:, None] == jnp.arange(EXPERTS, dtype=jnp.int32)[None, :]).astype(
        jnp.int32
    )
    earlier = jnp.cumsum(onehot_table, axis=0) - onehot_table
    places = jnp.sum(earlier * onehot_table, axis=1)
    slot_ids = flat_routes * CAP + places
    choice_ids = jnp.arange(flat_routes.shape[0], dtype=jnp.int32)
    source = jnp.zeros((EXPERTS * CAP,), jnp.int32).at[slot_ids].set(choice_ids)
    filled = jnp.zeros((EXPERTS * CAP,), jnp.int32).at[slot_ids].set(1) > 0
    return (slot_ids, source, filled)


def local_slots(source, filled, part_count, part_index):
    shaped_source = source.reshape(EXPERTS, part_count, -1)
    shaped_filled = filled.reshape(EXPERTS, part_count, -1)
    return (
        lax.dynamic_index_in_dim(shaped_source, part_index, 1, False).reshape(-1),
        lax.dynamic_index_in_dim(shaped_filled, part_index, 1, False).reshape(-1),
    )


def gather_rows(normed, part_source, part_filled):
    return jnp.where(part_filled[:, None], normed[part_source // TOP], jnp.zeros((), normed.dtype))


def scaled_rows(cotangent, flat_gates, part_source, part_filled):
    chosen_gates = jnp.where(part_filled, flat_gates[part_source], 0.0)
    picked_rows = cotangent[part_source // TOP]
    return (chosen_gates[:, None] * picked_rows.astype(jnp.float32)).astype(jnp.bfloat16)


def combine_slots(values, slot_ids, part_count, part_index, model_width):
    part_cap = CAP // part_count
    slot_place = slot_ids % CAP
    slot_expert = slot_ids // CAP
    inside = slot_place // part_cap == part_index
    row_ids = slot_expert * part_cap + slot_place % part_cap
    selected = jnp.where(inside[:, None], values[row_ids], 0.0)
    return selected.reshape(-1, TOP, model_width)


def expert_math(expert_rows, out_grads, gate_weight, up_weight, down_weight):
    gate_act = jnp.einsum(
        "gcd,gdf->gcf", expert_rows, gate_weight, preferred_element_type=jnp.float32
    )
    up_act = jnp.einsum("gcd,gdf->gcf", expert_rows, up_weight, preferred_element_type=jnp.float32)
    sigmoid_gate = jax.nn.sigmoid(gate_act)
    swish_act = gate_act * sigmoid_gate
    hidden = (swish_act * up_act).astype(jnp.bfloat16)
    expert_out = jnp.einsum("gcf,gdf->gcd", hidden, down_weight, preferred_element_type=jnp.float32)
    d_hidden = jnp.einsum(
        "gcd,gdf->gcf", out_grads, down_weight, preferred_element_type=jnp.float32
    )
    d_swish = sigmoid_gate * (1.0 + gate_act * (1.0 - sigmoid_gate))
    d_gate_act = (d_hidden * up_act * d_swish).astype(jnp.bfloat16)
    d_up_act = (d_hidden * swish_act).astype(jnp.bfloat16)
    d_expert_in = jnp.einsum(
        "gcf,gdf->gcd", d_gate_act, gate_weight, preferred_element_type=jnp.float32
    )
    d_expert_in = d_expert_in + jnp.einsum(
        "gcf,gdf->gcd", d_up_act, up_weight, preferred_element_type=jnp.float32
    )
    grad_gate = jnp.einsum(
        "gcd,gcf->gdf", expert_rows, d_gate_act, preferred_element_type=jnp.float32
    )
    grad_up = jnp.einsum("gcd,gcf->gdf", expert_rows, d_up_act, preferred_element_type=jnp.float32)
    grad_down = jnp.einsum("gcd,gcf->gdf", out_grads, hidden, preferred_element_type=jnp.float32)
    return (expert_out, d_expert_in, (grad_gate, grad_up, grad_down))


def spread_weight(weight, copies, part_count):
    return jnp.tile(jnp.repeat(weight, copies, axis=0), (1, 1, part_count))


def fold_grads(received, part_count, copies):
    shaped = received.reshape(part_count, EXPERTS, copies, received.shape[1], received.shape[2])
    return jnp.sum(shaped, axis=(0, 2))


def local(
    tokens,
    w_query,
    key_projection_weight,
    value_projection_weight,
    w_out,
    w_gate,
    w_up,
    w_down,
    norm_in,
    norm_mid,
    gate_values,
    routes,
    doc_ids,
    cotangent,
):
    query_weight, key_weight, value_weight, out_weight, gain_first, gain_second = (
        lax.all_gather(w_query, ("fsdp", "context"), axis=0, tiled=True),
        lax.all_gather(key_projection_weight, ("fsdp", "context"), axis=0, tiled=True),
        lax.all_gather(value_projection_weight, ("fsdp", "context"), axis=0, tiled=True),
        lax.all_gather(w_out, ("fsdp", "context"), axis=0, tiled=True),
        lax.all_gather(norm_in, ("fsdp", "context"), axis=0, tiled=True),
        lax.all_gather(norm_mid, ("fsdp", "context"), axis=0, tiled=True),
    )
    local_rows = tokens.shape[0]
    model_width = tokens.shape[1]
    context_index = lax.axis_index("context")
    documents = doc_ids[0]
    query_places = context_index * local_rows + jnp.arange(local_rows, dtype=jnp.int32)
    key_places = jnp.arange(documents.shape[0], dtype=jnp.int32)
    score_scale = HEAD_SIZE ** (-0.5)
    inputs = tokens.astype(jnp.float32)
    scale_in = rms_scale(inputs)
    gain_one = gain_first.astype(jnp.float32)
    gain_two = gain_second.astype(jnp.float32)
    normed_in = (inputs * scale_in * gain_one).astype(jnp.bfloat16)
    query_input = rotate(
        jnp.dot(normed_in, query_weight, preferred_element_type=jnp.float32), query_places, 1.0
    ).astype(jnp.bfloat16)
    key_local = rotate(
        jnp.dot(normed_in, key_weight, preferred_element_type=jnp.float32), query_places, 1.0
    ).astype(jnp.bfloat16)
    value_local = jnp.dot(normed_in, value_weight, preferred_element_type=jnp.float32).astype(
        jnp.bfloat16
    )
    keys_all, values_all = (
        lax.all_gather(key_local, "context", axis=0, tiled=True),
        lax.all_gather(value_local, "context", axis=0, tiled=True),
    )
    kv_heads = keys_all.shape[1] // HEAD_SIZE
    per_group = query_input.shape[1] // HEAD_SIZE // kv_heads
    query_head_rows = query_input.reshape(local_rows, kv_heads, per_group, HEAD_SIZE)
    key_head_rows = keys_all.reshape(keys_all.shape[0], kv_heads, HEAD_SIZE)
    value_head_rows = values_all.reshape(values_all.shape[0], kv_heads, HEAD_SIZE)
    visible = (key_places[None, :] <= query_places[:, None]) & (
        documents[None, :] == documents[query_places][:, None]
    )

    def masked_scores():
        raw_scores = (
            jnp.einsum(
                "rkgd,skd->kgrs", query_head_rows, key_head_rows, preferred_element_type=jnp.float32
            )
            * score_scale
        )
        return jnp.where(visible, raw_scores, -1e30)

    masked = masked_scores()
    highest = jnp.max(masked, axis=-1, keepdims=True)
    exponent = jnp.exp(masked - highest)
    totals = jnp.sum(exponent, axis=-1, keepdims=True)
    probs_low = (exponent / totals).astype(jnp.bfloat16)
    context = jnp.einsum(
        "kgrs,skd->rkgd", probs_low, value_head_rows, preferred_element_type=jnp.float32
    )
    context = context.reshape(local_rows, -1).astype(jnp.bfloat16)
    attn_part = lax.dot_general(
        context, out_weight, CONTRACT_COLUMNS, preferred_element_type=jnp.float32
    )
    attended = lax.psum(attn_part, "tensor")
    hidden_state = inputs + attended
    scale_mid = rms_scale(hidden_state)
    normed_mid = (hidden_state * scale_mid * gain_two).astype(jnp.bfloat16)
    d_output = cotangent.astype(jnp.float32)
    flat_gates = gate_values.reshape(-1)
    slot_ids, source, filled = slot_table(routes)
    owners = lax.axis_size(("fsdp", "context"))
    part_count = lax.axis_size("tensor")
    part_index = lax.axis_index("tensor")
    per_owner = max(EXPERTS // owners, 1)
    copies = max(owners // EXPERTS, 1)
    part_source, part_filled = local_slots(source, filled, part_count, part_index)
    send_rows = gather_rows(normed_mid, part_source, part_filled).reshape(
        owners, per_owner, -1, model_width
    )
    send_grads = scaled_rows(cotangent, flat_gates, part_source, part_filled).reshape(
        owners, per_owner, -1, model_width
    )
    owner_gate, owner_up, owner_down = (
        lax.all_to_all(
            lax.all_to_all(
                spread_weight(w_gate, copies, part_count),
                ("fsdp", "context"),
                split_axis=0,
                concat_axis=1,
                tiled=True,
            ),
            "tensor",
            split_axis=2,
            concat_axis=2,
            tiled=True,
        ),
        lax.all_to_all(
            lax.all_to_all(
                spread_weight(w_up, copies, part_count),
                ("fsdp", "context"),
                split_axis=0,
                concat_axis=1,
                tiled=True,
            ),
            "tensor",
            split_axis=2,
            concat_axis=2,
            tiled=True,
        ),
        lax.all_to_all(
            lax.all_to_all(
                spread_weight(w_down, copies, part_count),
                ("fsdp", "context"),
                split_axis=0,
                concat_axis=1,
                tiled=True,
            ),
            "tensor",
            split_axis=2,
            concat_axis=2,
            tiled=True,
        ),
    )
    owner_rows, owner_grads = (
        lax.all_to_all(send_rows, ("fsdp", "context"), split_axis=0, concat_axis=2, tiled=True),
        lax.all_to_all(send_grads, ("fsdp", "context"), split_axis=0, concat_axis=2, tiled=True),
    )
    owner_rows = owner_rows.reshape(per_owner, -1, model_width)
    owner_grads = owner_grads.reshape(per_owner, -1, model_width)
    out_rows, in_grads, weight_grads = expert_math(
        owner_rows, owner_grads, owner_gate, owner_up, owner_down
    )
    back_out, back_in = (
        lax.all_to_all(
            out_rows.reshape(1, per_owner, -1, model_width),
            ("fsdp", "context"),
            split_axis=2,
            concat_axis=0,
            tiled=True,
        ),
        lax.all_to_all(
            in_grads.reshape(1, per_owner, -1, model_width),
            ("fsdp", "context"),
            split_axis=2,
            concat_axis=0,
            tiled=True,
        ),
    )
    back_out = back_out.reshape(-1, model_width)
    back_in = back_in.reshape(-1, model_width)
    picked = combine_slots(back_out, slot_ids, part_count, part_index, model_width)
    moe_part = jnp.sum(gate_values[:, :, None] * picked, axis=1)
    moe_mixed = lax.psum(moe_part.astype(jnp.bfloat16), "tensor").astype(jnp.float32)
    output = (hidden_state + moe_mixed).astype(jnp.bfloat16)
    d_mid_part = jnp.sum(
        combine_slots(back_in, slot_ids, part_count, part_index, model_width), axis=1
    )
    d_mid = lax.psum(d_mid_part, "tensor")
    d_gain_mid = jnp.sum(d_mid * hidden_state * scale_mid, axis=0)
    d_hidden_state = (
        d_output
        + d_mid * gain_two * scale_mid
        - hidden_state
        * scale_mid**3
        * jnp.mean(gain_two * d_mid * hidden_state, axis=-1, keepdims=True)
    )
    d_attended = d_hidden_state.astype(jnp.bfloat16)
    d_out_weight = lax.dot_general(
        d_attended, context, CONTRACT_ROWS, preferred_element_type=jnp.float32
    )
    d_context = jnp.dot(d_attended, out_weight, preferred_element_type=jnp.float32).astype(
        jnp.bfloat16
    )
    d_context_heads = d_context.reshape(local_rows, kv_heads, per_group, HEAD_SIZE)
    attn_probs = jnp.exp(masked_scores() - highest) / totals
    d_probs = jnp.einsum(
        "rkgd,skd->kgrs", d_context_heads, value_head_rows, preferred_element_type=jnp.float32
    )
    d_scores = attn_probs * (d_probs - jnp.sum(attn_probs * d_probs, axis=-1, keepdims=True))
    d_scores_low = jnp.where(visible, d_scores, 0.0).astype(jnp.bfloat16)
    d_query_turned = jnp.einsum(
        "kgrs,skd->rkgd", d_scores_low, key_head_rows, preferred_element_type=jnp.float32
    )
    d_query_turned = d_query_turned.reshape(local_rows, -1) * score_scale
    d_keys = jnp.einsum(
        "kgrs,rkgd->skd", d_scores_low, query_head_rows, preferred_element_type=jnp.float32
    )
    d_keys = d_keys.reshape(keys_all.shape[0], -1) * score_scale
    d_values = jnp.einsum(
        "kgrs,rkgd->skd", probs_low, d_context_heads, preferred_element_type=jnp.float32
    )
    d_values = d_values.reshape(values_all.shape[0], -1)
    d_key_local, d_value_local = (
        lax.psum_scatter(d_keys, "context", scatter_dimension=0, tiled=True),
        lax.psum_scatter(d_values, "context", scatter_dimension=0, tiled=True),
    )
    d_query = rotate(d_query_turned, query_places, -1.0).astype(jnp.bfloat16)
    d_key = rotate(d_key_local, query_places, -1.0).astype(jnp.bfloat16)
    d_value = d_value_local.astype(jnp.bfloat16)
    d_query_weight = lax.dot_general(
        normed_in, d_query, CONTRACT_ROWS, preferred_element_type=jnp.float32
    )
    d_key_weight = lax.dot_general(
        normed_in, d_key, CONTRACT_ROWS, preferred_element_type=jnp.float32
    )
    d_value_weight = lax.dot_general(
        normed_in, d_value, CONTRACT_ROWS, preferred_element_type=jnp.float32
    )
    d_in_part = lax.dot_general(
        d_query, query_weight, CONTRACT_COLUMNS, preferred_element_type=jnp.float32
    )
    d_in_part = d_in_part + lax.dot_general(
        d_key, key_weight, CONTRACT_COLUMNS, preferred_element_type=jnp.float32
    )
    d_in_part = d_in_part + lax.dot_general(
        d_value, value_weight, CONTRACT_COLUMNS, preferred_element_type=jnp.float32
    )
    d_in = lax.psum(d_in_part, "tensor")
    d_gain_in = jnp.sum(d_in * inputs * scale_in, axis=0)
    d_inputs = (
        d_hidden_state
        + d_in * gain_one * scale_in
        - inputs * scale_in**3 * jnp.mean(gain_one * d_in * inputs, axis=-1, keepdims=True)
    )
    owned_query, owned_key, owned_value, owned_out, owned_gain_in, owned_gain_mid = side_by_side(
        (
            d_query_weight.astype(jnp.bfloat16),
            d_key_weight.astype(jnp.bfloat16),
            d_value_weight.astype(jnp.bfloat16),
            d_out_weight.astype(jnp.bfloat16),
            d_gain_in.astype(jnp.bfloat16),
            d_gain_mid.astype(jnp.bfloat16),
        ),
        ("fsdp", "context"),
        0,
        1,
    )
    summed_gate, summed_up, summed_down = (
        lax.all_to_all(
            lax.all_to_all(
                weight_grads[0].astype(jnp.bfloat16),
                ("fsdp", "context"),
                split_axis=1,
                concat_axis=0,
                tiled=True,
            ),
            "tensor",
            split_axis=2,
            concat_axis=0,
            tiled=True,
        ).astype(jnp.float32),
        lax.all_to_all(
            lax.all_to_all(
                weight_grads[1].astype(jnp.bfloat16),
                ("fsdp", "context"),
                split_axis=1,
                concat_axis=0,
                tiled=True,
            ),
            "tensor",
            split_axis=2,
            concat_axis=0,
            tiled=True,
        ).astype(jnp.float32),
        lax.all_to_all(
            lax.all_to_all(
                weight_grads[2].astype(jnp.bfloat16),
                ("fsdp", "context"),
                split_axis=1,
                concat_axis=0,
                tiled=True,
            ),
            "tensor",
            split_axis=2,
            concat_axis=0,
            tiled=True,
        ).astype(jnp.float32),
    )
    owned_gate = fold_grads(summed_gate, part_count, copies)
    owned_up = fold_grads(summed_up, part_count, copies)
    owned_down = fold_grads(summed_down, part_count, copies)
    return (
        output,
        d_inputs.astype(jnp.bfloat16),
        owned_query,
        owned_key,
        owned_value,
        owned_out,
        owned_gate,
        owned_up,
        owned_down,
        owned_gain_in,
        owned_gain_mid,
    )


def solution(mesh):
    placed = (
        P(("fsdp", "context"), None),
        P(("fsdp", "context"), "tensor"),
        P(("fsdp", "context"), "tensor"),
        P(("fsdp", "context"), "tensor"),
        P(("fsdp", "context"), "tensor"),
        P(None, ("fsdp", "context"), "tensor"),
        P(None, ("fsdp", "context"), "tensor"),
        P(None, ("fsdp", "context"), "tensor"),
        P(("fsdp", "context")),
        P(("fsdp", "context")),
        P(("fsdp", "context"), None),
        P(("fsdp", "context"), None),
        P("fsdp", None),
        P(("fsdp", "context"), None),
    )
    return jax.shard_map(
        local,
        mesh=mesh,
        in_specs=placed,
        out_specs=(
            P(("fsdp", "context"), None),
            P(("fsdp", "context"), None),
            P(("fsdp", "context"), "tensor"),
            P(("fsdp", "context"), "tensor"),
            P(("fsdp", "context"), "tensor"),
            P(("fsdp", "context"), "tensor"),
            P(None, ("fsdp", "context"), "tensor"),
            P(None, ("fsdp", "context"), "tensor"),
            P(None, ("fsdp", "context"), "tensor"),
            P(("fsdp", "context")),
            P(("fsdp", "context")),
        ),
        check_vma=False,
    )
```

profile of v0, /device:TPU:0, one launch (start us, length us, event | category | flops | bytes accessed | tf_op | source)
XLA Modules:
  0.0 1101.1 jit_solution(16774020764416832680)
XLA Ops:
  8.3 4.5 reduce-window.6
  15.4 8.1 scatter_custom_fusion.1
  23.5 8.1 scatter_custom_fusion
  32.1 3.6 gather_fusion.3
  43.1 7.4 all-to-all-start.8
  51.4 33.0 %all-gather = bf16[8,1,128]{2,1,0:T(2,128)(2,1)S(1)} all-gather(bf16[1,1,128]{2,1,0:T(2,128)(2,1)S(1)} %bitcast.279), channel_id=1, replica_groups=mesh['fsdp'=4,'context'=2,'tensor'=4] {'fsdp','context'}, dimensions={0}, use_global_device_ids=true | all-gather | bytes 2304 | tf_op jit(solution)/shard_map/all_gather | solution.py:167
  84.4 32.5 %all_gather.27 = bf16[1024,128]{1,0:T(8,128)(2,1)S(1)} all-gather(bf16[128,128]{1,0:T(8,128)(2,1)S(1)} %copy-done.40), channel_id=1, replica_groups=mesh['fsdp'=4,'context'=2,'tensor'=4] {'fsdp','context'}, dimensions={0}, use_global_device_ids=true | all-gather | bytes 294912 | tf_op jit(solution)/shard_map/all_gather | solution.py:164
  118.2 4.9 all_gather.28
  123.2 31.0 %all_gather.25 = bf16[1024,128]{1,0:T(8,128)(2,1)S(1)} all-gather(bf16[128,128]{1,0:T(8,128)(2,1)S(1)} %copy-done.41), channel_id=1, replica_groups=mesh['fsdp'=4,'context'=2,'tensor'=4] {'fsdp','context'}, dimensions={0}, use_global_device_ids=true | all-gather | bytes 294912 | tf_op jit(solution)/shard_map/all_gather | solution.py:165
  154.5 5.3 all_gather.26
  159.9 31.7 %all_gather.29 = bf16[1024,256]{1,0:T(8,128)(2,1)S(1)} all-gather(bf16[128,256]{1,0:T(8,128)(2,1)S(1)} %copy-done.34), channel_id=1, replica_groups=mesh['fsdp'=4,'context'=2,'tensor'=4] {'fsdp','context'}, dimensions={0}, use_global_device_ids=true | all-gather | bytes 589824 | tf_op jit(solution)/shard_map/all_gather | solution.py:163
  198.3 31.3 %all_gather.30 = bf16[1024,256]{1,0:T(8,128)(2,1)S(1)} all-gather(bf16[128,256]{1,0:T(8,128)(2,1)S(1)} %copy-done.35), channel_id=1, replica_groups=mesh['fsdp'=4,'context'=2,'tensor'=4] {'fsdp','context'}, dimensions={0}, use_global_device_ids=true | all-gather | bytes 589824 | tf_op jit(solution)/shard_map/all_gather | solution.py:166
  231.8 19.9 %all-gather.1 = bf16[8,1,128]{2,1,0:T(2,128)(2,1)S(1)} all-gather(bf16[1,1,128]{2,1,0:T(2,128)(2,1)S(1)} %bitcast.280), channel_id=1, replica_groups=mesh['fsdp'=4,'context'=2,'tensor'=4] {'fsdp','context'}, dimensions={0}, use_global_device_ids=true | all-gather | bytes 2304 | tf_op jit(solution)/shard_map/all_gather | solution.py:168
  251.7 16.5 %all-reduce.5.cloned.1.call-done = f32[256,1024]{1,0:T(8,128)} async-done(((f32[256,1024]{1,0:T(8,128)}), f32[256,1024]{1,0:T(8,128)}) %all-reduce.5.cloned.1.call-update) | async-done | bytes 1048592 | tf_op jit(solution)/shard_map/psum | solution.py:225
  278.2 5.5 all-to-all-start
  287.8 24.2 %all-to-all-done = bf16[8,2,36,1024]{3,1,2,0:T(2,128)(2,1)} async-done(((bf16[8,2,36,1024]{3,1,2,0:T(2,128)(2,1)}), bf16[8,2,36,1024]{3,1,2,0:T(2,128)(2,1)}, u32[]{:S(2)}, u32[]{:S(2)}) %all-to-all-start) | async-done | bytes 1179680 | tf_op jit(solution)/shard_map/all_to_all | solution.py:286
  312.1 4.3 all-to-all-start.1
  320.6 43.5 %all-to-all-done.1 = bf16[16,128,512]{2,1,0:T(8,128)(2,1)} async-done(((bf16[16,128,512]{2,1,0:T(8,128)(2,1)}), bf16[16,128,512]{2,1,0:T(8,128)(2,1)}, u32[]{:S(2)}, u32[]{:S(2)}) %all-to-all-start.1) | async-done | bytes 2097184 | tf_op jit(solution)/shard_map/all_to_all | solution.py:246
  364.1 4.4 all-to-all-start.3
  372.6 43.7 %all-to-all-done.3 = bf16[16,128,512]{2,1,0:T(8,128)(2,1)} async-done(((bf16[16,128,512]{2,1,0:T(8,128)(2,1)}), bf16[16,128,512]{2,1,0:T(8,128)(2,1)}, u32[]{:S(2)}, u32[]{:S(2)}) %all-to-all-start.3) | async-done | bytes 2097184 | tf_op jit(solution)/shard_map/all_to_all | solution.py:259
  416.2 3.6 all-to-all-start.5
  423.0 6.3 copy.197
  429.3 39.0 %all-to-all-done.5 = bf16[16,128,512]{2,1,0:T(8,128)(2,1)S(1)} async-done(((bf16[16,128,512]{2,1,0:T(8,128)(2,1)}), bf16[16,128,512]{2,1,0:T(8,128)(2,1)S(1)}, u32[]{:S(2)}, u32[]{:S(2)}) %all-to-all-start.5) | async-done | bytes 2097184 | tf_op jit(solution)/shard_map/all_to_all | solution.py:272
  469.6 3.6 all-to-all-start.2
  476.4 6.3 copy.205
  482.6 16.2 %all-to-all-done.2 = bf16[2,1024,512]{1,0,2:T(2,128)(2,1)S(1)} async-done(((bf16[2,1024,512]{1,0,2:T(2,128)(2,1)}), bf16[2,1024,512]{1,0,2:T(2,128)(2,1)S(1)}, u32[]{:S(2)}, u32[]{:S(2)}) %all-to-all-start.2) | async-done | bytes 2097184 | tf_op jit(solution)/shard_map/all_to_all | solution.py:245
  500.3 4.5 all-to-all-start.6
  506.5 4.1 copy.201
  510.6 19.9 %all-to-all-done.6 = bf16[2,1024,512]{1,0,2:T(2,128)(2,1)} async-done(((bf16[2,1024,512]{1,0,2:T(2,128)(2,1)}), bf16[2,1024,512]{1,0,2:T(2,128)(2,1)}, u32[]{:S(2)}, u32[]{:S(2)}) %all-to-all-start.6) | async-done | bytes 2097184 | tf_op jit(solution)/shard_map/all_to_all | solution.py:271
  530.5 4.9 all-to-all-start.4
  535.3 4.7 copy.199
  540.1 6.1 copy.206
  546.2 3.8 fusion.28
  553.1 7.9 all-to-all-done.4
  561.1 6.2 copy.203
  567.2 4.8 multiply_convert_fusion.3
  578.9 4.3 all-to-all-start.15
  589.5 42.1 %all-to-all-done.15 = bf16[2,1024,512]{2,0,1:T(2,128)(2,1)} async-done(((bf16[2,1024,512]{2,0,1:T(2,128)(2,1)}), bf16[2,1024,512]{2,0,1:T(2,128)(2,1)}, u32[]{:S(2)}, u32[]{:S(2)}) %all-to-all-start.15) | async-done | bytes 2097184 | tf_op jit(solution)/shard_map/all_to_all | solution.py:427
  631.6 4.5 all-to-all-start.13
  641.9 41.9 %all-to-all-done.13 = bf16[2,1024,512]{2,0,1:T(2,128)(2,1)} async-done(((bf16[2,1024,512]{2,0,1:T(2,128)(2,1)}), bf16[2,1024,512]{2,0,1:T(2,128)(2,1)}, u32[]{:S(2)}, u32[]{:S(2)}) %all-to-all-start.13) | async-done | bytes 2097184 | tf_op jit(solution)/shard_map/all_to_all | solution.py:414
  683.9 4.4 all-to-all-start.7
  694.4 47.2 %all-to-all-done.7 = f32[1,2,288,1024]{3,1,0,2:T(2,128)} async-done(((f32[1,2,288,1024]{3,1,0,2:T(2,128)}), f32[1,2,288,1024]{3,1,0,2:T(2,128)}, u32[]{:S(2)}, u32[]{:S(2)}) %all-to-all-start.7) | async-done | bytes 2359328 | tf_op jit(solution)/shard_map/all_to_all | solution.py:295
  741.7 3.6 all-to-all-start.9
  751.6 47.8 %all-to-all-done.9 = f32[1,2,288,1024]{3,1,0,2:T(2,128)S(1)} async-done(((f32[1,2,288,1024]{3,1,0,2:T(2,128)}), f32[1,2,288,1024]{3,1,0,2:T(2,128)S(1)}, u32[]{:S(2)}, u32[]{:S(2)}) %all-to-all-start.9) | async-done | bytes 2359328 | tf_op jit(solution)/shard_map/all_to_all | solution.py:302
  800.8 4.4 all-to-all-start.11
  807.0 3.9 copy.208
  812.8 3.9 copy.216
  819.6 13.4 %gather_fusion.5 = f32[2048,1024]{1,0:T(8,128)} fusion(f32[576,1024]{1,0:T(8,128)} %reshape.609, s32[2048]{0:T(1024)S(1)} %broadcast_clamp_fusion), kind=kCustom, calls=%fused_computation.5 | custom fusion | bytes 16785408 | tf_op jit(solution)/shard_map/gather | solution.py:104
  833.0 9.8 gather_fusion.2
  842.8 9.8 fusion.2
  858.0 4.6 all-to-all-start.16
  862.7 37.6 %all-reduce.9.cloned.1.call-done = f32[256,1024]{1,0:T(8,128)} async-done(((f32[256,1024]{1,0:T(8,128)}), f32[256,1024]{1,0:T(8,128)}) %all-reduce.9.cloned.1.call-update) | async-done | bytes 1048592 | tf_op jit(solution)/shard_map/psum | solution.py:319
  901.8 35.3 %all-reduce.7.cloned.1.call-done = bf16[256,1024]{1,0:T(8,128)(2,1)} async-done(((bf16[256,1024]{1,0:T(8,128)(2,1)}), bf16[256,1024]{1,0:T(8,128)(2,1)}) %all-reduce.7.cloned.1.call-update) | async-done | bytes 524304 | tf_op jit(solution)/shard_map/psum | solution.py:314
  941.9 5.0 fusion.11
  950.3 4.6 copy.235
  954.9 4.5 all-to-all-start.14
  963.2 4.5 copy.230
  969.7 4.2 convolution_multiply_fusion
  975.9 9.2 all-to-all-done.14
  985.1 4.5 all-to-all-start.12
  996.9 42.6 %all-reduce.11.cloned.1.call-done = f32[256,1024]{1,0:T(8,128)} async-done(((f32[256,1024]{1,0:T(8,128)}), f32[256,1024]{1,0:T(8,128)}) %all-reduce.11.cloned.1.call-update) | async-done | bytes 1048592 | tf_op jit(solution)/shard_map/psum | solution.py:379
  1041.1 5.1 concatenate.36
  1046.1 5.5 all-to-all-start.10
  1064.1 24.5 %all-to-all-done.10 = bf16[8,128,770]{1,2,0:T(8,128)(2,1)} async-done(((bf16[8,128,770]{1,2,0:T(8,128)(2,1)}), bf16[8,128,770]{1,2,0:T(8,128)(2,1)}, u32[]{:S(2)}, u32[]{:S(2)}) %all-to-all-start.10) | async-done | bytes 1576992 | tf_op jit(solution)/shard_map/all_to_all | solution.py:27
  (255 shorter events, 147.6 us)
Async XLA Ops:
  14.4 17.7 %copy-start.12 = (f32[256,8]{1,0:T(8,128)}, f32[256,8]{1,0:T(8,128)S(1)}, u32[]{:S(2)}) copy-start(f32[256,8]{1,0:T(8,128)S(1)} %copy.191) | copy-start | bytes 24580
  31.7 8.8 copy-start.38
  32.1 3.7 copy-start.1
  40.8 9.8 copy-start.5
  40.8 10.6 copy-start.48
  40.8 43.6 %copy-start.40 = (bf16[128,128]{1,0:T(8,128)(2,1)S(1)}, bf16[128,128]{1,0:T(8,128)(2,1)}, u32[]{:S(2)}) copy-start(bf16[128,128]{1,0:T(8,128)(2,1)} %param.16) | copy-start | bytes 98308
  43.1 80.1 %copy-start.41 = (bf16[128,128]{1,0:T(8,128)(2,1)S(1)}, bf16[128,128]{1,0:T(8,128)(2,1)}, u32[]{:S(2)}) copy-start(bf16[128,128]{1,0:T(8,128)(2,1)} %param.17) | copy-start | bytes 98308
  43.1 235.1 %all-to-all-start.8 = ((bf16[8,2,36,1024]{3,1,2,0:T(2,128)(2,1)}), bf16[8,2,36,1024]{3,1,2,0:T(2,128)(2,1)}, u32[]{:S(2)}, u32[]{:S(2)}) async-start(bf16[8,2,36,1024]{3,1,2,0:T(2,128)(2,1)} %copy.210), calls=%async_computation.8 | async-start | bytes 2359296 | tf_op jit(solution)/shard_map/all_to_all | solution.py:287
  50.5 217.8 %all-reduce.5.cloned.1.call-start = ((), (), s32[]{:S(2)}) async-start(), calls=%async_computation.19 | async-start | bytes 2097152 | tf_op jit(solution)/shard_map/psum | solution.py:225
  50.7 109.2 %copy-start.34 = (bf16[128,256]{1,0:T(8,128)(2,1)S(1)}, bf16[128,256]{1,0:T(8,128)(2,1)}, u32[]{:S(2)}) copy-start(bf16[128,256]{1,0:T(8,128)(2,1)} %param.15) | copy-start | bytes 196612
  51.4 140.2 %copy-start.44 = (f32[256]{0:T(256)}, f32[256]{0:T(256)S(1)}, u32[]{:S(2)}) copy-start(f32[256]{0:T(256)S(1)} %get-tuple-element.57) | copy-start | bytes 3076
  84.4 107.2 %copy-start.36 = (f32[8,1,128]{2,1,0:T(1,128)}, f32[8,1,128]{2,1,0:T(1,128)S(1)}, u32[]{:S(2)}) copy-start(f32[8,1,128]{2,1,0:T(1,128)S(1)} %convert_element_type.244) | copy-start | bytes 12292
  117.0 6.2 copy-start.14
  117.8 74.3 %copy-start.17 = (f32[256,32]{0,1:T(8,128)}, f32[256,32]{0,1:T(8,128)S(1)}, u32[]{:S(2)}) copy-start(f32[256,32]{0,1:T(8,128)S(1)} %get-tuple-element.55) | copy-start | bytes 98308
  123.2 73.3 %copy-start.27 = (bf16[512,128]{0,1:T(8,128)(2,1)}, bf16[512,128]{0,1:T(8,128)(2,1)S(1)}, u32[]{:S(2)}) copy-start(bf16[512,128]{0,1:T(8,128)(2,1)S(1)} %all_gather.28) | copy-start | bytes 393220
  154.1 5.7 copy-start.16
  154.1 38.0 %copy-start = (s32[1,512]{1,0:T(1,128)S(1)}, s32[1,512]{1,0:T(1,128)}, u32[]{:S(2)}) copy-start(s32[1,512]{1,0:T(1,128)} %param.26) | copy-start | bytes 6148
  159.9 36.6 %copy-start.21 = (bf16[512,128]{0,1:T(8,128)(2,1)}, bf16[512,128]{0,1:T(8,128)(2,1)S(1)}, u32[]{:S(2)}) copy-start(bf16[512,128]{0,1:T(8,128)(2,1)S(1)} %copy.189) | copy-start | bytes 393220
  191.6 4.9 copy-start.11
  194.3 4.0 copy-start.29
  194.3 4.0 copy-start.31
  198.3 71.4 %copy-start.23 = (bf16[2,64,2,256]{3,1,2,0:T(8,128)(2,1)}, bf16[2,64,2,256]{3,1,2,0:T(8,128)(2,1)S(1)}, u32[]{:S(2)}) copy-start(bf16[2,64,2,256]{3,1,2,0:T(8,128)(2,1)S(1)} %convolution_convert_fusion.8) | copy-start | bytes 393220
  198.3 33.5 %copy-start.49 = (bf16[128]{0:T(256)(128)(2,1)S(1)}, bf16[128]{0:T(256)(128)(2,1)}, u32[]{:S(2)}) copy-start(bf16[128]{0:T(256)(128)(2,1)} %param.23) | copy-start | bytes 772
  278.2 33.9 %all-to-all-start = ((bf16[8,2,36,1024]{3,1,2,0:T(2,128)(2,1)}), bf16[8,2,36,1024]{3,1,2,0:T(2,128)(2,1)}, u32[]{:S(2)}, u32[]{:S(2)}) async-start(bf16[8,2,36,1024]{3,1,2,0:T(2,128)(2,1)} %copy.195), calls=%async_computation | async-start | bytes 2359296 | tf_op jit(solution)/shard_map/all_to_all | solution.py:286
  312.1 52.0 %all-to-all-start.1 = ((bf16[16,128,512]{2,1,0:T(8,128)(2,1)}), bf16[16,128,512]{2,1,0:T(8,128)(2,1)}, u32[]{:S(2)}, u32[]{:S(2)}) async-start(bf16[16,128,512]{2,1,0:T(8,128)(2,1)} %tile.25), calls=%async_computation.1 | async-start | bytes 4194304 | tf_op jit(solution)/shard_map/all_to_all | solution.py:246
  364.1 52.2 %all-to-all-start.3 = ((bf16[16,128,512]{2,1,0:T(8,128)(2,1)}), bf16[16,128,512]{2,1,0:T(8,128)(2,1)}, u32[]{:S(2)}, u32[]{:S(2)}) async-start(bf16[16,128,512]{2,1,0:T(8,128)(2,1)} %tile.27), calls=%async_computation.3 | async-start | bytes 4194304 | tf_op jit(solution)/shard_map/all_to_all | solution.py:259
  416.2 52.0 %all-to-all-start.5 = ((bf16[16,128,512]{2,1,0:T(8,128)(2,1)}), bf16[16,128,512]{2,1,0:T(8,128)(2,1)S(1)}, u32[]{:S(2)}, u32[]{:S(2)}) async-start(bf16[16,128,512]{2,1,0:T(8,128)(2,1)} %tile.29), calls=%async_computation.5 | async-start | bytes 4194304 | tf_op jit(solution)/shard_map/all_to_all | solution.py:272
  469.6 29.3 %all-to-all-start.2 = ((bf16[2,1024,512]{1,0,2:T(2,128)(2,1)}), bf16[2,1024,512]{1,0,2:T(2,128)(2,1)S(1)}, u32[]{:S(2)}, u32[]{:S(2)}) async-start(bf16[2,1024,512]{1,0,2:T(2,128)(2,1)} %copy.197), calls=%async_computation.2 | async-start | bytes 4194304 | tf_op jit(solution)/shard_map/all_to_all | solution.py:245
  500.3 30.2 %all-to-all-start.6 = ((bf16[2,1024,512]{1,0,2:T(2,128)(2,1)}), bf16[2,1024,512]{1,0,2:T(2,128)(2,1)}, u32[]{:S(2)}, u32[]{:S(2)}) async-start(bf16[2,1024,512]{1,0,2:T(2,128)(2,1)} %copy.205), calls=%async_computation.6 | async-start | bytes 4194304 | tf_op jit(solution)/shard_map/all_to_all | solution.py:271
  530.5 30.6 %all-to-all-start.4 = ((bf16[2,1024,512]{1,0,2:T(2,128)(2,1)}), bf16[2,1024,512]{1,0,2:T(2,128)(2,1)}, u32[]{:S(2)}, u32[]{:S(2)}) async-start(bf16[2,1024,512]{1,0,2:T(2,128)(2,1)} %copy.201), calls=%async_computation.4 | async-start | bytes 4194304 | tf_op jit(solution)/shard_map/all_to_all | solution.py:258
  578.9 52.7 %all-to-all-start.15 = ((bf16[2,1024,512]{2,0,1:T(2,128)(2,1)}), bf16[2,1024,512]{2,0,1:T(2,128)(2,1)}, u32[]{:S(2)}, u32[]{:S(2)}) async-start(bf16[2,1024,512]{2,0,1:T(2,128)(2,1)} %copy.237), calls=%async_computation.17 | async-start | bytes 4194304 | tf_op jit(solution)/shard_map/all_to_all | solution.py:427
  631.6 52.3 %all-to-all-start.13 = ((bf16[2,1024,512]{2,0,1:T(2,128)(2,1)}), bf16[2,1024,512]{2,0,1:T(2,128)(2,1)}, u32[]{:S(2)}, u32[]{:S(2)}) async-start(bf16[2,1024,512]{2,0,1:T(2,128)(2,1)} %copy.232), calls=%async_computation.15 | async-start | bytes 4194304 | tf_op jit(solution)/shard_map/all_to_all | solution.py:414
  683.9 57.8 %all-to-all-start.7 = ((f32[1,2,288,1024]{3,1,0,2:T(2,128)}), f32[1,2,288,1024]{3,1,0,2:T(2,128)}, u32[]{:S(2)}, u32[]{:S(2)}) async-start(f32[1,2,288,1024]{3,1,0,2:T(2,128)} %copy.207), calls=%async_computation.7 | async-start | bytes 4718592 | tf_op jit(solution)/shard_map/all_to_all | solution.py:295
  688.3 2.0 copy-start.6
  688.3 2.0 copy-start.19
  741.7 57.7 %all-to-all-start.9 = ((f32[1,2,288,1024]{3,1,0,2:T(2,128)}), f32[1,2,288,1024]{3,1,0,2:T(2,128)S(1)}, u32[]{:S(2)}, u32[]{:S(2)}) async-start(f32[1,2,288,1024]{3,1,0,2:T(2,128)} %copy.215), calls=%async_computation.9 | async-start | bytes 4718592 | tf_op jit(solution)/shard_map/all_to_all | solution.py:302
  799.3 1.4 copy-start.4
  800.8 57.2 %all-to-all-start.11 = ((bf16[2,1024,512]{2,0,1:T(2,128)(2,1)}), bf16[2,1024,512]{2,0,1:T(2,128)(2,1)}, u32[]{:S(2)}, u32[]{:S(2)}) async-start(bf16[2,1024,512]{2,0,1:T(2,128)(2,1)} %copy.227), calls=%async_computation.13 | async-start | bytes 4194304 | tf_op jit(solution)/shard_map/all_to_all | solution.py:401
  805.2 95.1 %all-reduce.9.cloned.1.call-start = ((), (), s32[]{:S(2)}) async-start(), calls=%async_computation.21 | async-start | bytes 2097152 | tf_op jit(solution)/shard_map/psum | solution.py:319
  833.0 9.9 copy-start.13
  852.7 84.4 %all-reduce.7.cloned.1.call-start = ((), (), s32[]{:S(2)}) async-start(), calls=%async_computation.20 | async-start | bytes 1048576 | tf_op jit(solution)/shard_map/psum | solution.py:314
  858.0 42.4 %copy-start.3 = (f32[256,1024]{1,0:T(8,128)S(1)}, f32[256,1024]{1,0:T(8,128)}, u32[]{:S(2)}) copy-start(f32[256,1024]{1,0:T(8,128)} %copy-done.2) | copy-start | bytes 3145732
  858.0 42.3 %copy-start.43 = (f32[256]{0:T(256)S(1)}, f32[256]{0:T(256)}, u32[]{:S(2)}) copy-start(f32[256]{0:T(256)} %copy-done.42) | copy-start | bytes 3076
  858.0 96.9 %all-to-all-start.16 = ((bf16[16,128,512]{1,0,2:T(8,128)(2,1)}), bf16[16,128,512]{1,0,2:T(8,128)(2,1)}, u32[]{:S(2)}, u32[]{:S(2)}) async-start(bf16[16,128,512]{1,0,2:T(8,128)(2,1)} %copy.240), calls=%async_computation.18 | async-start | bytes 4194304 | tf_op jit(solution)/shard_map/all_to_all | solution.py:426
  862.6 74.5 %copy-start.47 = (f32[256]{0:T(256)S(1)}, f32[256]{0:T(256)}, u32[]{:S(2)}) copy-start(f32[256]{0:T(256)} %get-tuple-element.58) | copy-start | bytes 3076
  862.6 111.8 %reduce-scatter.3.cloned.1.call-start = ((), (), s32[]{:S(2)}) async-start(), calls=%async_computation.22 | async-start | bytes 393216 | tf_op jit(solution)/shard_map/reduce_scatter | solution.py:355
  937.1 2.6 copy-start.10
  937.1 3.0 copy-start.22
  939.7 2.2 copy-start.30
  939.7 2.2 copy-start.32
  939.7 2.2 copy-start.51
  954.9 30.2 %all-to-all-start.14 = ((bf16[16,128,512]{1,0,2:T(8,128)(2,1)}), bf16[16,128,512]{1,0,2:T(8,128)(2,1)}, u32[]{:S(2)}, u32[]{:S(2)}) async-start(bf16[16,128,512]{1,0,2:T(8,128)(2,1)} %copy.235), calls=%async_computation.16 | async-start | bytes 4194304 | tf_op jit(solution)/shard_map/all_to_all | solution.py:413
  959.4 31.5 %reduce-scatter.5.cloned.1.call-start = ((), (), s32[]{:S(2)}) async-start(), calls=%async_computation.23 | async-start | bytes 393216 | tf_op jit(solution)/shard_map/reduce_scatter | solution.py:356
  963.2 4.5 copy-start.28
  969.7 4.3 copy-start.18
  969.7 4.3 copy-start.25
  969.7 4.3 copy-start.24
  975.9 13.7 %copy-start.15 = (bf16[1024,128]{1,0:T(8,128)(2,1)S(1)}, bf16[1024,128]{1,0:T(8,128)(2,1)}, u32[]{:S(2)}) copy-start(bf16[1024,128]{1,0:T(8,128)(2,1)} %copy-done.14) | copy-start | bytes 786436
  985.1 61.0 %all-to-all-start.12 = ((bf16[16,128,512]{1,0,2:T(8,128)(2,1)}), bf16[16,128,512]{1,0,2:T(8,128)(2,1)}, u32[]{:S(2)}, u32[]{:S(2)}) async-start(bf16[16,128,512]{1,0,2:T(8,128)(2,1)} %copy.230), calls=%async_computation.14 | async-start | bytes 4194304 | tf_op jit(solution)/shard_map/all_to_all | solution.py:400
  989.6 49.9 %all-reduce.11.cloned.1.call-start = ((), (), s32[]{:S(2)}) async-start(), calls=%async_computation.24 | async-start | bytes 2097152 | tf_op jit(solution)/shard_map/psum | solution.py:379
  992.2 2.4 copy-start.37
  992.2 2.4 copy-start.45
  1046.1 42.5 %all-to-all-start.10 = ((bf16[8,128,770]{1,2,0:T(8,128)(2,1)}), bf16[8,128,770]{1,2,0:T(8,128)(2,1)}, u32[]{:S(2)}, u32[]{:S(2)}) async-start(bf16[8,128,770]{1,2,0:T(8,128)(2,1)} %concatenate.36), calls=%async_computation.12 | async-start | bytes 3178496 | tf_op jit(solution)/shard_map/all_to_all | solution.py:27
  1058.4 3.4 copy-start.46
  (11 other events, 11.3 us)
Sparse Core Ops, SparseCore 0:
  231.9 36.2 all-reduce.4
  852.8 47.4 all-reduce.8
  903.2 33.8 all-reduce.6
  947.0 11.6 reduce-scatter.2
  969.8 13.0 reduce-scatter.4
  994.7 44.7 all-reduce.10
where the time goes:
time: 1110 us; the launch traced here: 1100 us
  waiting for transfers between devices  539 us (49%)
  blocking collectives  190 us (17%)
  local copies, waits for them, and re-layouts  188 us (17%)
  starting transfers between devices  79.1 us (7%)
  matrix products  50.9 us (5%)
  other arithmetic  38.7 us (3%)
  between operations  15.7 us (1%)
    all_to_all x1, waiting for transfers between devices, local(): lax.all_to_all(in_grads.reshape(1, per_owner, -1, model_width), ('fsdp',...  47.8 us
    all_to_all x1, waiting for transfers between devices, local(): lax.all_to_all(out_rows.reshape(1, per_owner, -1, model_width), ('fsdp',...  47.2 us
    all_to_all x1, waiting for transfers between devices, local(): lax.all_to_all(spread_weight(w_up, copies, part_count), ('fsdp', 'context...  43.7 us
    all_to_all x1, waiting for transfers between devices, local(): lax.all_to_all(spread_weight(w_gate, copies, part_count), ('fsdp', 'conte...  43.5 us
    psum x1, waiting for transfers between devices, local(): d_in = lax.psum(d_in_part, 'tensor')  42.6 us
    all_to_all x1, waiting for transfers between devices, local(): lax.all_to_all(weight_grads[2].astype(jnp.bfloat16), ('fsdp', 'context'),...  42.1 us
    all_to_all x1, waiting for transfers between devices, local(): lax.all_to_all(weight_grads[1].astype(jnp.bfloat16), ('fsdp', 'context'),...  41.9 us
    all_to_all x1, waiting for transfers between devices, local(): lax.all_to_all(spread_weight(w_down, copies, part_count), ('fsdp', 'conte...  39 us
  transfers between devices with their start and end apart: 23, of which 17 were waited for; matrix products, arithmetic and copies ran while one was open for 19% of the time, Pallas kernels for 0%

commit v1 on v0

v1 whole, which is shorter than its diff:
```python
import functools

import jax
import jax.numpy as jnp
from jax import lax
from jax.experimental import pallas as pl
from jax.experimental.pallas import tpu as pltpu
from jax.sharding import PartitionSpec as P

HEAD_SIZE = 64
TOP = 8
EXPERTS = 16

EPSILON = 1e-06
CONTRACT_ROWS = (((0,), (0,)), ((), ()))
CONTRACT_COLUMNS = (((1,), (1,)), ((), ()))
MESH = pl.DeviceIdType.MESH
VMEM_BYTES = 48 * 1024 * 1024


def coordinate(dim):
    axis, size, stride = dim
    return lax.rem(lax.div(lax.axis_index(axis), stride), size)


def device_at(dim, place):
    axis, _, stride = dim
    return {axis: lax.axis_index(axis) + (place - coordinate(dim)) * stride}


def greet(dims):
    barrier = pltpu.get_barrier_semaphore()
    total = 0
    for dim in dims:
        for k in range(1, dim[1]):
            place = lax.rem(coordinate(dim) + k, dim[1])
            pl.semaphore_signal(
                barrier, inc=1, device_id=device_at(dim, place), device_id_type=MESH
            )
            total += 1
    pl.semaphore_wait(barrier, total)


def gather_kernel(dims, count, *refs):
    sources, outs = refs[:count], refs[count : 2 * count]
    send_sem, recv_sem, own_sem = refs[2 * count :]
    places = [coordinate(dim) for dim in dims]

    def slot(steps):
        return tuple(
            lax.rem(place - step + dim[1], dim[1]) for place, step, dim in zip(places, steps, dims)
        )

    zero = (0,) * len(dims)
    own = [
        pltpu.make_async_copy(sources[a], outs[a].at[slot(zero)], own_sem.at[a])
        for a in range(count)
    ]
    for copy in own:
        copy.start()
    greet(dims)
    queue = [(zero, 0, None)]
    sent = []
    at = 0
    while at < len(queue):
        steps, level, arriving = queue[at]
        at += 1
        if arriving is not None:
            for copy in arriving:
                copy.wait_recv()
        for s in range(level, len(dims)):
            for k in range(1, dims[s][1]):
                copies = []
                for a in range(count):
                    index = len(sent)
                    source = sources[a] if arriving is None else outs[a].at[slot(steps)]
                    copy = pltpu.make_async_remote_copy(
                        src_ref=source,
                        dst_ref=outs[a].at[slot(steps)],
                        send_sem=send_sem.at[index],
                        recv_sem=recv_sem.at[index],
                        device_id=device_at(dims[s], lax.rem(places[s] + k, dims[s][1])),
                        device_id_type=MESH,
                    )
                    copy.start()
                    copies.append(copy)
                    sent.append(copy)
                queue.append((steps[:s] + (k,) + steps[s + 1 :], s + 1, copies))
    for copy in sent:
        copy.wait_send()
    for copy in own:
        copy.wait()


def gather_pieces(arrays, dims, number):
    sizes = tuple(dim[1] for dim in dims)
    total = 1
    for size in sizes:
        total *= size
    copies = (total - 1) * len(arrays)
    any_spec = pl.BlockSpec(memory_space=pl.ANY)
    return pl.pallas_call(
        functools.partial(gather_kernel, dims, len(arrays)),
        out_shape=tuple(jax.ShapeDtypeStruct(sizes + a.shape, a.dtype) for a in arrays),
        in_specs=[any_spec] * len(arrays),
        out_specs=tuple(any_spec for _ in arrays),
        scratch_shapes=[
            pltpu.SemaphoreType.DMA((max(copies, 1),)),
            pltpu.SemaphoreType.DMA((max(copies, 1),)),
            pltpu.SemaphoreType.DMA((len(arrays),)),
        ],
        compiler_params=pltpu.CompilerParams(collective_id=number, has_side_effects=True),
    )(*arrays)


def reduce_kernel(halves, last, x_ref, out_ref, *scratch):
    stages = len(halves)
    landed = scratch[:stages]
    summed = scratch[stages : 2 * stages]
    final = scratch[2 * stages]
    send_sem, recv_sem = scratch[2 * stages + 1 :]
    n = last[1]
    place = coordinate(last)
    mine = [coordinate(dim) for dim in halves]
    greet(list(halves) + [last])
    order = [lax.rem(place + k, n) for k in list(range(1, n)) + [0]]

    def held(stage):
        return x_ref if stage == 0 else summed[stage - 1]

    def part(stage, j, which):
        return (j,) + (slice(None),) * (stages - 1 - stage) + (which,)

    copies = [[None] * n for _ in range(stages)]

    def push(stage, i):
        copies[stage][i] = pltpu.make_async_remote_copy(
            src_ref=held(stage).at[part(stage, order[i], 1 - mine[stage])],
            dst_ref=landed[stage].at[i],
            send_sem=send_sem.at[stage * n + i],
            recv_sem=recv_sem.at[stage * n + i],
            device_id=device_at(halves[stage], 1 - mine[stage]),
            device_id_type=MESH,
        )
        copies[stage][i].start()

    def merge(stage, i):
        copies[stage][i].wait_recv()
        kept = held(stage)[part(stage, order[i], mine[stage])]
        both = kept.astype(jnp.float32) + landed[stage][i].astype(jnp.float32)
        summed[stage][order[i]] = both.astype(summed[stage].dtype)

    for i in range(n):
        push(0, i)
    outgoing = []
    for tick in range(n + stages - 1):
        for stage in range(stages):
            i = tick - stage
            if 0 <= i < n:
                merge(stage, i)
                if stage + 1 < stages:
                    push(stage + 1, i)
                elif i < n - 1:
                    index = stages * n + i
                    copy = pltpu.make_async_remote_copy(
                        src_ref=summed[-1].at[order[i]],
                        dst_ref=final.at[i],
                        send_sem=send_sem.at[index],
                        recv_sem=recv_sem.at[index],
                        device_id=device_at(last, order[i]),
                        device_id_type=MESH,
                    )
                    copy.start()
                    outgoing.append(copy)
    total = summed[-1][place].astype(jnp.float32)
    for i, copy in enumerate(outgoing):
        copy.wait_recv()
        total = total + final[i].astype(jnp.float32)
    out_ref[...] = total
    for row in copies:
        for copy in row:
            copy.wait_send()
    for copy in outgoing:
        copy.wait_send()


def reduce_pieces(x, halves, last, number):
    rows, columns = x.shape[-2:]
    n = last[1]
    stages = len(halves)
    shapes = [(n,) + (2,) * (stages - 1 - s) + (rows, columns) for s in range(stages)]
    vmem = pl.BlockSpec(memory_space=pltpu.VMEM)
    return pl.pallas_call(
        functools.partial(reduce_kernel, tuple(halves), last),
        out_shape=jax.ShapeDtypeStruct((rows, columns), jnp.float32),
        in_specs=[vmem],
        out_specs=vmem,
        scratch_shapes=[pltpu.VMEM(shape, x.dtype) for shape in shapes]
        + [pltpu.VMEM(shape, x.dtype) for shape in shapes]
        + [
            pltpu.VMEM((n - 1, rows, columns), x.dtype),
            pltpu.SemaphoreType.DMA(((stages + 1) * n,)),
            pltpu.SemaphoreType.DMA(((stages + 1) * n,)),
        ],
        compiler_params=pltpu.CompilerParams(
            collective_id=number, has_side_effects=True, vmem_limit_bytes=VMEM_BYTES
        ),
    )(x)


def swapped(array, axis, step):
    size = lax.axis_size(axis)
    return lax.ppermute(array, axis, [(i, i ^ step) for i in range(size)])


def joined(array, other, place):
    return jnp.where(place == 0, jnp.stack([array, other]), jnp.stack([other, array]))


def by_fsdp(array, dim):
    axis, size, stride = dim
    count = lax.axis_size(axis)
    place = coordinate(dim)
    blocks = [array]
    for k in range(1, size):
        pairs = []
        for i in range(count):
            c = i // stride % size
            pairs.append((i, i + ((c - k) % size - c) * stride))
        blocks.append(lax.ppermute(array, axis, pairs))
    stacked = jnp.stack(blocks)
    order = lax.rem(jnp.arange(size, dtype=jnp.int32) - place + size, size)
    return stacked[order]


def rms_scale(values):
    return lax.rsqrt(jnp.mean(values * values, axis=-1, keepdims=True) + EPSILON)


def rotate(values, places, direction):
    head_count = values.shape[-1] // HEAD_SIZE
    shaped = values.reshape(values.shape[0], head_count, HEAD_SIZE)
    half_dim = HEAD_SIZE // 2
    frequency = 1.0 / 10000.0 ** (jnp.arange(half_dim, dtype=jnp.float32) * 2.0 / HEAD_SIZE)
    angles = places.astype(jnp.float32)[:, None, None] * frequency[None, None, :]
    cosine = jnp.cos(angles)
    sine_table = jnp.sin(angles) * direction
    first_half = shaped[..., :half_dim]
    second_half = shaped[..., half_dim:]
    turned = jnp.concatenate(
        [
            first_half * cosine - second_half * sine_table,
            second_half * cosine + first_half * sine_table,
        ],
        axis=-1,
    )
    return turned.reshape(values.shape)


def local(
    tokens,
    w_query,
    key_projection_weight,
    value_projection_weight,
    w_out,
    w_gate,
    w_up,
    w_down,
    norm_in,
    norm_mid,
    gate_values,
    routes,
    doc_ids,
    cotangent,
):
    local_rows, model_width = tokens.shape
    fsdp = lax.axis_size("fsdp")
    tensor = lax.axis_size("tensor")
    groups = min(fsdp, EXPERTS)
    copies = fsdp // groups
    per_owner = EXPERTS // groups
    piece = local_rows // tensor
    depth = w_gate.shape[1]
    hidden_width = w_gate.shape[2]
    context_index = lax.axis_index("context")
    tensor_index = lax.axis_index("tensor")
    fsdp_all = ("fsdp", fsdp, 1)
    fsdp_dim = ("fsdp", groups, copies)
    context_dim = ("context", lax.axis_size("context"), 1)
    core_dim = ("tensor", 2, 1)
    y_dim = ("tensor", tensor // 2, 2)
    q_width, k_width = w_query.shape[1], key_projection_weight.shape[1]
    columns = per_owner * hidden_width

    def to_owner(weight):
        blocks = jnp.transpose(weight.reshape(groups, per_owner, depth, hidden_width), (0, 2, 1, 3))
        return blocks.reshape(groups, depth, columns)

    packed = jnp.concatenate([to_owner(w_gate), to_owner(w_up), to_owner(w_down)], axis=2)
    packed = jnp.repeat(packed, copies, axis=0)
    from_fsdp = lax.all_to_all(packed, "fsdp", 0, 0, tiled=True)
    both_context = joined(from_fsdp, swapped(from_fsdp, "context", 1), context_index)
    expert_weight = jnp.swapaxes(both_context, 0, 1).reshape(model_width, 3 * columns)
    gate_up_weight = expert_weight[:, : 2 * columns]
    down_weight = expert_weight[:, 2 * columns :]

    cot_piece = lax.dynamic_slice_in_dim(cotangent, tensor_index * piece, piece, 0)
    cot_f = by_fsdp(cot_piece, fsdp_dim)
    cot_y = by_fsdp(cot_f, y_dim)
    cot_t = by_fsdp(cot_y, core_dim)
    cot_all = jnp.transpose(cot_t, (2, 1, 0, 3, 4)).reshape(-1, model_width)
    dense_gates = jnp.sum(
        jnp.where(
            routes.T[None, :, :] == jnp.arange(EXPERTS, dtype=jnp.int32)[:, None, None],
            gate_values.T[None, :, :],
            0.0,
        ),
        axis=1,
    )
    gates_all = by_fsdp(dense_gates, fsdp_dim)
    gates_own = lax.dynamic_slice_in_dim(
        gates_all, coordinate(fsdp_dim) * per_owner, per_owner, 1
    )
    gates_rows = jnp.transpose(gates_own, (0, 2, 1)).reshape(-1, per_owner)
    gates_wide = jnp.repeat(gates_rows, hidden_width, axis=1)

    attn_shard = jnp.concatenate(
        [w_query, key_projection_weight, value_projection_weight, w_out], axis=1
    )
    gain_shard = jnp.pad(
        jnp.stack([norm_in, norm_mid]).astype(jnp.float32), ((0, 6), (0, 128 - depth))
    )
    attn_weight, gains = gather_pieces([attn_shard, gain_shard], [fsdp_all, context_dim], 1)
    attn_weight = attn_weight.reshape(model_width, -1)
    gains = gains[..., :depth].reshape(-1, 8, depth)
    gain_one = gains[:, 0, :].reshape(-1)
    gain_two = gains[:, 1, :].reshape(-1)
    in_weight = attn_weight[:, : q_width + 2 * k_width]
    out_weight = attn_weight[:, q_width + 2 * k_width :]
    documents = doc_ids[0]
    query_places = context_index * local_rows + jnp.arange(local_rows, dtype=jnp.int32)
    key_places = jnp.arange(documents.shape[0], dtype=jnp.int32)
    score_scale = HEAD_SIZE ** (-0.5)
    inputs = tokens.astype(jnp.float32)
    scale_in = rms_scale(inputs)
    normed_in = (inputs * scale_in * gain_one).astype(jnp.bfloat16)
    projected = jnp.dot(normed_in, in_weight, preferred_element_type=jnp.float32)
    query_input = rotate(projected[:, :q_width], query_places, 1.0).astype(jnp.bfloat16)
    key_local = rotate(projected[:, q_width : q_width + k_width], query_places, 1.0)
    key_value = jnp.concatenate([key_local, projected[:, q_width + k_width :]], axis=1).astype(
        jnp.bfloat16
    )
    key_value = joined(key_value, swapped(key_value, "context", 1), context_index).reshape(
        -1, 2 * k_width
    )
    keys_all, values_all = key_value[:, :k_width], key_value[:, k_width:]
    kv_heads = keys_all.shape[1] // HEAD_SIZE
    per_group = query_input.shape[1] // HEAD_SIZE // kv_heads
    query_head_rows = query_input.reshape(local_rows, kv_heads, per_group, HEAD_SIZE)
    key_head_rows = keys_all.reshape(keys_all.shape[0], kv_heads, HEAD_SIZE)
    value_head_rows = values_all.reshape(values_all.shape[0], kv_heads, HEAD_SIZE)
    visible = (key_places[None, :] <= query_places[:, None]) & (
        documents[None, :] == documents[query_places][:, None]
    )

    def masked_scores():
        raw_scores = (
            jnp.einsum(
                "rkgd,skd->kgrs", query_head_rows, key_head_rows, preferred_element_type=jnp.float32
            )
            * score_scale
        )
        return jnp.where(visible, raw_scores, -1e30)

    masked = masked_scores()
    highest = jnp.max(masked, axis=-1, keepdims=True)
    exponent = jnp.exp(masked - highest)
    totals = jnp.sum(exponent, axis=-1, keepdims=True)
    probs_low = (exponent / totals).astype(jnp.bfloat16)
    context = jnp.einsum(
        "kgrs,skd->rkgd", probs_low, value_head_rows, preferred_element_type=jnp.float32
    )
    context = context.reshape(local_rows, -1).astype(jnp.bfloat16)
    attn_part = lax.dot_general(
        context, out_weight, CONTRACT_COLUMNS, preferred_element_type=jnp.float32
    )
    def by_tensor(part):
        return part.astype(jnp.bfloat16).reshape(tensor // 2, 2, piece, model_width)

    attended = reduce_pieces(by_tensor(attn_part), [core_dim], y_dim, 2)
    start_row = tensor_index * piece
    own_inputs = lax.dynamic_slice_in_dim(tokens, start_row, piece, 0).astype(jnp.float32)
    own_scale_in = lax.dynamic_slice_in_dim(scale_in, start_row, piece, 0)
    hidden_state = own_inputs + attended
    scale_mid = rms_scale(hidden_state)
    normed_mid = (hidden_state * scale_mid * gain_two).astype(jnp.bfloat16)
    (expert_rows,) = gather_pieces([normed_mid], [fsdp_dim, y_dim, core_dim], 3)
    expert_rows = expert_rows.reshape(-1, model_width)
    act = jnp.dot(expert_rows, gate_up_weight, preferred_element_type=jnp.float32)
    gate_act, up_act = act[:, :columns], act[:, columns:]
    sigmoid_gate = jax.nn.sigmoid(gate_act)
    swish_act = gate_act * sigmoid_gate
    hidden = (gates_wide * swish_act * up_act).astype(jnp.bfloat16)
    d_hidden = gates_wide * jnp.dot(cot_all, down_weight, preferred_element_type=jnp.float32)
    d_gate_act = d_hidden * up_act * sigmoid_gate * (1.0 + gate_act * (1.0 - sigmoid_gate))
    d_up_act = d_hidden * swish_act
    d_act = jnp.concatenate([d_gate_act, d_up_act], axis=1).astype(jnp.bfloat16)
    moe_part = lax.dot_general(
        hidden, down_weight, CONTRACT_COLUMNS, preferred_element_type=jnp.float32
    ).astype(jnp.bfloat16)
    d_mid_part = lax.dot_general(
        d_act, gate_up_weight, CONTRACT_COLUMNS, preferred_element_type=jnp.float32
    ).astype(jnp.bfloat16)
    split = (groups, tensor // 2, 2, piece, model_width)
    both_parts = jnp.concatenate([moe_part.reshape(split), d_mid_part.reshape(split)], axis=3)
    back = reduce_pieces(both_parts, [core_dim, y_dim], fsdp_dim, 4)
    grad_gate_up = lax.dot_general(
        expert_rows, d_act, CONTRACT_ROWS, preferred_element_type=jnp.float32
    )
    grad_down = lax.dot_general(cot_all, hidden, CONTRACT_ROWS, preferred_element_type=jnp.float32)
    expert_grad = jnp.concatenate([grad_gate_up, grad_down], axis=1).astype(jnp.bfloat16)
    expert_grad = jnp.swapaxes(expert_grad.reshape(fsdp, -1, depth, 3 * columns), 0, 1)
    kept = lax.dynamic_index_in_dim(expert_grad, context_index, 0, False)
    given = lax.dynamic_index_in_dim(expert_grad, 1 - context_index, 0, False)
    taken = swapped(given, "context", 1)
    half_grad = (kept.astype(jnp.float32) + taken.astype(jnp.float32)).astype(jnp.bfloat16)
    owned_grad = lax.all_to_all(half_grad, "fsdp", 0, 0, tiled=True).astype(jnp.float32)
    owned_grad = jnp.sum(owned_grad.reshape(groups, copies, depth, 3, per_owner, hidden_width), 1)
    owned_grad = jnp.transpose(owned_grad, (2, 0, 3, 1, 4)).reshape(
        3, EXPERTS, depth, hidden_width
    )

    moe_mixed, d_mid = back[:piece], back[piece:]
    own_output = (hidden_state + moe_mixed).astype(jnp.bfloat16)
    d_gain_mid = jnp.sum(d_mid * hidden_state * scale_mid, axis=0)
    d_hidden_state = (
        cot_piece.astype(jnp.float32)
        + d_mid * gain_two * scale_mid
        - hidden_state
        * scale_mid**3
        * jnp.mean(gain_two * d_mid * hidden_state, axis=-1, keepdims=True)
    )
    d_attended, output = gather_pieces(
        [d_hidden_state.astype(jnp.bfloat16), own_output], [y_dim, core_dim], 5
    )
    d_attended = d_attended.reshape(local_rows, model_width)
    output = output.reshape(local_rows, model_width)
    d_out_weight = lax.dot_general(
        d_attended, context, CONTRACT_ROWS, preferred_element_type=jnp.float32
    )
    d_context = jnp.dot(d_attended, out_weight, preferred_element_type=jnp.float32).astype(
        jnp.bfloat16
    )
    d_context_heads = d_context.reshape(local_rows, kv_heads, per_group, HEAD_SIZE)
    attn_probs = jnp.exp(masked_scores() - highest) / totals
    d_probs = jnp.einsum(
        "rkgd,skd->kgrs", d_context_heads, value_head_rows, preferred_element_type=jnp.float32
    )
    d_scores = attn_probs * (d_probs - jnp.sum(attn_probs * d_probs, axis=-1, keepdims=True))
    d_scores_low = jnp.where(visible, d_scores, 0.0).astype(jnp.bfloat16)
    d_query_turned = jnp.einsum(
        "kgrs,skd->rkgd", d_scores_low, key_head_rows, preferred_element_type=jnp.float32
    )
    d_query_turned = d_query_turned.reshape(local_rows, -1) * score_scale
    d_keys = jnp.einsum(
        "kgrs,rkgd->skd", d_scores_low, query_head_rows, preferred_element_type=jnp.float32
    )
    d_keys = d_keys.reshape(keys_all.shape[0], -1) * score_scale
    d_values = jnp.einsum(
        "kgrs,rkgd->skd", probs_low, d_context_heads, preferred_element_type=jnp.float32
    )
    d_values = d_values.reshape(values_all.shape[0], -1)
    d_both = jnp.concatenate([d_keys, d_values], axis=1).reshape(
        -1, local_rows, 2 * k_width
    )
    d_given = lax.dynamic_index_in_dim(d_both, 1 - context_index, 0, False)
    d_kept = lax.dynamic_index_in_dim(d_both, context_index, 0, False)
    d_own = d_kept + swapped(d_given, "context", 1)
    d_query = rotate(d_query_turned, query_places, -1.0).astype(jnp.bfloat16)
    d_key = rotate(d_own[:, :k_width], query_places, -1.0).astype(jnp.bfloat16)
    d_projected = jnp.concatenate(
        [d_query, d_key, d_own[:, k_width:].astype(jnp.bfloat16)], axis=1
    )
    d_in_part = lax.dot_general(
        d_projected, in_weight, CONTRACT_COLUMNS, preferred_element_type=jnp.float32
    )
    d_in = reduce_pieces(by_tensor(d_in_part), [core_dim], y_dim, 6)
    d_in_weight = lax.dot_general(
        normed_in, d_projected, CONTRACT_ROWS, preferred_element_type=jnp.float32
    )
    d_gain_in = jnp.sum(d_in * own_inputs * own_scale_in, axis=0)
    d_inputs = (
        d_hidden_state
        + d_in * gain_one * own_scale_in
        - own_inputs
        * own_scale_in**3
        * jnp.mean(gain_one * d_in * own_inputs, axis=-1, keepdims=True)
    ).astype(jnp.bfloat16)
    d_gains = jnp.pad(jnp.stack([d_gain_in, d_gain_mid]), ((0, 6), (0, 0)))
    d_tokens, d_gains = gather_pieces([d_inputs, d_gains], [y_dim, core_dim], 7)
    d_tokens = d_tokens.reshape(local_rows, model_width)
    d_gains = jnp.sum(d_gains, axis=(0, 1))[:2]
    d_attn = jnp.concatenate([d_in_weight, d_out_weight], axis=1).astype(jnp.bfloat16)
    d_attn = d_attn.reshape(fsdp, -1, depth, d_attn.shape[1])
    d_gains = jnp.transpose(d_gains.reshape(2, fsdp, -1, depth), (1, 2, 0, 3)).astype(jnp.bfloat16)
    d_gains = jnp.pad(d_gains, ((0, 0), (0, 0), (0, 14), (0, d_attn.shape[3] - depth)))
    owned = reduce_pieces(
        jnp.concatenate([d_attn, d_gains], axis=2), [context_dim], fsdp_all, 8
    )
    first, second = q_width, q_width + k_width
    third = q_width + 2 * k_width
    return (
        output,
        d_tokens,
        owned[:depth, :first],
        owned[:depth, first:second],
        owned[:depth, second:third],
        owned[:depth, third:],
        owned_grad[0],
        owned_grad[1],
        owned_grad[2],
        owned[depth, :depth],
        owned[depth + 1, :depth],
    )


def solution(mesh):
    placed = (
        P(("fsdp", "context"), None),
        P(("fsdp", "context"), "tensor"),
        P(("fsdp", "context"), "tensor"),
        P(("fsdp", "context"), "tensor"),
        P(("fsdp", "context"), "tensor"),
        P(None, ("fsdp", "context"), "tensor"),
        P(None, ("fsdp", "context"), "tensor"),
        P(None, ("fsdp", "context"), "tensor"),
        P(("fsdp", "context")),
        P(("fsdp", "context")),
        P(("fsdp", "context"), None),
        P(("fsdp", "context"), None),
        P("fsdp", None),
        P(("fsdp", "context"), None),
    )
    return jax.shard_map(
        local,
        mesh=mesh,
        in_specs=placed,
        out_specs=(
            P(("fsdp", "context"), None),
            P(("fsdp", "context"), None),
            P(("fsdp", "context"), "tensor"),
            P(("fsdp", "context"), "tensor"),
            P(("fsdp", "context"), "tensor"),
            P(("fsdp", "context"), "tensor"),
            P(None, ("fsdp", "context"), "tensor"),
            P(None, ("fsdp", "context"), "tensor"),
            P(None, ("fsdp", "context"), "tensor"),
            P(("fsdp", "context")),
            P(("fsdp", "context")),
        ),
        check_vma=False,
    )
```

time: 1110 us -> 340 us (0.31)
  waiting for transfers between devices: 539 us -> 10.4 us
  blocking collectives: 190 us -> 0 us
  Pallas kernels: 0 us -> 186 us
  local copies, waits for them, and re-layouts: 188 us -> 47.3 us
  starting transfers between devices: 79.1 us -> 24.5 us
  between operations: 15.7 us -> 1.56 us
  other arithmetic: 38.7 us -> 26.2 us
    all_to_all x17 -> x2, waiting for transfers between devices: 407 us -> 0.01 us  [the longest x1 0.01 us: local(): from_fsdp = lax.all_to_all(packed, 'fsdp', 0, 0, tiled=True)]
    all_gather x8 -> x0, blocking collectives: 190 us -> none  [the longest x1 33 us: local(): lax.all_gather(norm_in, ('fsdp', 'context'), axis=0, tiled=True)]
    pallas_call x0 -> x8, Pallas kernels: none -> 186 us  [the longest x4 97.9 us: gather_pieces(): pl.pallas_call(functools.partial(gather_kernel, dims, len(arrays)), out_s...]
    psum x4 -> x0, waiting for transfers between devices: 132 us -> none  [the longest x1 42.6 us: local(): d_in = lax.psum(d_in_part, 'tensor')]
    all_to_all x20 -> x0, local copies, waits for them, and re-layouts: 70.8 us -> none  [the longest x2 9.42 us: local(): lax.all_to_all(spread_weight(w_gate, copies, part_count), ('fsdp', 'conte...]
    all_to_all x17 -> x2, starting transfers between devices: 78.4 us -> 8.97 us  [the longest x1 4.49 us: local(): lax.all_to_all(half_grad, 'fsdp', 0, 0, tiled=True).astype(jnp.float32)]
    gather x7 -> x4, local copies, waits for them, and re-layouts: 35.1 us -> 3.78 us  [by_fsdp(): return stacked[order]]
    reduce_sum x7 -> x3, other arithmetic: 19.1 us -> 1.83 us  [the longest x1 0.92 us: local(): d_gains = jnp.sum(d_gains, axis=(0, 1))[:2]]
  transfers between devices with their start and end apart: 23 -> 14, of which waited for: 17 -> 2; matrix products, arithmetic and copies ran while one was open for 19% -> 22% of each run, Pallas kernels for 0% -> 55%
where the time goes in v1:
time: 340 us; the launch traced here: 338 us
  Pallas kernels  186 us (55%)
  local copies, waits for them, and re-layouts  47.3 us (14%)
  matrix products  42.3 us (12%)
  other arithmetic  26.2 us (8%)
  starting transfers between devices  24.5 us (7%)
  waiting for transfers between devices  10.4 us (3%)
    pallas_call x4, Pallas kernels, gather_pieces(): pl.pallas_call(functools.partial(gather_kernel, dims, len(arrays)), out_s...  97.9 us
    pallas_call x4, Pallas kernels, reduce_pieces(): pl.pallas_call(functools.partial(reduce_kernel, tuple(halves), last), out...  88.4 us
    ppermute x8, starting transfers between devices, by_fsdp(): blocks.append(lax.ppermute(array, axis, pairs))  12.4 us
    ppermute x8, waiting for transfers between devices, by_fsdp(): blocks.append(lax.ppermute(array, axis, pairs))  10.3 us
    unnamed x67, local copies, waits for them, and re-layouts  7.4 us
  transfers between devices with their start and end apart: 14, of which 2 were waited for; matrix products, arithmetic and copies ran while one was open for 22% of the time, Pallas kernels for 55%

profile of v1, /device:TPU:0, one launch (start us, length us, event | category | flops | bytes accessed | tf_op | source)
XLA Modules:
  0.0 338.5 jit_solution(8617700459145372645)
XLA Ops:
  0.7 1.0 constant_dynamic-slice_fusion.1
  1.6 5.1 %collective-permute-start.5 = (bf16[64,1024]{1,0:T(8,128)(2,1)S(1)}, bf16[64,1024]{1,0:T(8,128)(2,1)S(1)}, u32[]{:S(2)}, u32[]{:S(2)}) collective-permute-start(bf16[64,1024]{1,0:T(8,128)(2,1)S(1)} %constant_dynamic-slice_fusion.1), channel_id=1, source_target_pairs={{0,24},{8,0},{16,8},{24,16},{1,25},{9,1},{17,9},{25,17},{2,26},{10... | collective-permute-start | bytes 393224 | tf_op jit(solution)/shard_map/ppermute | solution.py:230
  8.0 2.6 collective-permute-start.1
  10.6 1.9 collective-permute-start.2
  12.5 1.3 copy.77
  13.8 1.3 copy.78
  15.4 1.3 pad_maximum_fusion.3
  16.8 4.5 %all-to-all-start = ((bf16[4,128,1536]{1,2,0:T(8,128)(2,1)}), bf16[4,128,1536]{1,2,0:T(8,128)(2,1)}, u32[]{:S(2)}, u32[]{:S(2)}) async-start(bf16[4,128,1536]{1,2,0:T(8,128)(2,1)} %pad_maximum_fusion.3), calls=%async_computation | async-start | bytes 3145728 | tf_op jit(solution)/shard_map/all_to_all | solution.py:301
  22.6 58.1 %shard_map.221 = (bf16[4,2,128,768]{3,2,1,0:T(8,128)(2,1)}, f32[4,2,8,128]{3,2,1,0:T(8,128)}) custom-call(bf16[128,768]{1,0:T(8,128)(2,1)} %pad_maximum_fusion.9.refs_0_, f32[8,128]{1,0:T(8,128)} %fusion.65.refs_1_), custom_call_target="tpu_custom_call" | custom-call | tf_op jit(solution)/shard_map/pallas_call | solution.py:102
  81.7 1.7 fusion.41
  84.2 1.9 gather_fusion.1
  86.3 0.9 fusion.111
  89.5 5.2 %collective-permute-done.7 = bf16[64,1024]{1,0:T(8,128)(2,1)S(1)} collective-permute-done((bf16[64,1024]{1,0:T(8,128)(2,1)S(1)}, bf16[64,1024]{1,0:T(8,128)(2,1)S(1)}, u32[]{:S(2)}, u32[]{:S(2)}) %collective-permute-start.7) | collective-permute-done | bytes 131104 | tf_op jit(solution)/shard_map/ppermute | solution.py:230
  95.3 1.6 collective-permute-start.8
  97.7 2.2 fusion.88
  100.1 5.2 %collective-permute-done.8 = bf16[4,64,1024]{2,1,0:T(8,128)(2,1)S(1)} collective-permute-done((bf16[4,64,1024]{2,1,0:T(8,128)(2,1)S(1)}, bf16[4,64,1024]{2,1,0:T(8,128)(2,1)S(1)}, u32[]{:S(2)}, u32[]{:S(2)}) %collective-permute-start.8) | collective-permute-done | bytes 524320 | tf_op jit(solution)/shard_map/ppermute | solution.py:230
  106.3 2.1 convolution_convert_fusion.8
  108.4 1.4 convolution_convert_fusion.6
  109.9 7.2 %shard_map.222 = f32[64,1024]{1,0:T(8,128)S(1)} custom-call(bf16[2,2,64,1024]{3,2,1,0:T(8,128)(2,1)S(1)} %bitcast.223), custom_call_target="tpu_custom_call" | custom-call | tf_op jit(solution)/shard_map/pallas_call | solution.py:193
  118.0 21.4 %shard_map.223 = bf16[4,2,2,64,1024]{4,3,2,1,0:T(8,128)(2,1)} custom-call(bf16[64,1024]{1,0:T(8,128)(2,1)} %multiply_convert_fusion.2.refs_0_), custom_call_target="tpu_custom_call" | custom-call | tf_op jit(solution)/shard_map/pallas_call | solution.py:102
  139.4 4.0 %copy.91 = bf16[1024,1024]{1,0:T(8,128)(2,1)} copy(bf16[1024,1024]{0,1:T(8,128)(2,1)} %bitcast.230) | data formatting | bytes 4194304 | tf_op jit(solution)/shard_map/dot_general | solution.py:417
  143.4 1.0 copy-done.9
  144.4 1.4 pad_maximum_fusion.1
  145.8 2.0 gather_fusion.4
  147.8 1.8 copy.81
  149.7 2.6 copy.111
  152.3 4.8 %fusion.3 = bf16[4,2,128,1536]{2,3,0,1:T(8,128)(2,1)} fusion(bf16[1,4,128,1536]{2,3,1,0:T(8,128)(2,1)} %bitcast.47, bf16[1,4,128,1536]{2,3,1,0:T(8,128)(2,1)} %bitcast.46, pred[]{:T(512)S(6)} %eq.35), kind=kLoop, calls=%fused_computation.15 | loop fusion | flops 4718592 | bytes 6291457 | tf_op jit(solution)/shard_map/transpose | solution.py:303
  157.1 4.7 %copy.80 = bf16[4,2,128,1536]{3,2,1,0:T(8,128)(2,1)} copy(bf16[4,2,128,1536]{2,3,0,1:T(8,128)(2,1)} %fusion.3) | data formatting | bytes 6291456 | tf_op jit(solution)/shard_map/transpose | solution.py:303
  161.8 4.8 %fusion.18 = f32[1024,1024]{0,1:T(8,128)S(1)} fusion(bf16[1024,1024]{1,0:T(8,128)(2,1)} %bitcast.231, bf16[1024,1536]{1,0:T(8,128)(2,1)} %bitcast.233), kind=kOutput, calls=%fused_computation.42 | convolution fusion | flops 2147483648 | bytes 8388608 | tf_op jit(solution)/shard_map/dot_general | solution.py:399
  166.5 2.2 multiply_convert_fusion.1
  168.7 2.4 convolution_convert_fusion
  171.1 2.4 fusion.13
  173.5 1.3 convolution_convert_fusion.1
  175.1 1.3 convolution_convert_fusion.2
  176.4 1.3 fusion.22
  178.8 37.6 %shard_map.224 = f32[128,1024]{1,0:T(8,128)S(1)} custom-call(bf16[4,2,2,128,1024]{4,3,2,1,0:T(8,128)(2,1)S(1)} %pad_maximum_fusion.x_ref), custom_call_target="tpu_custom_call" | custom-call | tf_op jit(solution)/shard_map/pallas_call | solution.py:193
  217.3 1.8 fusion.82
  219.0 10.3 %shard_map.225 = (bf16[2,2,64,1024]{3,2,1,0:T(8,128)(2,1)}, bf16[2,2,64,1024]{3,2,1,0:T(8,128)(2,1)}) custom-call(bf16[64,1024]{1,0:T(8,128)(2,1)} %get-tuple-element.29.refs_0_, bf16[64,1024]{1,0:T(8,128)(2,1)} %get-tuple-element.39.refs_1_), custom_call_target="tpu_custom_call" | custom-call | tf_op jit(solution)/shard_map/pallas_call | solution.py:102
  229.4 1.5 convolution_convert_fusion.7
  231.6 2.9 convolution_bitcast_fusion
  234.5 1.1 concatenate.81
  235.6 0.8 copy.86
  236.5 2.8 fusion.89
  239.3 5.0 %fusion.26 = f32[512,2,64]{0,2,1:T(8,128)} fusion(bf16[256,2,2,64]{0,3,2,1:T(8,128)(2,1)S(1)} %bitcast.278, f32[2,512,256,2]{2,1,3,0:T(8,128)} %fusion.89, pred[256,512]{0,1:T(8,128)(4,1)S(1)} %copy-done.19, f32[2,2,256,512]{2,3,1,0:T(8,128)} %get-tuple-element.66, f32[2,2,256]{2,1,0:T(2,128)S(1)} %get-tuple-element.65), kind=kOutput, calls=%fused_computation.60 | convolution fusion | flops 70845952 | bytes 4722688 | tf_op jit(solution)/shard_map/kgrs,rkgd->skd/dot_general | solution.py:465
  244.3 1.1 mul.442
  245.4 0.8 copy.85
  246.2 1.8 fusion.55
  248.1 1.8 copy.87
  249.8 1.5 collective-permute-start.10
  251.3 5.0 %convolution_multiply_fusion = f32[2,64,2,256]{3,1,2,0:T(8,128)} fusion(bf16[512,2,64,1]{0,2,3,1:T(8,128)(2,1)} %bitcast.282, f32[2,512,256,2]{2,1,3,0:T(8,128)} %fusion.89, pred[256,512]{0,1:T(8,128)(4,1)} %copy-done.18, f32[2,2,256,512]{2,3,1,0:T(8,128)} %get-tuple-element.66, f32[2,2,256]{2,1,0:T(2,128)S(1)} %get-tuple-element.65), kind=kOutput, calls=%fused_computation.61 | convolution fusion | flops 70845952 | bytes 4722688 | tf_op jit(solution)/shard_map/kgrs,skd->rkgd/dot_general | solution.py:461
  256.3 1.0 subtract_convert_fusion
  258.8 2.1 copy.89
  260.9 2.2 convolution_convert_fusion.4
  263.1 1.0 add.218
  264.8 3.0 fusion.4
  267.9 4.5 %all-to-all-start.1 = ((bf16[4,128,1536]{2,1,0:T(8,128)(2,1)}), bf16[4,128,1536]{2,1,0:T(8,128)(2,1)}, u32[]{:S(2)}, u32[]{:S(2)}) async-start(bf16[4,128,1536]{2,1,0:T(8,128)(2,1)} %fusion.4), calls=%async_computation.1 | async-start | bytes 3145728 | tf_op jit(solution)/shard_map/all_to_all | solution.py:427
  272.9 7.2 %shard_map.226 = f32[64,1024]{1,0:T(8,128)S(1)} custom-call(bf16[2,2,64,1024]{3,2,1,0:T(8,128)(2,1)S(1)} %bitcast.224), custom_call_target="tpu_custom_call" | custom-call | tf_op jit(solution)/shard_map/pallas_call | solution.py:193
  281.7 8.2 %shard_map.227 = (bf16[2,2,64,1024]{3,2,1,0:T(8,128)(2,1)}, f32[2,2,8,1024]{3,2,1,0:T(8,128)}) custom-call(bf16[64,1024]{1,0:T(8,128)(2,1)} %fusion.50.refs_0_, f32[8,1024]{1,0:T(8,128)} %select_maximum_fusion.refs_1_), custom_call_target="tpu_custom_call" | custom-call | tf_op jit(solution)/shard_map/pallas_call | solution.py:102
  289.9 0.9 reduce_sum.105
  291.6 36.4 %shard_map.228 = f32[144,768]{1,0:T(8,128)S(1)} custom-call(bf16[4,2,144,768]{3,2,1,0:T(8,128)(2,1)S(1)} %fusion.20.x_ref), custom_call_target="tpu_custom_call" | custom-call | tf_op jit(solution)/shard_map/pallas_call | solution.py:193
  329.9 3.0 reshape.500
  333.6 1.1 copy.95
  334.7 1.1 copy.96
  335.8 1.1 copy.97
  (151 shorter events, 22.4 us)
Async XLA Ops:
  0.6 14.5 %copy-start.13 = (bf16[16,128,128]{2,1,0:T(8,128)(2,1)S(1)}, bf16[16,128,128]{2,1,0:T(8,128)(2,1)}, u32[]{:S(2)}) copy-start(bf16[16,128,128]{2,1,0:T(8,128)(2,1)} %param.21) | copy-start | bytes 1572868
  1.6 87.8 %collective-permute-start.5 = (bf16[64,1024]{1,0:T(8,128)(2,1)S(1)}, bf16[64,1024]{1,0:T(8,128)(2,1)S(1)}, u32[]{:S(2)}, u32[]{:S(2)}) collective-permute-start(bf16[64,1024]{1,0:T(8,128)(2,1)S(1)} %constant_dynamic-slice_fusion.1), channel_id=1, source_target_pairs={{0,24},{8,0},{16,8},{24,16},{1,25},{9,1},{17,9},{25,17},{2,26},{10... | collective-permute-start | bytes 393224 | tf_op jit(solution)/shard_map/ppermute | solution.py:230
  6.7 82.7 %collective-permute-start.6 = (bf16[64,1024]{1,0:T(8,128)(2,1)S(1)}, bf16[64,1024]{1,0:T(8,128)(2,1)S(1)}, u32[]{:S(2)}, u32[]{:S(2)}) collective-permute-start(bf16[64,1024]{1,0:T(8,128)(2,1)S(1)} %constant_dynamic-slice_fusion.1), channel_id=1, source_target_pairs={{0,16},{8,24},{16,0},{24,8},{1,17},{9,25},{17,1},{25,9},{2,18},{10... | collective-permute-start | bytes 393224 | tf_op jit(solution)/shard_map/ppermute | solution.py:230
  7.5 80.2 %collective-permute-start = (f32[16,256]{1,0:T(8,128)S(1)}, f32[16,256]{1,0:T(8,128)S(1)}, u32[]{:S(2)}, u32[]{:S(2)}) collective-permute-start(f32[16,256]{1,0:T(8,128)S(1)} %select_reduce_fusion), channel_id=1, source_target_pairs={{0,24},{8,0},{16,8},{24,16},{1,25},{9,1},{17,9},{25,17},{2,26},{10... | collective-permute-start | bytes 49160 | tf_op jit(solution)/shard_map/ppermute | solution.py:230
  8.0 80.3 %collective-permute-start.1 = (f32[16,256]{1,0:T(8,128)S(1)}, f32[16,256]{1,0:T(8,128)S(1)}, u32[]{:S(2)}, u32[]{:S(2)}) collective-permute-start(f32[16,256]{1,0:T(8,128)S(1)} %select_reduce_fusion), channel_id=1, source_target_pairs={{0,16},{8,24},{16,0},{24,8},{1,17},{9,25},{17,1},{25,9},{2,18},{10... | collective-permute-start | bytes 49160 | tf_op jit(solution)/shard_map/ppermute | solution.py:230
  10.6 78.3 %collective-permute-start.2 = (f32[16,256]{1,0:T(8,128)S(1)}, f32[16,256]{1,0:T(8,128)S(1)}, u32[]{:S(2)}, u32[]{:S(2)}) collective-permute-start(f32[16,256]{1,0:T(8,128)S(1)} %select_reduce_fusion), channel_id=1, source_target_pairs={{0,8},{8,16},{16,24},{24,0},{1,9},{9,17},{17,25},{25,1},{2,10},{10... | collective-permute-start | bytes 49160 | tf_op jit(solution)/shard_map/ppermute | solution.py:230
  16.7 4.6 %copy-start.29 = (bf16[128]{0:T(256)(128)(2,1)S(1)}, bf16[128]{0:T(256)(128)(2,1)}, u32[]{:S(2)}) copy-start(bf16[128]{0:T(256)(128)(2,1)} %param.23) | copy-start | bytes 772
  16.7 4.6 %copy-start.30 = (bf16[128]{0:T(256)(128)(2,1)S(1)}, bf16[128]{0:T(256)(128)(2,1)}, u32[]{:S(2)}) copy-start(bf16[128]{0:T(256)(128)(2,1)} %param.22) | copy-start | bytes 772
  16.7 5.2 %copy-start.25 = (bf16[128,256]{1,0:T(8,128)(2,1)S(1)}, bf16[128,256]{1,0:T(8,128)(2,1)}, u32[]{:S(2)}) copy-start(bf16[128,256]{1,0:T(8,128)(2,1)} %param.18) | copy-start | bytes 196612
  16.7 5.2 %copy-start.26 = (bf16[128,256]{1,0:T(8,128)(2,1)S(1)}, bf16[128,256]{1,0:T(8,128)(2,1)}, u32[]{:S(2)}) copy-start(bf16[128,256]{1,0:T(8,128)(2,1)} %param.15) | copy-start | bytes 196612
  16.7 5.2 %copy-start.27 = (bf16[128,128]{1,0:T(8,128)(2,1)S(1)}, bf16[128,128]{1,0:T(8,128)(2,1)}, u32[]{:S(2)}) copy-start(bf16[128,128]{1,0:T(8,128)(2,1)} %param.17) | copy-start | bytes 98308
  16.8 5.2 %copy-start.28 = (bf16[128,128]{1,0:T(8,128)(2,1)S(1)}, bf16[128,128]{1,0:T(8,128)(2,1)}, u32[]{:S(2)}) copy-start(bf16[128,128]{1,0:T(8,128)(2,1)} %param.16) | copy-start | bytes 98308
  16.8 64.7 %copy-start.5 = (bf16[256,1024]{1,0:T(8,128)(2,1)S(1)}, bf16[256,1024]{1,0:T(8,128)(2,1)}, u32[]{:S(2)}) copy-start(bf16[256,1024]{1,0:T(8,128)(2,1)} %param.14) | copy-start | bytes 1572868
  16.8 80.3 %all-to-all-start = ((bf16[4,128,1536]{1,2,0:T(8,128)(2,1)}), bf16[4,128,1536]{1,2,0:T(8,128)(2,1)}, u32[]{:S(2)}, u32[]{:S(2)}) async-start(bf16[4,128,1536]{1,2,0:T(8,128)(2,1)} %pad_maximum_fusion.3), calls=%async_computation | async-start | bytes 3145728 | tf_op jit(solution)/shard_map/all_to_all | solution.py:301
  81.7 2.5 copy-start
  87.3 12.7 %copy-start.20 = (bf16[256,4,64]{0,2,1:T(8,128)(2,1)}, bf16[256,4,64]{0,2,1:T(8,128)(2,1)S(1)}, u32[]{:S(2)}) copy-start(bf16[256,4,64]{0,2,1:T(8,128)(2,1)S(1)} %pad_maximum_fusion.11) | copy-start | bytes 393220
  87.5 12.5 %copy-start.18 = (pred[256,512]{0,1:T(8,128)(4,1)}, pred[256,512]{0,1:T(8,128)(4,1)S(1)}, u32[]{:S(2)}) copy-start(pred[256,512]{0,1:T(8,128)(4,1)S(1)} %fusion.45) | copy-start | bytes 393220
  87.7 6.9 %collective-permute-start.7 = (bf16[64,1024]{1,0:T(8,128)(2,1)S(1)}, bf16[64,1024]{1,0:T(8,128)(2,1)S(1)}, u32[]{:S(2)}, u32[]{:S(2)}) collective-permute-start(bf16[64,1024]{1,0:T(8,128)(2,1)S(1)} %constant_dynamic-slice_fusion.1), channel_id=1, source_target_pairs={{0,8},{8,16},{16,24},{24,0},{1,9},{9,17},{17,25},{25,1},{2,10},{10... | collective-permute-start | bytes 393224 | tf_op jit(solution)/shard_map/ppermute | solution.py:230
  88.3 8.6 %collective-permute-start.3 = (bf16[256,256]{1,0:T(8,128)(2,1)S(1)}, bf16[256,256]{1,0:T(8,128)(2,1)S(1)}, u32[]{:S(2)}, u32[]{:S(2)}) collective-permute-start(bf16[256,256]{1,0:T(8,128)(2,1)S(1)} %pad_maximum_fusion.10), channel_id=1, source_target_pairs={{0,4},{4,0},{1,5},{5,1},{2,6},{6,2},{3,7},{7,3},{8,12},{12,8},{9,1... | collective-permute-start | bytes 393224 | tf_op jit(solution)/shard_map/ppermute | solution.py:213
  95.3 10.0 %collective-permute-start.8 = (bf16[4,64,1024]{2,1,0:T(8,128)(2,1)S(1)}, bf16[4,64,1024]{2,1,0:T(8,128)(2,1)S(1)}, u32[]{:S(2)}, u32[]{:S(2)}) collective-permute-start(bf16[4,64,1024]{2,1,0:T(8,128)(2,1)S(1)} %gather_fusion.2), channel_id=1, source_target_pairs={{0,2},{1,3},{2,0},{3,1},{4,6},{5,7},{6,4},{7,5},{8,10},{9,11},{10,... | collective-permute-start | bytes 1572872 | tf_op jit(solution)/shard_map/ppermute | solution.py:230
  97.1 8.2 %copy-start.23 = (bf16[512,128]{0,1:T(8,128)(2,1)}, bf16[512,128]{0,1:T(8,128)(2,1)S(1)}, u32[]{:S(2)}) copy-start(bf16[512,128]{0,1:T(8,128)(2,1)S(1)} %copy.74) | copy-start | bytes 393220
  97.1 55.2 %collective-permute-start.4 = (bf16[4,128,1536]{1,2,0:T(8,128)(2,1)}, bf16[4,128,1536]{1,2,0:T(8,128)(2,1)}, u32[]{:S(2)}, u32[]{:S(2)}) collective-permute-start(bf16[4,128,1536]{1,2,0:T(8,128)(2,1)} %all-to-all-done), channel_id=1, source_target_pairs={{0,4},{4,0},{1,5},{5,1},{2,6},{6,2},{3,7},{7,3},{8,12},{12,8},{9,1... | collective-permute-start | bytes 4718600 | tf_op jit(solution)/shard_map/ppermute | solution.py:213
  100.1 6.0 %copy-start.12 = (bf16[512,128]{0,1:T(8,128)(2,1)}, bf16[512,128]{0,1:T(8,128)(2,1)S(1)}, u32[]{:S(2)}) copy-start(bf16[512,128]{0,1:T(8,128)(2,1)S(1)} %copy.73) | copy-start | bytes 393220
  105.4 0.9 copy-start.21
  106.0 37.4 %collective-permute-start.9 = (bf16[2,4,64,1024]{3,2,1,0:T(8,128)(2,1)S(1)}, bf16[2,4,64,1024]{3,2,1,0:T(8,128)(2,1)S(1)}, u32[]{:S(2)}, u32[]{:S(2)}) collective-permute-start(bf16[2,4,64,1024]{3,2,1,0:T(8,128)(2,1)S(1)} %gather_fusion.3), channel_id=1, source_target_pairs={{0,1},{1,0},{2,3},{3,2},{4,5},{5,4},{6,7},{7,6},{8,9},{9,8},{10,11... | collective-permute-start | bytes 3145736 | tf_op jit(solution)/shard_map/ppermute | solution.py:230
  108.4 1.5 copy-start.11
  143.4 1.0 copy-start.9
  161.7 4.8 %copy-start.1 = (bf16[4,2,128,1536]{3,2,1,0:T(8,128)(2,1)S(1)}, bf16[4,2,128,1536]{3,2,1,0:T(8,128)(2,1)}, u32[]{:S(2)}) copy-start(bf16[4,2,128,1536]{3,2,1,0:T(8,128)(2,1)} %copy.80) | copy-start | bytes 9437188
  168.7 2.4 copy-start.3
  173.5 1.6 copy-start.4
  177.7 87.1 %collective-permute-start.11 = (bf16[4,128,1536]{2,1,0:T(8,128)(2,1)}, bf16[4,128,1536]{2,1,0:T(8,128)(2,1)}, u32[]{:S(2)}, u32[]{:S(2)}) collective-permute-start(bf16[4,128,1536]{2,1,0:T(8,128)(2,1)} %fusion.22), channel_id=1, source_target_pairs={{0,4},{4,0},{1,5},{5,1},{2,6},{6,2},{3,7},{7,3},{8,12},{12,8},{9,1... | collective-permute-start | bytes 4718600 | tf_op jit(solution)/shard_map/ppermute | solution.py:213
  230.9 0.7 copy-start.17
  236.5 2.8 copy-start.19
  236.5 2.8 copy-start.22
  249.8 13.2 %collective-permute-start.10 = (f32[256,256]{0,1:T(8,128)}, f32[256,256]{0,1:T(8,128)}, u32[]{:S(2)}, u32[]{:S(2)}) collective-permute-start(f32[256,256]{0,1:T(8,128)} %copy.87), channel_id=1, source_target_pairs={{0,4},{4,0},{1,5},{5,1},{2,6},{6,2},{3,7},{7,3},{8,12},{12,8},{9,1... | collective-permute-start | bytes 786440 | tf_op jit(solution)/shard_map/ppermute | solution.py:213
  258.8 4.3 %copy-start.7 = (f32[256,256]{0,1:T(8,128)S(1)}, f32[256,256]{0,1:T(8,128)}, u32[]{:S(2)}) copy-start(f32[256,256]{0,1:T(8,128)} %copy.88) | copy-start | bytes 786436
  264.1 0.7 copy-start.10
  267.8 4.5 %slice-start = ((f32[256,256]{0,1:T(8,128)}), f32[256,128]{0,1:T(8,128)S(1)}, s32[]{:S(2)}) async-start(f32[256,256]{0,1:T(8,128)} %copy-done.10), calls=%async_computation.2 | async-start | bytes 262144 | tf_op jit(solution)/shard_map/slice | solution.py:480
  267.8 4.6 %copy-start.16 = (bf16[4,2,128,768]{3,2,1,0:T(8,128)(2,1)S(1)}, bf16[4,2,128,768]{3,2,1,0:T(8,128)(2,1)}, u32[]{:S(2)}) copy-start(bf16[4,2,128,768]{3,2,1,0:T(8,128)(2,1)} %get-tuple-element.18) | copy-start | bytes 4718596
  267.8 4.6 %copy-start.24 = (bf16[256,4,64]{0,2,1:T(8,128)(2,1)S(1)}, bf16[256,4,64]{0,2,1:T(8,128)(2,1)}, u32[]{:S(2)}) copy-start(bf16[256,4,64]{0,2,1:T(8,128)(2,1)} %pad_maximum_fusion.12) | copy-start | bytes 393220
  267.9 62.0 %all-to-all-start.1 = ((bf16[4,128,1536]{2,1,0:T(8,128)(2,1)}), bf16[4,128,1536]{2,1,0:T(8,128)(2,1)}, u32[]{:S(2)}, u32[]{:S(2)}) async-start(bf16[4,128,1536]{2,1,0:T(8,128)(2,1)} %fusion.4), calls=%async_computation.1 | async-start | bytes 3145728 | tf_op jit(solution)/shard_map/all_to_all | solution.py:427
  272.3 7.8 %copy-start.6 = (bf16[256,1024]{1,0:T(8,128)(2,1)S(1)}, bf16[256,1024]{1,0:T(8,128)(2,1)}, u32[]{:S(2)}) copy-start(bf16[256,1024]{1,0:T(8,128)(2,1)} %param.14) | copy-start | bytes 1572868
  272.4 8.6 %copy-start.8 = (f32[64,1024]{1,0:T(8,128)S(1)}, f32[64,1024]{1,0:T(8,128)}, u32[]{:S(2)}) copy-start(f32[64,1024]{1,0:T(8,128)} %get-tuple-element.30) | copy-start | bytes 786436
  280.1 11.3 %copy-start.2 = (bf16[4,2,128,256]{3,2,1,0:T(8,128)(2,1)S(1)}, bf16[4,2,128,256]{3,2,1,0:T(8,128)(2,1)}, u32[]{:S(2)}) copy-start(bf16[4,2,128,256]{3,2,1,0:T(8,128)(2,1)} %convolution_convert_fusion.4) | copy-start | bytes 1572868
  334.7 2.2 copy-start.14
  335.8 1.9 copy-start.15

commit v2 on v1

--- a/solution.py
+++ b/solution.py
@@ -1,4 +1,5 @@
 import functools
+import math
 
 import jax
 import jax.numpy as jnp
@@ -41,79 +42,92 @@
     pl.semaphore_wait(barrier, total)
 
 
-def gather_kernel(dims, count, *refs):
+def gather_kernel(jobs, *refs):
+    count = len(jobs)
     sources, outs = refs[:count], refs[count : 2 * count]
     send_sem, recv_sem, own_sem = refs[2 * count :]
-    places = [coordinate(dim) for dim in dims]
-
-    def slot(steps):
+
+    def slot(dims, steps):
         return tuple(
-            lax.rem(place - step + dim[1], dim[1]) for place, step, dim in zip(places, steps, dims)
+            lax.rem(coordinate(dim) - step + dim[1], dim[1]) for step, dim in zip(steps, dims)
         )
 
-    zero = (0,) * len(dims)
-    own = [
-        pltpu.make_async_copy(sources[a], outs[a].at[slot(zero)], own_sem.at[a])
-        for a in range(count)
-    ]
+    own = []
+    for a, dims in enumerate(jobs):
+        at = slot(dims, (0,) * len(dims))
+        own.append(pltpu.make_async_copy(sources[a], outs[a].at[at], own_sem.at[a]))
+    greet(unique(dim for dims in jobs for dim in dims))
+    sent = []
+    queues = [[] for _ in jobs]
+
+    def forward(a, steps, level, source):
+        dims = jobs[a]
+        for s in range(level, len(dims)):
+            for k in range(1, dims[s][1]):
+                index = len(sent)
+                copy = pltpu.make_async_remote_copy(
+                    src_ref=source,
+                    dst_ref=outs[a].at[slot(dims, steps)],
+                    send_sem=send_sem.at[index],
+                    recv_sem=recv_sem.at[index],
+                    device_id=device_at(dims[s], lax.rem(coordinate(dims[s]) + k, dims[s][1])),
+                    device_id_type=MESH,
+                )
+                copy.start()
+                sent.append(copy)
+                queues[a].append((steps[:s] + (k,) + steps[s + 1 :], s + 1, copy))
+
+    for a, dims in enumerate(jobs):
+        forward(a, (0,) * len(dims), 0, sources[a])
     for copy in own:
         copy.start()
-    greet(dims)
-    queue = [(zero, 0, None)]
-    sent = []
-    at = 0
-    while at < len(queue):
-        steps, level, arriving = queue[at]
-        at += 1
-        if arriving is not None:
-            for copy in arriving:
-                copy.wait_recv()
-        for s in range(level, len(dims)):
-            for k in range(1, dims[s][1]):
-                copies = []
-                for a in range(count):
-                    index = len(sent)
-                    source = sources[a] if arriving is None else outs[a].at[slot(steps)]
-                    copy = pltpu.make_async_remote_copy(
-                        src_ref=source,
-                        dst_ref=outs[a].at[slot(steps)],
-                        send_sem=send_sem.at[index],
-                        recv_sem=recv_sem.at[index],
-                        device_id=device_at(dims[s], lax.rem(places[s] + k, dims[s][1])),
-                        device_id_type=MESH,
-                    )
-                    copy.start()
-                    copies.append(copy)
-                    sent.append(copy)
-                queue.append((steps[:s] + (k,) + steps[s + 1 :], s + 1, copies))
+    for a, dims in enumerate(jobs):
+        at = 0
+        while at < len(queues[a]):
+            steps, level, copy = queues[a][at]
+            at += 1
+            copy.wait_recv()
+            forward(a, steps, level, outs[a].at[slot(dims, steps)])
     for copy in sent:
         copy.wait_send()
     for copy in own:
         copy.wait()
 
 
-def gather_pieces(arrays, dims, number):
-    sizes = tuple(dim[1] for dim in dims)
-    total = 1
-    for size in sizes:
-        total *= size
-    copies = (total - 1) * len(arrays)
+def unique(dims):
+    kept = []
+    for dim in dims:
+        if dim not in kept:
+            kept.append(dim)
+    return kept
+
+
+def gather_pieces(arrays, jobs, number):
+    shapes, copies = [], 0
+    for a, dims in zip(arrays, jobs):
+        sizes = tuple(dim[1] for dim in dims)
+        shapes.append(jax.ShapeDtypeStruct(sizes + a.shape, a.dtype))
+        copies += math.prod(sizes) - 1
     any_spec = pl.BlockSpec(memory_space=pl.ANY)
     return pl.pallas_call(
-        functools.partial(gather_kernel, dims, len(arrays)),
-        out_shape=tuple(jax.ShapeDtypeStruct(sizes + a.shape, a.dtype) for a in arrays),
+        functools.partial(gather_kernel, jobs),
+        out_shape=tuple(shapes),
         in_specs=[any_spec] * len(arrays),
         out_specs=tuple(any_spec for _ in arrays),
         scratch_shapes=[
-            pltpu.SemaphoreType.DMA((max(copies, 1),)),
-            pltpu.SemaphoreType.DMA((max(copies, 1),)),
+            pltpu.SemaphoreType.DMA((copies,)),
+            pltpu.SemaphoreType.DMA((copies,)),
             pltpu.SemaphoreType.DMA((len(arrays),)),
         ],
         compiler_params=pltpu.CompilerParams(collective_id=number, has_side_effects=True),
     )(*arrays)
 
 
-def reduce_kernel(halves, last, x_ref, out_ref, *scratch):
+def reduce_kernel(halves, last, side, *refs):
+    if side is None:
+        x_ref, out_ref, *scratch = refs
+    else:
+        x_ref, given_ref, out_ref, taken_ref, *scratch, side_send, side_recv = refs
     stages = len(halves)
     landed = scratch[:stages]
     summed = scratch[stages : 2 * stages]
@@ -122,7 +136,7 @@
     n = last[1]
     place = coordinate(last)
     mine = [coordinate(dim) for dim in halves]
-    greet(list(halves) + [last])
+    greet(list(halves) + [last] + ([] if side is None else [side]))
     order = [lax.rem(place + k, n) for k in list(range(1, n)) + [0]]
 
     def held(stage):
@@ -152,6 +166,16 @@
 
     for i in range(n):
         push(0, i)
+    if side is not None:
+        exchange = pltpu.make_async_remote_copy(
+            src_ref=given_ref.at[1 - coordinate(side)],
+            dst_ref=taken_ref,
+            send_sem=side_send,
+            recv_sem=side_recv,
+            device_id=device_at(side, 1 - coordinate(side)),
+            device_id_type=MESH,
+        )
+        exchange.start()
     outgoing = []
     for tick in range(n + stages - 1):
         for stage in range(stages):
@@ -182,30 +206,42 @@
             copy.wait_send()
     for copy in outgoing:
         copy.wait_send()
-
-
-def reduce_pieces(x, halves, last, number):
+    if side is not None:
+        exchange.wait()
+
+
+def reduce_pieces(x, halves, last, number, given=None, side=None):
     rows, columns = x.shape[-2:]
     n = last[1]
     stages = len(halves)
     shapes = [(n,) + (2,) * (stages - 1 - s) + (rows, columns) for s in range(stages)]
     vmem = pl.BlockSpec(memory_space=pltpu.VMEM)
+    out_shape, in_specs, out_specs = [jax.ShapeDtypeStruct((rows, columns), jnp.float32)], [vmem], [vmem]
+    operands, semaphores = [x], []
+    if side is not None:
+        any_spec = pl.BlockSpec(memory_space=pl.ANY)
+        out_shape.append(jax.ShapeDtypeStruct(given.shape[1:], given.dtype))
+        in_specs.append(any_spec)
+        out_specs.append(any_spec)
+        operands.append(given)
+        semaphores = [pltpu.SemaphoreType.DMA, pltpu.SemaphoreType.DMA]
     return pl.pallas_call(
-        functools.partial(reduce_kernel, tuple(halves), last),
-        out_shape=jax.ShapeDtypeStruct((rows, columns), jnp.float32),
-        in_specs=[vmem],
-        out_specs=vmem,
+        functools.partial(reduce_kernel, tuple(halves), last, side),
+        out_shape=tuple(out_shape),
+        in_specs=in_specs,
+        out_specs=tuple(out_specs),
         scratch_shapes=[pltpu.VMEM(shape, x.dtype) for shape in shapes]
         + [pltpu.VMEM(shape, x.dtype) for shape in shapes]
         + [
             pltpu.VMEM((n - 1, rows, columns), x.dtype),
             pltpu.SemaphoreType.DMA(((stages + 1) * n,)),
             pltpu.SemaphoreType.DMA(((stages + 1) * n,)),
-        ],
+        ]
+        + semaphores,
         compiler_params=pltpu.CompilerParams(
             collective_id=number, has_side_effects=True, vmem_limit_bytes=VMEM_BYTES
         ),
-    )(x)
+    )(*operands)
 
 
 def swapped(array, axis, step):
@@ -298,17 +334,7 @@
 
     packed = jnp.concatenate([to_owner(w_gate), to_owner(w_up), to_owner(w_down)], axis=2)
     packed = jnp.repeat(packed, copies, axis=0)
-    from_fsdp = lax.all_to_all(packed, "fsdp", 0, 0, tiled=True)
-    both_context = joined(from_fsdp, swapped(from_fsdp, "context", 1), context_index)
-    expert_weight = jnp.swapaxes(both_context, 0, 1).reshape(model_width, 3 * columns)
-    gate_up_weight = expert_weight[:, : 2 * columns]
-    down_weight = expert_weight[:, 2 * columns :]
-
     cot_piece = lax.dynamic_slice_in_dim(cotangent, tensor_index * piece, piece, 0)
-    cot_f = by_fsdp(cot_piece, fsdp_dim)
-    cot_y = by_fsdp(cot_f, y_dim)
-    cot_t = by_fsdp(cot_y, core_dim)
-    cot_all = jnp.transpose(cot_t, (2, 1, 0, 3, 4)).reshape(-1, model_width)
     dense_gates = jnp.sum(
         jnp.where(
             routes.T[None, :, :] == jnp.arange(EXPERTS, dtype=jnp.int32)[:, None, None],
@@ -317,6 +343,23 @@
         ),
         axis=1,
     )
+    attn_shard = jnp.concatenate(
+        [w_query, key_projection_weight, value_projection_weight, w_out], axis=1
+    )
+    gain_shard = jnp.pad(
+        jnp.stack([norm_in, norm_mid]).astype(jnp.float32), ((0, 6), (0, 128 - depth))
+    )
+    attn_weight, gains = gather_pieces(
+        [attn_shard, gain_shard], [[fsdp_all, context_dim]] * 2, 1
+    )
+    packed, cot_first, dense_gates, attn_weight = lax.optimization_barrier(
+        (packed, cot_piece, dense_gates, attn_weight)
+    )
+    from_fsdp = lax.all_to_all(packed, "fsdp", 0, 0, tiled=True)
+    cot_f = by_fsdp(cot_first, fsdp_dim)
+    cot_y = by_fsdp(cot_f, y_dim)
+    cot_t = by_fsdp(cot_y, core_dim)
+    cot_all = jnp.transpose(cot_t, (2, 1, 0, 3, 4)).reshape(-1, model_width)
     gates_all = by_fsdp(dense_gates, fsdp_dim)
     gates_own = lax.dynamic_slice_in_dim(
         gates_all, coordinate(fsdp_dim) * per_owner, per_owner, 1
@@ -324,13 +367,6 @@
     gates_rows = jnp.transpose(gates_own, (0, 2, 1)).reshape(-1, per_owner)
     gates_wide = jnp.repeat(gates_rows, hidden_width, axis=1)
 
-    attn_shard = jnp.concatenate(
-        [w_query, key_projection_weight, value_projection_weight, w_out], axis=1
-    )
-    gain_shard = jnp.pad(
-        jnp.stack([norm_in, norm_mid]).astype(jnp.float32), ((0, 6), (0, 128 - depth))
-    )
-    attn_weight, gains = gather_pieces([attn_shard, gain_shard], [fsdp_all, context_dim], 1)
     attn_weight = attn_weight.reshape(model_width, -1)
     gains = gains[..., :depth].reshape(-1, 8, depth)
     gain_one = gains[:, 0, :].reshape(-1)
@@ -387,14 +423,19 @@
     def by_tensor(part):
         return part.astype(jnp.bfloat16).reshape(tensor // 2, 2, piece, model_width)
 
-    attended = reduce_pieces(by_tensor(attn_part), [core_dim], y_dim, 2)
+    attended = reduce_pieces(by_tensor(attn_part), [core_dim], y_dim, 2)[0]
     start_row = tensor_index * piece
     own_inputs = lax.dynamic_slice_in_dim(tokens, start_row, piece, 0).astype(jnp.float32)
     own_scale_in = lax.dynamic_slice_in_dim(scale_in, start_row, piece, 0)
     hidden_state = own_inputs + attended
     scale_mid = rms_scale(hidden_state)
     normed_mid = (hidden_state * scale_mid * gain_two).astype(jnp.bfloat16)
-    (expert_rows,) = gather_pieces([normed_mid], [fsdp_dim, y_dim, core_dim], 3)
+    expert_rows, both_context = gather_pieces(
+        [normed_mid, from_fsdp], [[fsdp_dim, y_dim, core_dim], [context_dim]], 3
+    )
+    expert_weight = jnp.swapaxes(both_context, 0, 1).reshape(model_width, 3 * columns)
+    gate_up_weight = expert_weight[:, : 2 * columns]
+    down_weight = expert_weight[:, 2 * columns :]
     expert_rows = expert_rows.reshape(-1, model_width)
     act = jnp.dot(expert_rows, gate_up_weight, preferred_element_type=jnp.float32)
     gate_act, up_act = act[:, :columns], act[:, columns:]
@@ -413,7 +454,6 @@
     ).astype(jnp.bfloat16)
     split = (groups, tensor // 2, 2, piece, model_width)
     both_parts = jnp.concatenate([moe_part.reshape(split), d_mid_part.reshape(split)], axis=3)
-    back = reduce_pieces(both_parts, [core_dim, y_dim], fsdp_dim, 4)
     grad_gate_up = lax.dot_general(
         expert_rows, d_act, CONTRACT_ROWS, preferred_element_type=jnp.float32
     )
@@ -421,8 +461,9 @@
     expert_grad = jnp.concatenate([grad_gate_up, grad_down], axis=1).astype(jnp.bfloat16)
     expert_grad = jnp.swapaxes(expert_grad.reshape(fsdp, -1, depth, 3 * columns), 0, 1)
     kept = lax.dynamic_index_in_dim(expert_grad, context_index, 0, False)
-    given = lax.dynamic_index_in_dim(expert_grad, 1 - context_index, 0, False)
-    taken = swapped(given, "context", 1)
+    back, taken = reduce_pieces(
+        both_parts, [core_dim, y_dim], fsdp_dim, 4, expert_grad, context_dim
+    )
     half_grad = (kept.astype(jnp.float32) + taken.astype(jnp.float32)).astype(jnp.bfloat16)
     owned_grad = lax.all_to_all(half_grad, "fsdp", 0, 0, tiled=True).astype(jnp.float32)
     owned_grad = jnp.sum(owned_grad.reshape(groups, copies, depth, 3, per_owner, hidden_width), 1)
@@ -441,7 +482,7 @@
         * jnp.mean(gain_two * d_mid * hidden_state, axis=-1, keepdims=True)
     )
     d_attended, output = gather_pieces(
-        [d_hidden_state.astype(jnp.bfloat16), own_output], [y_dim, core_dim], 5
+        [d_hidden_state.astype(jnp.bfloat16), own_output], [[y_dim, core_dim]] * 2, 5
     )
     d_attended = d_attended.reshape(local_rows, model_width)
     output = output.reshape(local_rows, model_width)
@@ -484,7 +525,7 @@
     d_in_part = lax.dot_general(
         d_projected, in_weight, CONTRACT_COLUMNS, preferred_element_type=jnp.float32
     )
-    d_in = reduce_pieces(by_tensor(d_in_part), [core_dim], y_dim, 6)
+    d_in = reduce_pieces(by_tensor(d_in_part), [core_dim], y_dim, 6)[0]
     d_in_weight = lax.dot_general(
         normed_in, d_projected, CONTRACT_ROWS, preferred_element_type=jnp.float32
     )
@@ -497,7 +538,7 @@
         * jnp.mean(gain_one * d_in * own_inputs, axis=-1, keepdims=True)
     ).astype(jnp.bfloat16)
     d_gains = jnp.pad(jnp.stack([d_gain_in, d_gain_mid]), ((0, 6), (0, 0)))
-    d_tokens, d_gains = gather_pieces([d_inputs, d_gains], [y_dim, core_dim], 7)
+    d_tokens, d_gains = gather_pieces([d_inputs, d_gains], [[y_dim, core_dim]] * 2, 7)
     d_tokens = d_tokens.reshape(local_rows, model_width)
     d_gains = jnp.sum(d_gains, axis=(0, 1))[:2]
     d_attn = jnp.concatenate([d_in_weight, d_out_weight], axis=1).astype(jnp.bfloat16)
@@ -506,7 +547,7 @@
     d_gains = jnp.pad(d_gains, ((0, 0), (0, 0), (0, 14), (0, d_attn.shape[3] - depth)))
     owned = reduce_pieces(
         jnp.concatenate([d_attn, d_gains], axis=2), [context_dim], fsdp_all, 8
-    )
+    )[0]
     first, second = q_width, q_width + k_width
     third = q_width + 2 * k_width
     return (

time: 340 us -> 348 us (1.024)
  waiting for transfers between devices: 10.4 us -> 30.3 us
  Pallas kernels: 186 us -> 196 us
  local copies, waits for them, and re-layouts: 47.3 us -> 37.4 us
  other arithmetic: 26.2 us -> 17 us
  matrix products: 42.3 us -> 38.7 us
    ppermute x8, waiting for transfers between devices: 10.3 us -> 23.7 us  [by_fsdp(): blocks.append(lax.ppermute(array, axis, pairs))]
    pallas_call x8, Pallas kernels: 186 us -> 196 us  [the longest x4 114 us: gather_pieces(): pl.pallas_call(functools.partial(gather_kernel, jobs), out_shape=tuple(sh...]
    ppermute x4 -> x2, waiting for transfers between devices: 0.01 us -> 6.59 us  [swapped(): return lax.ppermute(array, axis, [(i, i ^ step) for i in range(size)])]
    transpose x1, other arithmetic: 4.78 us -> 0.25 us  [local(): jnp.swapaxes(expert_grad.reshape(fsdp, -1, depth, 3 * columns), 0, 1)]
    unnamed x67 -> x70, local copies, waits for them, and re-layouts: 7.4 us -> 3.94 us
  transfers between devices with their start and end apart: 14 -> 12, of which waited for: 2 -> 3; matrix products, arithmetic and copies ran while one was open for 22% -> 9% of each run, Pallas kernels for 55% -> 15%
where the time goes in v2:
time: 348 us; the launch traced here: 347 us
  Pallas kernels  196 us (56%)
  matrix products  38.7 us (11%)
  local copies, waits for them, and re-layouts  37.4 us (11%)
  waiting for transfers between devices  30.3 us (9%)
  starting transfers between devices  26.2 us (8%)
  other arithmetic  17 us (5%)
    pallas_call x4, Pallas kernels, gather_pieces(): pl.pallas_call(functools.partial(gather_kernel, jobs), out_shape=tuple(sh...  114 us
    pallas_call x4, Pallas kernels, reduce_pieces(): pl.pallas_call(functools.partial(reduce_kernel, tuple(halves), last, side...  81.9 us
    ppermute x8, waiting for transfers between devices, by_fsdp(): blocks.append(lax.ppermute(array, axis, pairs))  23.7 us
    ppermute x8, starting transfers between devices, by_fsdp(): blocks.append(lax.ppermute(array, axis, pairs))  15 us
  transfers between devices with their start and end apart: 12, of which 3 were waited for; matrix products, arithmetic and copies ran while one was open for 9% of the time, Pallas kernels for 15%

profile of v2, /device:TPU:0, one launch (start us, length us, event | category | flops | bytes accessed | tf_op | source)
XLA Modules:
  0.0 347.3 jit_solution(3643793771384882129)
XLA Ops:
  0.7 1.5 copy.141
  3.8 0.9 constant_dynamic-slice_fusion.1
  5.3 0.7 pad_maximum_fusion.10.refs_0_
  6.0 32.2 %shard_map.221 = (bf16[4,2,128,768]{3,2,1,0:T(8,128)(2,1)}, f32[4,2,8,128]{3,2,1,0:T(8,128)}) custom-call(bf16[128,768]{1,0:T(8,128)(2,1)} %pad_maximum_fusion.10.refs_0_, f32[8,128]{1,0:T(8,128)} %fusion.71.refs_1_), custom_call_target="tpu_custom_call" | custom-call | tf_op jit(solution)/shard_map/pallas_call | solution.py:112
  38.3 1.3 pad_maximum_fusion.4
  39.6 6.4 %collective-permute-start.4 = (bf16[64,1024]{1,0:T(8,128)(2,1)S(1)}, bf16[64,1024]{1,0:T(8,128)(2,1)S(1)}, u32[]{:S(2)}, u32[]{:S(2)}) collective-permute-start(bf16[64,1024]{1,0:T(8,128)(2,1)S(1)} %constant_dynamic-slice_fusion.1), channel_id=1, source_target_pairs={{0,24},{8,0},{16,8},{24,16},{1,25},{9,1},{17,9},{25,17},{2,26},{10... | collective-permute-start | bytes 393224 | tf_op jit(solution)/shard_map/ppermute | solution.py:266
  46.1 2.9 collective-permute-start.1
  48.9 2.0 collective-permute-start.2
  50.9 4.3 %all-to-all-start = ((bf16[4,128,1536]{2,1,0:T(8,128)(2,1)}), bf16[4,128,1536]{2,1,0:T(8,128)(2,1)}, u32[]{:S(2)}, u32[]{:S(2)}) async-start(bf16[4,128,1536]{2,1,0:T(8,128)(2,1)} %pad_maximum_fusion.4), calls=%async_computation | async-start | bytes 3145728 | tf_op jit(solution)/shard_map/all_to_all | solution.py:358
  55.3 0.8 fusion.93
  56.4 1.7 fusion.47
  59.0 1.9 gather_fusion.1
  61.4 2.0 collective-permute-start.6
  63.4 1.5 collective-permute-start.3
  65.5 18.7 %collective-permute-done.6 = bf16[64,1024]{1,0:T(8,128)(2,1)S(1)} collective-permute-done((bf16[64,1024]{1,0:T(8,128)(2,1)S(1)}, bf16[64,1024]{1,0:T(8,128)(2,1)S(1)}, u32[]{:S(2)}, u32[]{:S(2)}) %collective-permute-start.6) | collective-permute-done | bytes 131104 | tf_op jit(solution)/shard_map/ppermute | solution.py:266
  84.9 1.6 collective-permute-start.7
  86.8 2.2 fusion.94
  89.1 5.0 %collective-permute-done.7 = bf16[4,64,1024]{2,1,0:T(8,128)(2,1)S(1)} collective-permute-done((bf16[4,64,1024]{2,1,0:T(8,128)(2,1)S(1)}, bf16[4,64,1024]{2,1,0:T(8,128)(2,1)S(1)}, u32[]{:S(2)}, u32[]{:S(2)}) %collective-permute-start.7) | collective-permute-done | bytes 524320 | tf_op jit(solution)/shard_map/ppermute | solution.py:266
  95.1 2.1 convolution_convert_fusion.7
  97.3 1.4 convolution_convert_fusion.5
  98.7 7.2 %shard_map.222 = f32[64,1024]{1,0:T(8,128)S(1)} custom-call(bf16[2,2,64,1024]{3,2,1,0:T(8,128)(2,1)S(1)} %bitcast.218), custom_call_target="tpu_custom_call" | custom-call | tf_op jit(solution)/shard_map/pallas_call | solution.py:228
  106.1 0.8 multiply_convert_fusion.2.refs_0_
  106.9 1.0 copy-done.7
  107.8 1.4 pad_maximum_fusion.2
  109.2 2.0 gather_fusion.4
  111.3 1.8 copy.88
  113.1 2.7 copy.124
  115.8 61.7 %shard_map.223 = (bf16[4,2,2,64,1024]{4,3,2,1,0:T(8,128)(2,1)}, bf16[2,4,128,1536]{3,2,1,0:T(8,128)(2,1)}) custom-call(bf16[64,1024]{1,0:T(8,128)(2,1)} %multiply_convert_fusion.2.refs_0_, bf16[4,128,1536]{2,1,0:T(8,128)(2,1)} %all-to-all-done.refs_1_), custom_call_target="tpu_custom_call" | custom-call | tf_op jit(solution)/shard_map/pallas_call | solution.py:112
  177.5 3.8 %copy.87 = bf16[4,2,128,1536]{3,2,1,0:T(8,128)(2,1)} copy(bf16[4,2,128,1536]{3,2,0,1:T(8,128)(2,1)} %bitcast.231) | data formatting | bytes 6291456 | tf_op jit(solution)/shard_map/transpose | solution.py:436
  181.3 3.9 %copy.89 = bf16[1024,1024]{1,0:T(8,128)(2,1)} copy(bf16[1024,1024]{0,1:T(8,128)(2,1)} %bitcast.234) | data formatting | bytes 4194304 | tf_op jit(solution)/shard_map/dot_general | solution.py:457
  185.3 4.8 %fusion.23 = f32[1024,1024]{0,1:T(8,128)S(1)} fusion(bf16[1024,1024]{1,0:T(8,128)(2,1)} %bitcast.235, bf16[1024,1536]{1,0:T(8,128)(2,1)} %bitcast.226), kind=kOutput, calls=%fused_computation.43 | convolution fusion | flops 2147483648 | bytes 8388608 | tf_op jit(solution)/shard_map/dot_general | solution.py:440
  190.0 2.2 multiply_convert_fusion.1
  192.2 2.4 convolution_convert_fusion
  194.6 2.4 fusion.16
  197.0 1.3 convolution_convert_fusion.1
  198.3 1.0 copy-done.3
  199.4 1.3 fusion.28
  200.9 2.6 pad_maximum_fusion.refs_0_
  203.5 39.1 %shard_map.224 = (f32[128,1024]{1,0:T(8,128)S(1)}, bf16[4,128,1536]{2,1,0:T(8,128)(2,1)S(1)}) custom-call(bf16[4,2,2,128,1024]{4,3,2,1,0:T(8,128)(2,1)} %pad_maximum_fusion.refs_0_, bf16[2,4,128,1536]{3,2,1,0:T(8,128)(2,1)S(1)} %fusion.3.refs_1_), custom_call_target="tpu_custom_call" | custom-call | tf_op jit(solution)/shard_map/pallas_call | solution.py:228
  242.6 0.8 multiply_reduce_fusion
  243.4 1.7 fusion.88
  245.1 10.6 %shard_map.225 = (bf16[2,2,64,1024]{3,2,1,0:T(8,128)(2,1)}, bf16[2,2,64,1024]{3,2,1,0:T(8,128)(2,1)}) custom-call(bf16[64,1024]{1,0:T(8,128)(2,1)} %get-tuple-element.45.refs_0_, bf16[64,1024]{1,0:T(8,128)(2,1)} %get-tuple-element.55.refs_1_), custom_call_target="tpu_custom_call" | custom-call | tf_op jit(solution)/shard_map/pallas_call | solution.py:112
  255.7 1.5 convolution_convert_fusion.6
  257.3 1.8 fusion.95
  259.1 2.2 convolution_bitcast_fusion
  261.3 5.0 %convolution_multiply_fusion = f32[2,64,2,256]{3,1,2,0:T(8,128)} fusion(bf16[512,2,64,1]{0,2,3,1:T(8,128)(2,1)} %bitcast.282, f32[2,512,256,2]{2,1,3,0:T(8,128)} %fusion.95, pred[256,512]{0,1:T(8,128)(4,1)} %copy-done.23, f32[2,2,256,512]{2,3,1,0:T(8,128)} %get-tuple-element.82, f32[2,2,256]{2,1,0:T(2,128)S(1)} %get-tuple-element.81), kind=kOutput, calls=%fused_computation.60 | convolution fusion | flops 70845952 | bytes 4722688 | tf_op jit(solution)/shard_map/kgrs,skd->rkgd/dot_general | solution.py:502
  266.3 5.0 %fusion.32 = f32[512,2,64]{0,2,1:T(8,128)} fusion(bf16[256,2,2,64]{0,3,2,1:T(8,128)(2,1)S(1)} %bitcast.278, f32[2,512,256,2]{2,1,3,0:T(8,128)} %fusion.95, pred[256,512]{0,1:T(8,128)(4,1)S(1)} %copy-done.24, f32[2,2,256,512]{2,3,1,0:T(8,128)} %get-tuple-element.82, f32[2,2,256]{2,1,0:T(2,128)S(1)} %get-tuple-element.81), kind=kOutput, calls=%fused_computation.59 | convolution fusion | flops 70845952 | bytes 4722688 | tf_op jit(solution)/shard_map/kgrs,rkgd->skd/dot_general | solution.py:506
  271.3 2.9 fusion.4
  274.1 4.5 %all-to-all-start.1 = ((bf16[4,128,1536]{2,1,0:T(8,128)(2,1)}), bf16[4,128,1536]{2,1,0:T(8,128)(2,1)}, u32[]{:S(2)}, u32[]{:S(2)}) async-start(bf16[4,128,1536]{2,1,0:T(8,128)(2,1)} %fusion.4), calls=%async_computation.1 | async-start | bytes 3145728 | tf_op jit(solution)/shard_map/all_to_all | solution.py:468
  279.5 0.9 collective-permute-start.9
  281.1 6.6 %collective-permute-done.9 = f32[256,256]{0,1:T(8,128)S(1)} collective-permute-done((f32[256,256]{0,1:T(8,128)S(1)}, f32[256,256]{0,1:T(8,128)S(1)}, u32[]{:S(2)}, u32[]{:S(2)}) %collective-permute-start.9) | collective-permute-done | bytes 262176 | tf_op jit(solution)/shard_map/ppermute | solution.py:249
  288.4 5.9 %shard_map.226 = f32[64,1024]{1,0:T(8,128)S(1)} custom-call(bf16[2,2,64,1024]{3,2,1,0:T(8,128)(2,1)S(1)} %bitcast.219), custom_call_target="tpu_custom_call" | custom-call | tf_op jit(solution)/shard_map/pallas_call | solution.py:228
  295.1 0.8 fusion.56.refs_0_
  295.9 9.6 %shard_map.227 = (bf16[2,2,64,1024]{3,2,1,0:T(8,128)(2,1)}, f32[2,2,8,1024]{3,2,1,0:T(8,128)}) custom-call(bf16[64,1024]{1,0:T(8,128)(2,1)} %fusion.56.refs_0_, f32[8,1024]{1,0:T(8,128)} %select_maximum_fusion.refs_1_), custom_call_target="tpu_custom_call" | custom-call | tf_op jit(solution)/shard_map/pallas_call | solution.py:112
  305.5 0.9 reduce_sum.105
  307.1 29.7 %shard_map.228 = f32[144,768]{1,0:T(8,128)S(1)} custom-call(bf16[4,2,144,768]{3,2,1,0:T(8,128)(2,1)S(1)} %fusion.25.refs_0_), custom_call_target="tpu_custom_call" | custom-call | tf_op jit(solution)/shard_map/pallas_call | solution.py:228
  338.0 0.7 fusion.90
  338.7 3.0 reshape.498
  341.7 0.7 fusion.89
  342.4 1.1 copy.104
  343.5 1.1 copy.105
  344.6 1.1 copy.106
  345.7 0.8 copy.144
  346.5 0.8 copy.145
  (153 shorter events, 11.3 us)
Async XLA Ops:
  0.6 1.8 copy-start.12
  0.7 2.5 copy-start.13
  2.4 2.3 copy-start.32
  2.4 2.3 copy-start.33
  2.4 2.9 copy-start.26
  2.5 2.9 copy-start.27
  2.5 2.9 copy-start.28
  2.5 2.8 copy-start.29
  2.9 35.3 %copy-start.30 = (f32[256,8]{0,1:T(8,128)S(1)}, f32[256,8]{0,1:T(8,128)}, u32[]{:S(2)}) copy-start(f32[256,8]{0,1:T(8,128)} %param.24) | copy-start | bytes 24580
  2.9 35.3 %copy-start.31 = (s32[256,8]{0,1:T(8,128)S(1)}, s32[256,8]{0,1:T(8,128)}, u32[]{:S(2)}) copy-start(s32[256,8]{0,1:T(8,128)} %param.25) | copy-start | bytes 24580
  39.6 16.6 %copy-start.5 = (bf16[256,1024]{1,0:T(8,128)(2,1)S(1)}, bf16[256,1024]{1,0:T(8,128)(2,1)}, u32[]{:S(2)}) copy-start(bf16[256,1024]{1,0:T(8,128)(2,1)} %param.14) | copy-start | bytes 1572868
  39.6 25.9 %collective-permute-start.4 = (bf16[64,1024]{1,0:T(8,128)(2,1)S(1)}, bf16[64,1024]{1,0:T(8,128)(2,1)S(1)}, u32[]{:S(2)}, u32[]{:S(2)}) collective-permute-start(bf16[64,1024]{1,0:T(8,128)(2,1)S(1)} %constant_dynamic-slice_fusion.1), channel_id=1, source_target_pairs={{0,24},{8,0},{16,8},{24,16},{1,25},{9,1},{17,9},{25,17},{2,26},{10... | collective-permute-start | bytes 393224 | tf_op jit(solution)/shard_map/ppermute | solution.py:266
  46.0 19.5 %collective-permute-start.5 = (bf16[64,1024]{1,0:T(8,128)(2,1)S(1)}, bf16[64,1024]{1,0:T(8,128)(2,1)S(1)}, u32[]{:S(2)}, u32[]{:S(2)}) collective-permute-start(bf16[64,1024]{1,0:T(8,128)(2,1)S(1)} %constant_dynamic-slice_fusion.1), channel_id=1, source_target_pairs={{0,16},{8,24},{16,0},{24,8},{1,17},{9,25},{17,1},{25,9},{2,18},{10... | collective-permute-start | bytes 393224 | tf_op jit(solution)/shard_map/ppermute | solution.py:266
  46.0 15.4 %collective-permute-start = (f32[16,256]{1,0:T(8,128)S(1)}, f32[16,256]{1,0:T(8,128)S(1)}, u32[]{:S(2)}, u32[]{:S(2)}) collective-permute-start(f32[16,256]{1,0:T(8,128)S(1)} %select_reduce_fusion), channel_id=1, source_target_pairs={{0,24},{8,0},{16,8},{24,16},{1,25},{9,1},{17,9},{25,17},{2,26},{10... | collective-permute-start | bytes 49160 | tf_op jit(solution)/shard_map/ppermute | solution.py:266
  46.1 17.4 %collective-permute-start.1 = (f32[16,256]{1,0:T(8,128)S(1)}, f32[16,256]{1,0:T(8,128)S(1)}, u32[]{:S(2)}, u32[]{:S(2)}) collective-permute-start(f32[16,256]{1,0:T(8,128)S(1)} %select_reduce_fusion), channel_id=1, source_target_pairs={{0,16},{8,24},{16,0},{24,8},{1,17},{9,25},{17,1},{25,9},{2,18},{10... | collective-permute-start | bytes 49160 | tf_op jit(solution)/shard_map/ppermute | solution.py:266
  48.9 16.0 %collective-permute-start.2 = (f32[16,256]{1,0:T(8,128)S(1)}, f32[16,256]{1,0:T(8,128)S(1)}, u32[]{:S(2)}, u32[]{:S(2)}) collective-permute-start(f32[16,256]{1,0:T(8,128)S(1)} %select_reduce_fusion), channel_id=1, source_target_pairs={{0,8},{8,16},{16,24},{24,0},{1,9},{9,17},{17,25},{25,1},{2,10},{10... | collective-permute-start | bytes 49160 | tf_op jit(solution)/shard_map/ppermute | solution.py:266
  50.9 64.9 %all-to-all-start = ((bf16[4,128,1536]{2,1,0:T(8,128)(2,1)}), bf16[4,128,1536]{2,1,0:T(8,128)(2,1)}, u32[]{:S(2)}, u32[]{:S(2)}) async-start(bf16[4,128,1536]{2,1,0:T(8,128)(2,1)} %pad_maximum_fusion.4), calls=%async_computation | async-start | bytes 3145728 | tf_op jit(solution)/shard_map/all_to_all | solution.py:358
  58.1 1.0 copy-start
  59.0 27.8 %copy-start.20 = (bf16[256,4,64]{0,2,1:T(8,128)(2,1)}, bf16[256,4,64]{0,2,1:T(8,128)(2,1)S(1)}, u32[]{:S(2)}) copy-start(bf16[256,4,64]{0,2,1:T(8,128)(2,1)S(1)} %pad_maximum_fusion.12) | copy-start | bytes 393220
  61.2 27.9 %copy-start.23 = (pred[256,512]{0,1:T(8,128)(4,1)}, pred[256,512]{0,1:T(8,128)(4,1)S(1)}, u32[]{:S(2)}) copy-start(pred[256,512]{0,1:T(8,128)(4,1)S(1)} %fusion.51) | copy-start | bytes 393220
  61.4 22.8 %collective-permute-start.6 = (bf16[64,1024]{1,0:T(8,128)(2,1)S(1)}, bf16[64,1024]{1,0:T(8,128)(2,1)S(1)}, u32[]{:S(2)}, u32[]{:S(2)}) collective-permute-start(bf16[64,1024]{1,0:T(8,128)(2,1)S(1)} %constant_dynamic-slice_fusion.1), channel_id=1, source_target_pairs={{0,8},{8,16},{16,24},{24,0},{1,9},{9,17},{17,25},{25,1},{2,10},{10... | collective-permute-start | bytes 393224 | tf_op jit(solution)/shard_map/ppermute | solution.py:266
  63.4 23.0 %collective-permute-start.3 = (bf16[256,256]{1,0:T(8,128)(2,1)S(1)}, bf16[256,256]{1,0:T(8,128)(2,1)S(1)}, u32[]{:S(2)}, u32[]{:S(2)}) collective-permute-start(bf16[256,256]{1,0:T(8,128)(2,1)S(1)} %pad_maximum_fusion.11), channel_id=1, source_target_pairs={{0,4},{4,0},{1,5},{5,1},{2,6},{6,2},{3,7},{7,3},{8,12},{12,8},{9,1... | collective-permute-start | bytes 393224 | tf_op jit(solution)/shard_map/ppermute | solution.py:249
  84.9 9.2 %collective-permute-start.7 = (bf16[4,64,1024]{2,1,0:T(8,128)(2,1)S(1)}, bf16[4,64,1024]{2,1,0:T(8,128)(2,1)S(1)}, u32[]{:S(2)}, u32[]{:S(2)}) collective-permute-start(bf16[4,64,1024]{2,1,0:T(8,128)(2,1)S(1)} %gather_fusion.2), channel_id=1, source_target_pairs={{0,2},{1,3},{2,0},{3,1},{4,6},{5,7},{6,4},{7,5},{8,10},{9,11},{10,... | collective-permute-start | bytes 1572872 | tf_op jit(solution)/shard_map/ppermute | solution.py:266
  86.7 7.5 %copy-start.25 = (bf16[512,128]{0,1:T(8,128)(2,1)}, bf16[512,128]{0,1:T(8,128)(2,1)S(1)}, u32[]{:S(2)}) copy-start(bf16[512,128]{0,1:T(8,128)(2,1)S(1)} %copy.84) | copy-start | bytes 393220
  86.8 8.1 %copy-start.10 = (bf16[512,128]{0,1:T(8,128)(2,1)}, bf16[512,128]{0,1:T(8,128)(2,1)S(1)}, u32[]{:S(2)}) copy-start(bf16[512,128]{0,1:T(8,128)(2,1)S(1)} %copy.83) | copy-start | bytes 393220
  94.2 0.9 copy-start.21
  94.9 12.0 %collective-permute-start.8 = (bf16[2,4,64,1024]{3,2,1,0:T(8,128)(2,1)S(1)}, bf16[2,4,64,1024]{3,2,1,0:T(8,128)(2,1)S(1)}, u32[]{:S(2)}, u32[]{:S(2)}) collective-permute-start(bf16[2,4,64,1024]{3,2,1,0:T(8,128)(2,1)S(1)} %gather_fusion.3), channel_id=1, source_target_pairs={{0,1},{1,0},{2,3},{3,2},{4,5},{5,4},{6,7},{7,6},{8,9},{9,8},{10,11... | collective-permute-start | bytes 3145736 | tf_op jit(solution)/shard_map/ppermute | solution.py:266
  97.3 1.5 copy-start.8
  106.9 1.0 copy-start.7
  185.3 4.8 %copy-start.2 = (bf16[4,2,128,1536]{3,2,1,0:T(8,128)(2,1)S(1)}, bf16[4,2,128,1536]{3,2,1,0:T(8,128)(2,1)}, u32[]{:S(2)}) copy-start(bf16[4,2,128,1536]{3,2,1,0:T(8,128)(2,1)} %copy.87) | copy-start | bytes 9437188
  192.2 2.4 copy-start.4
  197.0 3.6 %copy-start.1 = (bf16[4,2,128,1024]{3,2,0,1:T(8,128)(2,1)}, bf16[4,2,128,1024]{3,2,0,1:T(8,128)(2,1)S(1)}, u32[]{:S(2)}) copy-start(bf16[4,2,128,1024]{3,2,0,1:T(8,128)(2,1)S(1)} %fusion.16) | copy-start | bytes 6291460
  197.0 2.3 copy-start.3
  242.6 14.7 %copy-start.11 = (bf16[512,128]{0,1:T(8,128)(2,1)S(1)}, bf16[512,128]{0,1:T(8,128)(2,1)}, u32[]{:S(2)}) copy-start(bf16[512,128]{0,1:T(8,128)(2,1)} %copy-done.10) | copy-start | bytes 393220
  245.1 14.0 %copy-start.22 = (bf16[256,4,64]{0,2,1:T(8,128)(2,1)S(1)}, bf16[256,4,64]{0,2,1:T(8,128)(2,1)}, u32[]{:S(2)}) copy-start(bf16[256,4,64]{0,2,1:T(8,128)(2,1)} %copy-done.20) | copy-start | bytes 393220
  261.3 5.0 %copy-start.24 = (pred[256,512]{0,1:T(8,128)(4,1)S(1)}, pred[256,512]{0,1:T(8,128)(4,1)}, u32[]{:S(2)}) copy-start(pred[256,512]{0,1:T(8,128)(4,1)} %copy-done.23) | copy-start | bytes 393220
  274.1 4.8 %copy-start.18 = (f32[512,2,64]{0,2,1:T(8,128)S(1)}, f32[512,2,64]{0,2,1:T(8,128)}, u32[]{:S(2)}) copy-start(f32[512,2,64]{0,2,1:T(8,128)} %fusion.32) | copy-start | bytes 786436
  274.1 64.5 %all-to-all-start.1 = ((bf16[4,128,1536]{2,1,0:T(8,128)(2,1)}), bf16[4,128,1536]{2,1,0:T(8,128)(2,1)}, u32[]{:S(2)}, u32[]{:S(2)}) async-start(bf16[4,128,1536]{2,1,0:T(8,128)(2,1)} %fusion.4), calls=%async_computation.1 | async-start | bytes 3145728 | tf_op jit(solution)/shard_map/all_to_all | solution.py:468
  278.6 1.7 copy-start.17
  278.8 1.7 copy-start.15
  279.2 1.6 copy-start.9
  279.5 8.2 %collective-permute-start.9 = (f32[256,256]{0,1:T(8,128)S(1)}, f32[256,256]{0,1:T(8,128)S(1)}, u32[]{:S(2)}, u32[]{:S(2)}) collective-permute-start(f32[256,256]{0,1:T(8,128)S(1)} %copy.100), channel_id=1, source_target_pairs={{0,4},{4,0},{1,5},{5,1},{2,6},{6,2},{3,7},{7,3},{8,12},{12,8},{9,1... | collective-permute-start | bytes 786440 | tf_op jit(solution)/shard_map/ppermute | solution.py:249
  280.8 7.1 %copy-start.19 = (bf16[4,2,128,768]{3,2,1,0:T(8,128)(2,1)S(1)}, bf16[4,2,128,768]{3,2,1,0:T(8,128)(2,1)}, u32[]{:S(2)}) copy-start(bf16[4,2,128,768]{3,2,1,0:T(8,128)(2,1)} %get-tuple-element.28) | copy-start | bytes 4718596
  287.8 6.5 %copy-start.6 = (bf16[256,1024]{1,0:T(8,128)(2,1)S(1)}, bf16[256,1024]{1,0:T(8,128)(2,1)}, u32[]{:S(2)}) copy-start(bf16[256,1024]{1,0:T(8,128)(2,1)} %param.14) | copy-start | bytes 1572868
  343.5 2.2 copy-start.14
  344.6 1.9 copy-start.16

commit v3 on v2

--- a/solution.py
+++ b/solution.py
@@ -119,6 +119,7 @@
             pltpu.SemaphoreType.DMA((copies,)),
             pltpu.SemaphoreType.DMA((len(arrays),)),
         ],
+        cost_estimate=pl.CostEstimate(flops=0, bytes_accessed=60_000_000, transcendentals=0),
         compiler_params=pltpu.CompilerParams(collective_id=number, has_side_effects=True),
     )(*arrays)
 
@@ -168,7 +169,7 @@
         push(0, i)
     if side is not None:
         exchange = pltpu.make_async_remote_copy(
-            src_ref=given_ref.at[1 - coordinate(side)],
+            src_ref=given_ref.at[1],
             dst_ref=taken_ref,
             send_sem=side_send,
             recv_sem=side_recv,
@@ -238,6 +239,7 @@
             pltpu.SemaphoreType.DMA(((stages + 1) * n,)),
         ]
         + semaphores,
+        cost_estimate=pl.CostEstimate(flops=0, bytes_accessed=60_000_000, transcendentals=0),
         compiler_params=pltpu.CompilerParams(
             collective_id=number, has_side_effects=True, vmem_limit_bytes=VMEM_BYTES
         ),
@@ -253,20 +255,15 @@
     return jnp.where(place == 0, jnp.stack([array, other]), jnp.stack([other, array]))
 
 
-def by_fsdp(array, dim):
-    axis, size, stride = dim
-    count = lax.axis_size(axis)
-    place = coordinate(dim)
-    blocks = [array]
-    for k in range(1, size):
-        pairs = []
-        for i in range(count):
-            c = i // stride % size
-            pairs.append((i, i + ((c - k) % size - c) * stride))
-        blocks.append(lax.ppermute(array, axis, pairs))
-    stacked = jnp.stack(blocks)
-    order = lax.rem(jnp.arange(size, dtype=jnp.int32) - place + size, size)
-    return stacked[order]
+def own_first(rows, place, depth):
+    parts = jnp.swapaxes(rows.reshape(rows.shape[0], -1, 2, depth), 1, 2)
+    return jnp.where(place == 0, parts, parts[:, ::-1]).reshape(rows.shape)
+
+
+def in_order(rows, place, depth):
+    parts = rows.reshape(rows.shape[0], 2, -1, depth)
+    parts = jnp.where(place == 0, parts, parts[:, ::-1])
+    return jnp.swapaxes(parts, 1, 2).reshape(rows.shape)
 
 
 def rms_scale(values):
@@ -349,24 +346,19 @@
     gain_shard = jnp.pad(
         jnp.stack([norm_in, norm_mid]).astype(jnp.float32), ((0, 6), (0, 128 - depth))
     )
-    attn_weight, gains = gather_pieces(
-        [attn_shard, gain_shard], [[fsdp_all, context_dim]] * 2, 1
-    )
-    packed, cot_first, dense_gates, attn_weight = lax.optimization_barrier(
-        (packed, cot_piece, dense_gates, attn_weight)
-    )
+    attn_weight, gains, gates_all, cot_all = gather_pieces(
+        [attn_shard, gain_shard, dense_gates, own_first(cot_piece, context_index, depth)],
+        [[fsdp_all, context_dim]] * 2 + [[fsdp_dim], [fsdp_dim, y_dim, core_dim]],
+        1,
+    )
+    cot_all = cot_all.reshape(-1, model_width)
+    packed, attn_weight = lax.optimization_barrier((packed, attn_weight))
     from_fsdp = lax.all_to_all(packed, "fsdp", 0, 0, tiled=True)
-    cot_f = by_fsdp(cot_first, fsdp_dim)
-    cot_y = by_fsdp(cot_f, y_dim)
-    cot_t = by_fsdp(cot_y, core_dim)
-    cot_all = jnp.transpose(cot_t, (2, 1, 0, 3, 4)).reshape(-1, model_width)
-    gates_all = by_fsdp(dense_gates, fsdp_dim)
     gates_own = lax.dynamic_slice_in_dim(
         gates_all, coordinate(fsdp_dim) * per_owner, per_owner, 1
     )
     gates_rows = jnp.transpose(gates_own, (0, 2, 1)).reshape(-1, per_owner)
     gates_wide = jnp.repeat(gates_rows, hidden_width, axis=1)
-
     attn_weight = attn_weight.reshape(model_width, -1)
     gains = gains[..., :depth].reshape(-1, 8, depth)
     gain_one = gains[:, 0, :].reshape(-1)
@@ -423,6 +415,8 @@
     def by_tensor(part):
         return part.astype(jnp.bfloat16).reshape(tensor // 2, 2, piece, model_width)
 
+    attn_part, from_fsdp = lax.optimization_barrier((attn_part, from_fsdp))
+    from_context = swapped(from_fsdp, "context", 1)
     attended = reduce_pieces(by_tensor(attn_part), [core_dim], y_dim, 2)[0]
     start_row = tensor_index * piece
     own_inputs = lax.dynamic_slice_in_dim(tokens, start_row, piece, 0).astype(jnp.float32)
@@ -430,10 +424,10 @@
     hidden_state = own_inputs + attended
     scale_mid = rms_scale(hidden_state)
     normed_mid = (hidden_state * scale_mid * gain_two).astype(jnp.bfloat16)
-    expert_rows, both_context = gather_pieces(
-        [normed_mid, from_fsdp], [[fsdp_dim, y_dim, core_dim], [context_dim]], 3
-    )
-    expert_weight = jnp.swapaxes(both_context, 0, 1).reshape(model_width, 3 * columns)
+    (expert_rows,) = gather_pieces(
+        [own_first(normed_mid, context_index, depth)], [[fsdp_dim, y_dim, core_dim]], 3
+    )
+    expert_weight = jnp.concatenate([from_fsdp, from_context]).reshape(model_width, 3 * columns)
     gate_up_weight = expert_weight[:, : 2 * columns]
     down_weight = expert_weight[:, 2 * columns :]
     expert_rows = expert_rows.reshape(-1, model_width)
@@ -459,8 +453,8 @@
     )
     grad_down = lax.dot_general(cot_all, hidden, CONTRACT_ROWS, preferred_element_type=jnp.float32)
     expert_grad = jnp.concatenate([grad_gate_up, grad_down], axis=1).astype(jnp.bfloat16)
-    expert_grad = jnp.swapaxes(expert_grad.reshape(fsdp, -1, depth, 3 * columns), 0, 1)
-    kept = lax.dynamic_index_in_dim(expert_grad, context_index, 0, False)
+    expert_grad = expert_grad.reshape(2, fsdp, depth, 3 * columns)
+    kept = expert_grad[0]
     back, taken = reduce_pieces(
         both_parts, [core_dim, y_dim], fsdp_dim, 4, expert_grad, context_dim
     )
@@ -471,6 +465,7 @@
         3, EXPERTS, depth, hidden_width
     )
 
+    back = in_order(back, context_index, depth)
     moe_mixed, d_mid = back[:piece], back[piece:]
     own_output = (hidden_state + moe_mixed).astype(jnp.bfloat16)
     d_gain_mid = jnp.sum(d_mid * hidden_state * scale_mid, axis=0)

time: 348 us -> 306 us (0.88)
  Pallas kernels: 196 us -> 168 us
  local copies, waits for them, and re-layouts: 37.4 us -> 27.4 us
  starting transfers between devices: 26.2 us -> 18.2 us
    pallas_call x4, Pallas kernels: 114 us -> 86.2 us  [gather_pieces(): pl.pallas_call(functools.partial(gather_kernel, jobs), out_shape=tuple(sh...]
    ppermute x8 -> x0, waiting for transfers between devices: 23.7 us -> none  [by_fsdp(): blocks.append(lax.ppermute(array, axis, pairs))]
    all_to_all x1, waiting for transfers between devices: 0.01 us -> 21.5 us  [local(): from_fsdp = lax.all_to_all(packed, 'fsdp', 0, 0, tiled=True)]
    ppermute x8 -> x0, starting transfers between devices: 15 us -> none  [by_fsdp(): blocks.append(lax.ppermute(array, axis, pairs))]
    dot_general x2 -> x0, local copies, waits for them, and re-layouts: 6.61 us -> none  [the longest x1 3.94 us: local(): lax.dot_general(expert_rows, d_act, CONTRACT_ROWS, preferred_element_type...]
    transpose x2 -> x0, local copies, waits for them, and re-layouts: 5.62 us -> none  [the longest x1 3.77 us: local(): jnp.swapaxes(both_context, 0, 1).reshape(model_width, 3 * columns)]
    ppermute x2 -> x3, waiting for transfers between devices: 6.59 us -> 11.6 us  [swapped(): return lax.ppermute(array, axis, [(i, i ^ step) for i in range(size)])]
    all_to_all x1, starting transfers between devices: 4.33 us -> 8.93 us  [local(): from_fsdp = lax.all_to_all(packed, 'fsdp', 0, 0, tiled=True)]
  transfers between devices with their start and end apart: 12 -> 5, of which waited for: 3 -> 4; matrix products, arithmetic and copies ran while one was open for 9% -> 7% of each run, Pallas kernels for 15% -> 24%
where the time goes in v3:
time: 306 us; the launch traced here: 305 us
  Pallas kernels  168 us (55%)
  matrix products  36.9 us (12%)
  waiting for transfers between devices  33.1 us (11%)
  local copies, waits for them, and re-layouts  27.4 us (9%)
  other arithmetic  20 us (7%)
  starting transfers between devices  18.2 us (6%)
    pallas_call x4, Pallas kernels, gather_pieces(): pl.pallas_call(functools.partial(gather_kernel, jobs), out_shape=tuple(sh...  86.2 us
    pallas_call x4, Pallas kernels, reduce_pieces(): pl.pallas_call(functools.partial(reduce_kernel, tuple(halves), last, side...  81.3 us
    all_to_all x1, waiting for transfers between devices, local(): from_fsdp = lax.all_to_all(packed, 'fsdp', 0, 0, tiled=True)  21.5 us
    ppermute x3, waiting for transfers between devices, swapped(): return lax.ppermute(array, axis, [(i, i ^ step) for i in range(size)])  11.6 us
    all_to_all x1, starting transfers between devices, local(): from_fsdp = lax.all_to_all(packed, 'fsdp', 0, 0, tiled=True)  8.93 us
  transfers between devices with their start and end apart: 5, of which 4 were waited for; matrix products, arithmetic and copies ran while one was open for 7% of the time, Pallas kernels for 24%

profile of v3, /device:TPU:0, one launch (start us, length us, event | category | flops | bytes accessed | tf_op | source)
XLA Modules:
  0.0 304.7 jit_solution(2184271111026831572)
XLA Ops:
  0.7 1.0 constant_dynamic-slice_fusion.1
  1.8 0.7 rev.9
  2.7 0.7 reshape.378.refs_3_
  3.4 1.3 copy.97
  6.6 1.2 pad_maximum_fusion.5
  7.9 0.7 pad_maximum_fusion.9.refs_0_
  8.6 45.1 %shard_map.221 = (bf16[4,2,128,768]{3,2,1,0:T(8,128)(2,1)}, f32[4,2,8,128]{3,2,1,0:T(8,128)}, f32[4,16,256]{2,1,0:T(8,128)}, bf16[4,2,2,64,1024]{4,3,2,1,0:T(8,128)(2,1)}) custom-call(bf16[128,768]{1,0:T(8,128)(2,1)} %pad_maximum_fusion.9.refs_0_, f32[8,128]{1,0:T(8,128)} %fusion.55.refs_1_, f32[16,256]{1,0:T(8,128)} %select_reduce_fusion.refs_2_, ...), custom_call_target="tpu_custom_call" | custom-call | bytes 60000000 | tf_op jit(solution)/shard_map/pallas_call | solution.py:112
  53.8 8.9 %all-to-all-start = ((bf16[4,128,1536]{1,2,0:T(8,128)(2,1)}), bf16[4,128,1536]{1,2,0:T(8,128)(2,1)S(1)}, u32[]{:S(2)}, u32[]{:S(2)}) async-start(bf16[4,128,1536]{1,2,0:T(8,128)(2,1)} %pad_maximum_fusion.5), calls=%async_computation | async-start | bytes 3145728 | tf_op jit(solution)/shard_map/all_to_all | solution.py:356
  62.7 0.8 fusion.72
  63.8 1.7 fusion.30
  66.0 0.7 pad_maximum_fusion.10
  66.7 1.5 collective-permute-start
  68.4 1.9 gather_fusion
  70.7 1.8 collective-permute-done
  72.6 1.1 maximum_select_fusion
  73.9 2.2 fusion.73
  76.1 1.1 convolution_convert_fusion.8
  77.3 1.4 fusion.36
  78.7 21.5 %all-to-all-done = bf16[4,128,1536]{1,2,0:T(8,128)(2,1)S(1)} async-done(((bf16[4,128,1536]{1,2,0:T(8,128)(2,1)}), bf16[4,128,1536]{1,2,0:T(8,128)(2,1)S(1)}, u32[]{:S(2)}, u32[]{:S(2)}) %all-to-all-start) | async-done | bytes 1572896 | tf_op jit(solution)/shard_map/all_to_all | solution.py:356
  100.2 1.5 collective-permute-start.1
  101.8 0.8 constant_dynamic-slice_fusion
  102.6 5.9 %shard_map.222 = f32[64,1024]{1,0:T(8,128)S(1)} custom-call(bf16[2,2,64,1024]{3,2,1,0:T(8,128)(2,1)S(1)} %bitcast.189), custom_call_target="tpu_custom_call" | custom-call | bytes 60000000 | tf_op jit(solution)/shard_map/pallas_call | solution.py:229
  108.8 0.7 rev.10
  109.7 0.7 reshape.396.refs_0_
  110.4 21.7 %shard_map.223 = bf16[4,2,2,64,1024]{4,3,2,1,0:T(8,128)(2,1)} custom-call(bf16[64,1024]{1,0:T(8,128)(2,1)} %reshape.396.refs_0_), custom_call_target="tpu_custom_call" | custom-call | bytes 60000000 | tf_op jit(solution)/shard_map/pallas_call | solution.py:112
  132.2 3.8 %collective-permute-done.1 = bf16[4,128,1536]{1,2,0:T(8,128)(2,1)} collective-permute-done((bf16[4,128,1536]{1,2,0:T(8,128)(2,1)S(1)}, bf16[4,128,1536]{1,2,0:T(8,128)(2,1)}, u32[]{:S(2)}, u32[]{:S(2)}) %collective-permute-start.1) | collective-permute-done | bytes 1572896 | tf_op jit(solution)/shard_map/ppermute | solution.py:251
  136.0 2.2 pad_maximum_fusion.1
  138.1 2.8 copy.108
  141.0 4.8 %fusion.12 = f32[1024,1024]{0,1:T(8,128)S(1)} fusion(bf16[1024,1024]{1,0:T(8,128)(2,1)} %bitcast.203, bf16[1024,1536]{1,0:T(8,128)(2,1)} %bitcast.196), kind=kOutput, calls=%fused_computation.31 | convolution fusion | flops 2147483648 | bytes 8388608 | tf_op jit(solution)/shard_map/dot_general | solution.py:434
  145.8 2.2 multiply_convert_fusion.1
  147.9 1.3 convolution_convert_fusion.4
  149.2 1.3 convolution_convert_fusion.2
  150.8 2.4 convolution_convert_fusion
  153.2 2.4 convolution_convert_fusion.1
  155.6 1.3 pad_maximum_fusion.4
  157.3 2.6 pad_maximum_fusion.refs_0_
  160.0 39.0 %shard_map.224 = (f32[128,1024]{1,0:T(8,128)S(1)}, bf16[4,128,1536]{2,1,0:T(8,128)(2,1)S(1)}) custom-call(bf16[4,2,2,128,1024]{4,3,2,1,0:T(8,128)(2,1)} %pad_maximum_fusion.refs_0_, bf16[2,4,128,1536]{3,2,1,0:T(8,128)(2,1)S(1)} %pad_maximum_fusion.2.refs_1_), custom_call_target="tpu_custom_call" | custom-call | bytes 60000000 | tf_op jit(solution)/shard_map/pallas_call | solution.py:229
  199.5 1.4 rev.11
  201.7 0.8 multiply_reduce_fusion
  202.6 1.8 fusion.66
  204.4 10.0 %shard_map.225 = (bf16[2,2,64,1024]{3,2,1,0:T(8,128)(2,1)}, bf16[2,2,64,1024]{3,2,1,0:T(8,128)(2,1)}) custom-call(bf16[64,1024]{1,0:T(8,128)(2,1)} %get-tuple-element.45.refs_0_, bf16[64,1024]{1,0:T(8,128)(2,1)} %get-tuple-element.69.refs_1_), custom_call_target="tpu_custom_call" | custom-call | bytes 60000000 | tf_op jit(solution)/shard_map/pallas_call | solution.py:112
  214.4 1.5 convolution_convert_fusion.7
  216.0 1.9 fusion.74
  217.9 1.9 convolution_bitcast_fusion
  219.8 4.2 %convolution_multiply_fusion = f32[2,64,2,256]{3,1,2,0:T(8,128)S(1)} fusion(bf16[512,2,64,1]{0,2,3,1:T(8,128)(2,1)S(1)} %bitcast.245, f32[2,512,256,2]{2,1,3,0:T(8,128)} %fusion.74, pred[256,512]{0,1:T(8,128)(4,1)S(1)} %copy-done.22, f32[2,2,256,512]{2,3,1,0:T(8,128)} %get-tuple-element.84, f32[2,2,256]{2,1,0:T(2,128)S(1)} %get-tuple-element.83), kind=kOutput, calls=%fused_computation.46 | convolution fusion | flops 70845952 | bytes 4722688 | tf_op jit(solution)/shard_map/kgrs,skd->rkgd/dot_general | solution.py:497
  224.0 5.1 %fusion.16 = f32[512,2,64]{0,2,1:T(8,128)} fusion(bf16[256,2,2,64]{0,3,2,1:T(8,128)(2,1)} %bitcast.240, f32[2,512,256,2]{2,1,3,0:T(8,128)} %fusion.74, pred[256,512]{0,1:T(8,128)(4,1)} %copy-done.21, f32[2,2,256,512]{2,3,1,0:T(8,128)} %get-tuple-element.84, f32[2,2,256]{2,1,0:T(2,128)S(1)} %get-tuple-element.83), kind=kOutput, calls=%fused_computation.45 | convolution fusion | flops 70845952 | bytes 4722688 | tf_op jit(solution)/shard_map/kgrs,rkgd->skd/dot_general | solution.py:501
  229.1 1.6 fusion.3
  230.7 4.7 %all-to-all-start.1 = ((bf16[4,128,1536]{2,1,0:T(8,128)(2,1)}), bf16[4,128,1536]{2,1,0:T(8,128)(2,1)}, u32[]{:S(2)}, u32[]{:S(2)}) async-start(bf16[4,128,1536]{2,1,0:T(8,128)(2,1)} %fusion.3), calls=%async_computation.1 | async-start | bytes 3145728 | tf_op jit(solution)/shard_map/all_to_all | solution.py:462
  236.3 1.5 collective-permute-start.2
  238.6 5.9 %collective-permute-done.2 = f32[256,256]{0,1:T(8,128)S(1)} collective-permute-done((f32[256,256]{0,1:T(8,128)S(1)}, f32[256,256]{0,1:T(8,128)S(1)}, u32[]{:S(2)}, u32[]{:S(2)}) %collective-permute-start.2) | collective-permute-done | bytes 262176 | tf_op jit(solution)/shard_map/ppermute | solution.py:251
  245.2 6.9 %shard_map.226 = f32[64,1024]{1,0:T(8,128)S(1)} custom-call(bf16[2,2,64,1024]{3,2,1,0:T(8,128)(2,1)S(1)} %bitcast.190), custom_call_target="tpu_custom_call" | custom-call | bytes 60000000 | tf_op jit(solution)/shard_map/pallas_call | solution.py:229
  252.9 0.8 fusion.40.refs_0_
  253.6 9.3 %shard_map.227 = (bf16[2,2,64,1024]{3,2,1,0:T(8,128)(2,1)}, f32[2,2,8,1024]{3,2,1,0:T(8,128)}) custom-call(bf16[64,1024]{1,0:T(8,128)(2,1)} %fusion.40.refs_0_, f32[8,1024]{1,0:T(8,128)} %select_maximum_fusion.refs_1_), custom_call_target="tpu_custom_call" | custom-call | bytes 60000000 | tf_op jit(solution)/shard_map/pallas_call | solution.py:112
  263.0 0.9 reduce_sum.105
  264.6 29.6 %shard_map.228 = f32[144,768]{1,0:T(8,128)S(1)} custom-call(bf16[4,2,144,768]{3,2,1,0:T(8,128)(2,1)S(1)} %fusion.14.refs_0_), custom_call_target="tpu_custom_call" | custom-call | bytes 60000000 | tf_op jit(solution)/shard_map/pallas_call | solution.py:229
  294.7 0.7 fusion.70
  295.4 0.7 fusion.69
  296.1 3.0 reshape.410
  299.1 0.7 fusion.67
  299.8 1.1 copy.120
  300.9 1.1 copy.121
  302.0 1.1 copy.122
  303.2 0.8 copy.136
  303.9 0.8 copy.137
  (140 shorter events, 10.4 us)
Async XLA Ops:
  0.6 4.1 %copy-start.13 = (bf16[16,128,128]{2,1,0:T(8,128)(2,1)S(1)}, bf16[16,128,128]{2,1,0:T(8,128)(2,1)}, u32[]{:S(2)}) copy-start(bf16[16,128,128]{2,1,0:T(8,128)(2,1)} %param.20) | copy-start | bytes 1572868
  0.7 4.4 %copy-start.14 = (bf16[16,128,128]{2,1,0:T(8,128)(2,1)S(1)}, bf16[16,128,128]{2,1,0:T(8,128)(2,1)}, u32[]{:S(2)}) copy-start(bf16[16,128,128]{2,1,0:T(8,128)(2,1)} %param.21) | copy-start | bytes 1572868
  2.4 2.9 copy-start.31
  2.4 2.9 copy-start.32
  2.4 3.6 %copy-start.33 = (bf16[128]{0:T(256)(128)(2,1)S(1)}, bf16[128]{0:T(256)(128)(2,1)}, u32[]{:S(2)}) copy-start(bf16[128]{0:T(256)(128)(2,1)} %param.23) | copy-start | bytes 772
  2.5 3.6 %copy-start.34 = (bf16[128]{0:T(256)(128)(2,1)S(1)}, bf16[128]{0:T(256)(128)(2,1)}, u32[]{:S(2)}) copy-start(bf16[128]{0:T(256)(128)(2,1)} %param.22) | copy-start | bytes 772
  5.0 2.9 copy-start.27
  5.0 2.8 copy-start.28
  5.1 2.8 copy-start.29
  5.1 2.8 copy-start.30
  7.9 55.7 %copy-start.6 = (bf16[256,1024]{1,0:T(8,128)(2,1)S(1)}, bf16[256,1024]{1,0:T(8,128)(2,1)}, u32[]{:S(2)}) copy-start(bf16[256,1024]{1,0:T(8,128)(2,1)} %param.14) | copy-start | bytes 1572868
  53.8 46.5 %all-to-all-start = ((bf16[4,128,1536]{1,2,0:T(8,128)(2,1)}), bf16[4,128,1536]{1,2,0:T(8,128)(2,1)S(1)}, u32[]{:S(2)}, u32[]{:S(2)}) async-start(bf16[4,128,1536]{1,2,0:T(8,128)(2,1)} %pad_maximum_fusion.5), calls=%async_computation | async-start | bytes 3145728 | tf_op jit(solution)/shard_map/all_to_all | solution.py:356
  63.7 4.6 %copy-start = (s32[1,512]{1,0:T(1,128)S(1)}, s32[1,512]{1,0:T(1,128)}, u32[]{:S(2)}) copy-start(s32[1,512]{1,0:T(1,128)} %param.26) | copy-start | bytes 6148
  66.7 5.9 %collective-permute-start = (bf16[256,256]{1,0:T(8,128)(2,1)}, bf16[256,256]{1,0:T(8,128)(2,1)}, u32[]{:S(2)}, u32[]{:S(2)}) collective-permute-start(bf16[256,256]{1,0:T(8,128)(2,1)} %pad_maximum_fusion.10), channel_id=1, source_target_pairs={{0,4},{4,0},{1,5},{5,1},{2,6},{6,2},{3,7},{7,3},{8,12},{12,8},{9,1... | collective-permute-start | bytes 393224 | tf_op jit(solution)/shard_map/ppermute | solution.py:251
  70.6 5.5 %copy-start.21 = (pred[256,512]{0,1:T(8,128)(4,1)}, pred[256,512]{0,1:T(8,128)(4,1)S(1)}, u32[]{:S(2)}) copy-start(pred[256,512]{0,1:T(8,128)(4,1)S(1)} %fusion.34) | copy-start | bytes 393220
  70.7 5.3 %copy-start.23 = (bf16[256,4,64]{0,2,1:T(8,128)(2,1)}, bf16[256,4,64]{0,2,1:T(8,128)(2,1)S(1)}, u32[]{:S(2)}) copy-start(bf16[256,4,64]{0,2,1:T(8,128)(2,1)S(1)} %pad_maximum_fusion.11) | copy-start | bytes 393220
  73.8 3.5 %copy-start.25 = (bf16[512,128]{0,1:T(8,128)(2,1)}, bf16[512,128]{0,1:T(8,128)(2,1)S(1)}, u32[]{:S(2)}) copy-start(bf16[512,128]{0,1:T(8,128)(2,1)S(1)} %copy.104) | copy-start | bytes 393220
  73.9 3.4 %copy-start.11 = (bf16[512,128]{0,1:T(8,128)(2,1)}, bf16[512,128]{0,1:T(8,128)(2,1)S(1)}, u32[]{:S(2)}) copy-start(bf16[512,128]{0,1:T(8,128)(2,1)S(1)} %copy.103) | copy-start | bytes 393220
  77.2 32.4 %copy-start.9 = (bf16[2,64,2,256]{3,1,2,0:T(8,128)(2,1)}, bf16[2,64,2,256]{3,1,2,0:T(8,128)(2,1)S(1)}, u32[]{:S(2)}) copy-start(bf16[2,64,2,256]{3,1,2,0:T(8,128)(2,1)S(1)} %convolution_convert_fusion.8) | copy-start | bytes 393220
  100.2 31.9 %copy-start.1 = (bf16[4,128,1536]{1,2,0:T(8,128)(2,1)}, bf16[4,128,1536]{1,2,0:T(8,128)(2,1)S(1)}, u32[]{:S(2)}) copy-start(bf16[4,128,1536]{1,2,0:T(8,128)(2,1)S(1)} %all-to-all-done) | copy-start | bytes 4718596
  100.2 35.7 %collective-permute-start.1 = (bf16[4,128,1536]{1,2,0:T(8,128)(2,1)S(1)}, bf16[4,128,1536]{1,2,0:T(8,128)(2,1)}, u32[]{:S(2)}, u32[]{:S(2)}) collective-permute-start(bf16[4,128,1536]{1,2,0:T(8,128)(2,1)S(1)} %all-to-all-done), channel_id=1, source_target_pairs={{0,4},{4,0},{1,5},{5,1},{2,6},{6,2},{3,7},{7,3},{8,12},{12,8},{9,1... | collective-permute-start | bytes 4718600 | tf_op jit(solution)/shard_map/ppermute | solution.py:251
  141.0 4.8 %copy-start.3 = (bf16[8,128,1536]{2,1,0:T(8,128)(2,1)S(1)}, bf16[8,128,1536]{2,1,0:T(8,128)(2,1)}, u32[]{:S(2)}) copy-start(bf16[8,128,1536]{2,1,0:T(8,128)(2,1)} %copy.108) | copy-start | bytes 9437188
  141.0 4.8 %copy-start.4 = (bf16[4,2,2,64,1024]{4,3,2,1,0:T(8,128)(2,1)S(1)}, bf16[4,2,2,64,1024]{4,3,2,1,0:T(8,128)(2,1)}, u32[]{:S(2)}) copy-start(bf16[4,2,2,64,1024]{4,3,2,1,0:T(8,128)(2,1)} %get-tuple-element.32) | copy-start | bytes 6291460
  149.2 1.6 copy-start.5
  201.5 14.5 %copy-start.12 = (bf16[512,128]{0,1:T(8,128)(2,1)S(1)}, bf16[512,128]{0,1:T(8,128)(2,1)}, u32[]{:S(2)}) copy-start(bf16[512,128]{0,1:T(8,128)(2,1)} %copy-done.11) | copy-start | bytes 393220
  204.3 13.5 %copy-start.22 = (pred[256,512]{0,1:T(8,128)(4,1)S(1)}, pred[256,512]{0,1:T(8,128)(4,1)}, u32[]{:S(2)}) copy-start(pred[256,512]{0,1:T(8,128)(4,1)} %copy-done.21) | copy-start | bytes 393220
  204.3 13.5 %copy-start.24 = (bf16[256,4,64]{0,2,1:T(8,128)(2,1)S(1)}, bf16[256,4,64]{0,2,1:T(8,128)(2,1)}, u32[]{:S(2)}) copy-start(bf16[256,4,64]{0,2,1:T(8,128)(2,1)} %copy-done.23) | copy-start | bytes 393220
  204.3 13.5 %copy-start.26 = (bf16[512,128]{0,1:T(8,128)(2,1)S(1)}, bf16[512,128]{0,1:T(8,128)(2,1)}, u32[]{:S(2)}) copy-start(bf16[512,128]{0,1:T(8,128)(2,1)} %copy-done.25) | copy-start | bytes 393220
  224.0 5.2 %copy-start.2 = (bf16[512,1536]{1,0:T(8,128)(2,1)S(1)}, bf16[512,1536]{1,0:T(8,128)(2,1)}, u32[]{:S(2)}) copy-start(bf16[512,1536]{1,0:T(8,128)(2,1)} %pad_maximum_fusion.4) | copy-start | bytes 4718596
  230.7 4.8 %copy-start.18 = (f32[512,2,64]{0,2,1:T(8,128)S(1)}, f32[512,2,64]{0,2,1:T(8,128)}, u32[]{:S(2)}) copy-start(f32[512,2,64]{0,2,1:T(8,128)} %convolution_bitcast_fusion) | copy-start | bytes 786436
  230.7 5.1 %copy-start.19 = (f32[512,2,64]{0,2,1:T(8,128)S(1)}, f32[512,2,64]{0,2,1:T(8,128)}, u32[]{:S(2)}) copy-start(f32[512,2,64]{0,2,1:T(8,128)} %fusion.16) | copy-start | bytes 786436
  230.7 65.4 %all-to-all-start.1 = ((bf16[4,128,1536]{2,1,0:T(8,128)(2,1)}), bf16[4,128,1536]{2,1,0:T(8,128)(2,1)}, u32[]{:S(2)}, u32[]{:S(2)}) async-start(bf16[4,128,1536]{2,1,0:T(8,128)(2,1)} %fusion.3), calls=%async_computation.1 | async-start | bytes 3145728 | tf_op jit(solution)/shard_map/all_to_all | solution.py:462
  235.6 2.4 copy-start.16
  236.0 2.3 copy-start.10
  236.3 8.2 %collective-permute-start.2 = (f32[256,256]{0,1:T(8,128)S(1)}, f32[256,256]{0,1:T(8,128)S(1)}, u32[]{:S(2)}, u32[]{:S(2)}) collective-permute-start(f32[256,256]{0,1:T(8,128)S(1)} %copy.116), channel_id=1, source_target_pairs={{0,4},{4,0},{1,5},{5,1},{2,6},{6,2},{3,7},{7,3},{8,12},{12,8},{9,1... | collective-permute-start | bytes 786440 | tf_op jit(solution)/shard_map/ppermute | solution.py:251
  238.3 6.4 %copy-start.20 = (bf16[4,2,128,768]{3,2,1,0:T(8,128)(2,1)S(1)}, bf16[4,2,128,768]{3,2,1,0:T(8,128)(2,1)}, u32[]{:S(2)}) copy-start(bf16[4,2,128,768]{3,2,1,0:T(8,128)(2,1)} %get-tuple-element.28) | copy-start | bytes 4718596
  244.6 7.5 %copy-start.7 = (bf16[256,1024]{1,0:T(8,128)(2,1)S(1)}, bf16[256,1024]{1,0:T(8,128)(2,1)}, u32[]{:S(2)}) copy-start(bf16[256,1024]{1,0:T(8,128)(2,1)} %param.14) | copy-start | bytes 1572868
  244.6 8.2 %copy-start.8 = (f32[64,1024]{1,0:T(8,128)S(1)}, f32[64,1024]{1,0:T(8,128)}, u32[]{:S(2)}) copy-start(f32[64,1024]{1,0:T(8,128)} %get-tuple-element.46) | copy-start | bytes 786436
  300.9 2.2 copy-start.15
  302.0 1.9 copy-start.17

commit v4 on v3

--- a/solution.py
+++ b/solution.py
@@ -459,12 +459,6 @@
         both_parts, [core_dim, y_dim], fsdp_dim, 4, expert_grad, context_dim
     )
     half_grad = (kept.astype(jnp.float32) + taken.astype(jnp.float32)).astype(jnp.bfloat16)
-    owned_grad = lax.all_to_all(half_grad, "fsdp", 0, 0, tiled=True).astype(jnp.float32)
-    owned_grad = jnp.sum(owned_grad.reshape(groups, copies, depth, 3, per_owner, hidden_width), 1)
-    owned_grad = jnp.transpose(owned_grad, (2, 0, 3, 1, 4)).reshape(
-        3, EXPERTS, depth, hidden_width
-    )
-
     back = in_order(back, context_index, depth)
     moe_mixed, d_mid = back[:piece], back[piece:]
     own_output = (hidden_state + moe_mixed).astype(jnp.bfloat16)
@@ -476,8 +470,16 @@
         * scale_mid**3
         * jnp.mean(gain_two * d_mid * hidden_state, axis=-1, keepdims=True)
     )
+    own_attended, half_grad = lax.optimization_barrier(
+        (d_hidden_state.astype(jnp.bfloat16), half_grad)
+    )
+    owned_grad = lax.all_to_all(half_grad, "fsdp", 0, 0, tiled=True).astype(jnp.float32)
+    owned_grad = jnp.sum(owned_grad.reshape(groups, copies, depth, 3, per_owner, hidden_width), 1)
+    owned_grad = jnp.transpose(owned_grad, (2, 0, 3, 1, 4)).reshape(
+        3, EXPERTS, depth, hidden_width
+    )
     d_attended, output = gather_pieces(
-        [d_hidden_state.astype(jnp.bfloat16), own_output], [[y_dim, core_dim]] * 2, 5
+        [own_attended, own_output], [[y_dim, core_dim]] * 2, 5
     )
     d_attended = d_attended.reshape(local_rows, model_width)
     output = output.reshape(local_rows, model_width)

time: 306 us -> 307 us (level)
  matrix products: 36.9 us -> 31.4 us
  local copies, waits for them, and re-layouts: 27.4 us -> 32.8 us
  waiting for transfers between devices: 33.1 us -> 28.2 us
    ppermute x3, waiting for transfers between devices: 11.6 us -> 6.62 us  [swapped(): return lax.ppermute(array, axis, [(i, i ^ step) for i in range(size)])]
    slice x3, local copies, waits for them, and re-layouts: 0.46 us -> 4.55 us  [local(): moe_mixed, d_mid = (back[:piece], back[piece:])]
    pallas_call x4, Pallas kernels: 81.3 us -> 85.2 us  [reduce_pieces(): pl.pallas_call(functools.partial(reduce_kernel, tuple(halves), last, side...]
  transfers between devices with their start and end apart: 5 -> 5, of which waited for: 4 -> 4; matrix products, arithmetic and copies ran while one was open for 7% -> 7% of each run, Pallas kernels for 24% -> 25%
where the time goes in v4:
time: 307 us; the launch traced here: 306 us
  Pallas kernels  171 us (56%)
  local copies, waits for them, and re-layouts  32.8 us (11%)
  matrix products  31.4 us (10%)
  waiting for transfers between devices  28.2 us (9%)
  other arithmetic  22.2 us (7%)
  starting transfers between devices  18.4 us (6%)
    pallas_call x4, Pallas kernels, gather_pieces(): pl.pallas_call(functools.partial(gather_kernel, jobs), out_shape=tuple(sh...  86.2 us
    pallas_call x4, Pallas kernels, reduce_pieces(): pl.pallas_call(functools.partial(reduce_kernel, tuple(halves), last, side...  85.2 us
    all_to_all x1, waiting for transfers between devices, local(): from_fsdp = lax.all_to_all(packed, 'fsdp', 0, 0, tiled=True)  21.5 us
    all_to_all x1, starting transfers between devices, local(): from_fsdp = lax.all_to_all(packed, 'fsdp', 0, 0, tiled=True)  8.93 us
    ppermute x3, waiting for transfers between devices, swapped(): return lax.ppermute(array, axis, [(i, i ^ step) for i in range(size)])  6.62 us
  transfers between devices with their start and end apart: 5, of which 4 were waited for; matrix products, arithmetic and copies ran while one was open for 7% of the time, Pallas kernels for 25%

profile of v4, /device:TPU:0, one launch (start us, length us, event | category | flops | bytes accessed | tf_op | source)
XLA Modules:
  0.0 306.0 jit_solution(2983003686326610407)
XLA Ops:
  0.7 1.0 constant_dynamic-slice_fusion.1
  2.7 0.7 reshape.378.refs_3_
  3.4 1.3 copy.97
  6.6 1.2 pad_maximum_fusion.5
  7.9 0.7 pad_maximum_fusion.9.refs_0_
  8.6 45.1 %shard_map.221 = (bf16[4,2,128,768]{3,2,1,0:T(8,128)(2,1)}, f32[4,2,8,128]{3,2,1,0:T(8,128)}, f32[4,16,256]{2,1,0:T(8,128)}, bf16[4,2,2,64,1024]{4,3,2,1,0:T(8,128)(2,1)}) custom-call(bf16[128,768]{1,0:T(8,128)(2,1)} %pad_maximum_fusion.9.refs_0_, f32[8,128]{1,0:T(8,128)} %fusion.55.refs_1_, f32[16,256]{1,0:T(8,128)} %select_reduce_fusion.refs_2_, ...), custom_call_target="tpu_custom_call" | custom-call | bytes 60000000 | tf_op jit(solution)/shard_map/pallas_call | solution.py:112
  53.8 8.9 %all-to-all-start = ((bf16[4,128,1536]{1,2,0:T(8,128)(2,1)}), bf16[4,128,1536]{1,2,0:T(8,128)(2,1)S(1)}, u32[]{:S(2)}, u32[]{:S(2)}) async-start(bf16[4,128,1536]{1,2,0:T(8,128)(2,1)} %pad_maximum_fusion.5), calls=%async_computation | async-start | bytes 3145728 | tf_op jit(solution)/shard_map/all_to_all | solution.py:356
  62.7 0.8 fusion.72
  63.8 1.7 fusion.30
  66.0 0.7 pad_maximum_fusion.10
  66.7 1.5 collective-permute-start
  68.4 1.9 gather_fusion
  70.7 1.8 collective-permute-done
  72.5 1.1 maximum_select_fusion
  73.9 2.2 fusion.73
  76.1 1.1 convolution_convert_fusion.8
  77.3 1.4 fusion.36
  78.7 21.5 %all-to-all-done = bf16[4,128,1536]{1,2,0:T(8,128)(2,1)S(1)} async-done(((bf16[4,128,1536]{1,2,0:T(8,128)(2,1)}), bf16[4,128,1536]{1,2,0:T(8,128)(2,1)S(1)}, u32[]{:S(2)}, u32[]{:S(2)}) %all-to-all-start) | async-done | bytes 1572896 | tf_op jit(solution)/shard_map/all_to_all | solution.py:356
  100.2 1.5 collective-permute-start.1
  101.8 0.8 constant_dynamic-slice_fusion
  102.6 5.9 %shard_map.222 = f32[64,1024]{1,0:T(8,128)S(1)} custom-call(bf16[2,2,64,1024]{3,2,1,0:T(8,128)(2,1)S(1)} %bitcast.189), custom_call_target="tpu_custom_call" | custom-call | bytes 60000000 | tf_op jit(solution)/shard_map/pallas_call | solution.py:229
  109.7 0.7 reshape.396.refs_0_
  110.4 21.7 %shard_map.223 = bf16[4,2,2,64,1024]{4,3,2,1,0:T(8,128)(2,1)} custom-call(bf16[64,1024]{1,0:T(8,128)(2,1)} %reshape.396.refs_0_), custom_call_target="tpu_custom_call" | custom-call | bytes 60000000 | tf_op jit(solution)/shard_map/pallas_call | solution.py:112
  132.1 3.8 %collective-permute-done.1 = bf16[4,128,1536]{1,2,0:T(8,128)(2,1)} collective-permute-done((bf16[4,128,1536]{1,2,0:T(8,128)(2,1)S(1)}, bf16[4,128,1536]{1,2,0:T(8,128)(2,1)}, u32[]{:S(2)}, u32[]{:S(2)}) %collective-permute-start.1) | collective-permute-done | bytes 1572896 | tf_op jit(solution)/shard_map/ppermute | solution.py:251
  136.0 2.2 pad_maximum_fusion.1
  138.1 2.9 copy.108
  141.0 4.8 %fusion.12 = f32[1024,1024]{0,1:T(8,128)S(1)} fusion(bf16[1024,1024]{1,0:T(8,128)(2,1)} %bitcast.203, bf16[1024,1536]{1,0:T(8,128)(2,1)} %bitcast.196), kind=kOutput, calls=%fused_computation.31 | convolution fusion | flops 2147483648 | bytes 8388608 | tf_op jit(solution)/shard_map/dot_general | solution.py:434
  145.8 2.2 multiply_convert_fusion.1
  148.0 1.3 convolution_convert_fusion.4
  149.3 1.3 convolution_convert_fusion.2
  150.9 2.4 convolution_convert_fusion
  153.2 2.4 convolution_convert_fusion.1
  155.6 1.3 pad_maximum_fusion.4
  157.4 2.6 pad_maximum_fusion.refs_0_
  160.0 39.0 %shard_map.224 = (f32[128,1024]{1,0:T(8,128)S(1)}, bf16[4,128,1536]{2,1,0:T(8,128)(2,1)S(1)}) custom-call(bf16[4,2,2,128,1024]{4,3,2,1,0:T(8,128)(2,1)} %pad_maximum_fusion.refs_0_, bf16[2,4,128,1536]{3,2,1,0:T(8,128)(2,1)S(1)} %pad_maximum_fusion.2.refs_1_), custom_call_target="tpu_custom_call" | custom-call | bytes 60000000 | tf_op jit(solution)/shard_map/pallas_call | solution.py:229
  200.1 2.2 rev.11
  202.3 1.5 select_bitcast_fusion
  203.8 0.8 fusion.68
  204.6 1.9 slice.138
  206.4 1.9 slice.141
  208.3 1.8 multiply_reduce_fusion
  210.2 1.6 fusion.3
  211.8 1.7 fusion.66
  213.5 10.0 %shard_map.225 = (bf16[2,2,64,1024]{3,2,1,0:T(8,128)(2,1)}, bf16[2,2,64,1024]{3,2,1,0:T(8,128)(2,1)}) custom-call(bf16[64,1024]{1,0:T(8,128)(2,1)} %get-tuple-element.37.refs_0_, bf16[64,1024]{1,0:T(8,128)(2,1)} %get-tuple-element.73.refs_1_), custom_call_target="tpu_custom_call" | custom-call | bytes 60000000 | tf_op jit(solution)/shard_map/pallas_call | solution.py:112
  223.5 1.6 convolution_convert_fusion.7
  225.6 1.2 convolution_bitcast_fusion
  226.8 3.0 convolution_multiply_fusion
  229.8 3.0 fusion.16
  233.7 1.7 collective-permute-start.2
  235.6 4.8 %all-to-all-start.1 = ((bf16[4,128,1536]{2,1,0:T(8,128)(2,1)}), bf16[4,128,1536]{2,1,0:T(8,128)(2,1)}, u32[]{:S(2)}, u32[]{:S(2)}) async-start(bf16[4,128,1536]{2,1,0:T(8,128)(2,1)} %fusion.3), calls=%async_computation.1 | async-start | bytes 3145728 | tf_op jit(solution)/shard_map/all_to_all | solution.py:476
  240.9 1.0 collective-permute-done.2
  242.5 6.9 %shard_map.226 = f32[64,1024]{1,0:T(8,128)S(1)} custom-call(bf16[2,2,64,1024]{3,2,1,0:T(8,128)(2,1)S(1)} %bitcast.190), custom_call_target="tpu_custom_call" | custom-call | bytes 60000000 | tf_op jit(solution)/shard_map/pallas_call | solution.py:229
  250.2 0.8 fusion.40.refs_0_
  251.0 9.3 %shard_map.227 = (bf16[2,2,64,1024]{3,2,1,0:T(8,128)(2,1)}, f32[2,2,8,1024]{3,2,1,0:T(8,128)}) custom-call(bf16[64,1024]{1,0:T(8,128)(2,1)} %fusion.40.refs_0_, f32[8,1024]{1,0:T(8,128)} %select_maximum_fusion.refs_1_), custom_call_target="tpu_custom_call" | custom-call | bytes 60000000 | tf_op jit(solution)/shard_map/pallas_call | solution.py:112
  260.3 0.9 reduce_sum.105
  262.0 33.5 %shard_map.228 = f32[144,768]{1,0:T(8,128)S(1)} custom-call(bf16[4,2,144,768]{3,2,1,0:T(8,128)(2,1)S(1)} %fusion.14.refs_0_), custom_call_target="tpu_custom_call" | custom-call | bytes 60000000 | tf_op jit(solution)/shard_map/pallas_call | solution.py:229
  296.6 0.7 fusion.69
  297.3 3.0 reshape.410
  300.3 0.7 fusion.67
  301.1 1.1 copy.120
  302.2 1.1 copy.121
  303.3 1.1 copy.122
  304.4 0.8 copy.136
  305.2 0.8 copy.137
  (138 shorter events, 12.6 us)
Async XLA Ops:
  0.6 4.1 %copy-start.14 = (bf16[16,128,128]{2,1,0:T(8,128)(2,1)S(1)}, bf16[16,128,128]{2,1,0:T(8,128)(2,1)}, u32[]{:S(2)}) copy-start(bf16[16,128,128]{2,1,0:T(8,128)(2,1)} %param.20) | copy-start | bytes 1572868
  0.7 4.4 %copy-start.15 = (bf16[16,128,128]{2,1,0:T(8,128)(2,1)S(1)}, bf16[16,128,128]{2,1,0:T(8,128)(2,1)}, u32[]{:S(2)}) copy-start(bf16[16,128,128]{2,1,0:T(8,128)(2,1)} %param.21) | copy-start | bytes 1572868
  2.4 2.9 copy-start.30
  2.4 2.9 copy-start.31
  2.4 3.6 %copy-start.32 = (bf16[128]{0:T(256)(128)(2,1)S(1)}, bf16[128]{0:T(256)(128)(2,1)}, u32[]{:S(2)}) copy-start(bf16[128]{0:T(256)(128)(2,1)} %param.23) | copy-start | bytes 772
  2.5 3.6 %copy-start.33 = (bf16[128]{0:T(256)(128)(2,1)S(1)}, bf16[128]{0:T(256)(128)(2,1)}, u32[]{:S(2)}) copy-start(bf16[128]{0:T(256)(128)(2,1)} %param.22) | copy-start | bytes 772
  5.0 2.9 copy-start.26
  5.0 2.8 copy-start.27
  5.1 2.8 copy-start.28
  5.1 2.8 copy-start.29
  7.9 55.7 %copy-start.8 = (bf16[256,1024]{1,0:T(8,128)(2,1)S(1)}, bf16[256,1024]{1,0:T(8,128)(2,1)}, u32[]{:S(2)}) copy-start(bf16[256,1024]{1,0:T(8,128)(2,1)} %param.14) | copy-start | bytes 1572868
  53.8 46.5 %all-to-all-start = ((bf16[4,128,1536]{1,2,0:T(8,128)(2,1)}), bf16[4,128,1536]{1,2,0:T(8,128)(2,1)S(1)}, u32[]{:S(2)}, u32[]{:S(2)}) async-start(bf16[4,128,1536]{1,2,0:T(8,128)(2,1)} %pad_maximum_fusion.5), calls=%async_computation | async-start | bytes 3145728 | tf_op jit(solution)/shard_map/all_to_all | solution.py:356
  63.7 4.6 %copy-start = (s32[1,512]{1,0:T(1,128)S(1)}, s32[1,512]{1,0:T(1,128)}, u32[]{:S(2)}) copy-start(s32[1,512]{1,0:T(1,128)} %param.26) | copy-start | bytes 6148
  66.7 5.9 %collective-permute-start = (bf16[256,256]{1,0:T(8,128)(2,1)}, bf16[256,256]{1,0:T(8,128)(2,1)}, u32[]{:S(2)}, u32[]{:S(2)}) collective-permute-start(bf16[256,256]{1,0:T(8,128)(2,1)} %pad_maximum_fusion.10), channel_id=1, source_target_pairs={{0,4},{4,0},{1,5},{5,1},{2,6},{6,2},{3,7},{7,3},{8,12},{12,8},{9,1... | collective-permute-start | bytes 393224 | tf_op jit(solution)/shard_map/ppermute | solution.py:251
  70.6 5.5 %copy-start.20 = (pred[256,512]{0,1:T(8,128)(4,1)}, pred[256,512]{0,1:T(8,128)(4,1)S(1)}, u32[]{:S(2)}) copy-start(pred[256,512]{0,1:T(8,128)(4,1)S(1)} %fusion.34) | copy-start | bytes 393220
  70.7 5.3 %copy-start.22 = (bf16[256,4,64]{0,2,1:T(8,128)(2,1)}, bf16[256,4,64]{0,2,1:T(8,128)(2,1)S(1)}, u32[]{:S(2)}) copy-start(bf16[256,4,64]{0,2,1:T(8,128)(2,1)S(1)} %pad_maximum_fusion.11) | copy-start | bytes 393220
  73.7 3.5 %copy-start.24 = (bf16[512,128]{0,1:T(8,128)(2,1)}, bf16[512,128]{0,1:T(8,128)(2,1)S(1)}, u32[]{:S(2)}) copy-start(bf16[512,128]{0,1:T(8,128)(2,1)S(1)} %copy.104) | copy-start | bytes 393220
  73.9 3.4 %copy-start.12 = (bf16[512,128]{0,1:T(8,128)(2,1)}, bf16[512,128]{0,1:T(8,128)(2,1)S(1)}, u32[]{:S(2)}) copy-start(bf16[512,128]{0,1:T(8,128)(2,1)S(1)} %copy.103) | copy-start | bytes 393220
  77.3 32.4 %copy-start.10 = (bf16[2,64,2,256]{3,1,2,0:T(8,128)(2,1)}, bf16[2,64,2,256]{3,1,2,0:T(8,128)(2,1)S(1)}, u32[]{:S(2)}) copy-start(bf16[2,64,2,256]{3,1,2,0:T(8,128)(2,1)S(1)} %convolution_convert_fusion.8) | copy-start | bytes 393220
  100.2 31.9 %copy-start.1 = (bf16[4,128,1536]{1,2,0:T(8,128)(2,1)}, bf16[4,128,1536]{1,2,0:T(8,128)(2,1)S(1)}, u32[]{:S(2)}) copy-start(bf16[4,128,1536]{1,2,0:T(8,128)(2,1)S(1)} %all-to-all-done) | copy-start | bytes 4718596
  100.2 35.7 %collective-permute-start.1 = (bf16[4,128,1536]{1,2,0:T(8,128)(2,1)S(1)}, bf16[4,128,1536]{1,2,0:T(8,128)(2,1)}, u32[]{:S(2)}, u32[]{:S(2)}) collective-permute-start(bf16[4,128,1536]{1,2,0:T(8,128)(2,1)S(1)} %all-to-all-done), channel_id=1, source_target_pairs={{0,4},{4,0},{1,5},{5,1},{2,6},{6,2},{3,7},{7,3},{8,12},{12,8},{9,1... | collective-permute-start | bytes 4718600 | tf_op jit(solution)/shard_map/ppermute | solution.py:251
  141.0 4.8 %copy-start.3 = (bf16[8,128,1536]{2,1,0:T(8,128)(2,1)S(1)}, bf16[8,128,1536]{2,1,0:T(8,128)(2,1)}, u32[]{:S(2)}) copy-start(bf16[8,128,1536]{2,1,0:T(8,128)(2,1)} %copy.108) | copy-start | bytes 9437188
  141.0 4.8 %copy-start.6 = (bf16[4,2,2,64,1024]{4,3,2,1,0:T(8,128)(2,1)S(1)}, bf16[4,2,2,64,1024]{4,3,2,1,0:T(8,128)(2,1)}, u32[]{:S(2)}) copy-start(bf16[4,2,2,64,1024]{4,3,2,1,0:T(8,128)(2,1)} %get-tuple-element.34) | copy-start | bytes 6291460
  149.3 1.6 copy-start.7
  199.3 0.8 copy-start.4
  202.3 7.9 %copy-start.2 = (bf16[512,1536]{1,0:T(8,128)(2,1)S(1)}, bf16[512,1536]{1,0:T(8,128)(2,1)}, u32[]{:S(2)}) copy-start(bf16[512,1536]{1,0:T(8,128)(2,1)} %pad_maximum_fusion.4) | copy-start | bytes 4718596
  210.2 1.6 copy-start.5
  211.8 13.3 %copy-start.13 = (bf16[512,128]{0,1:T(8,128)(2,1)S(1)}, bf16[512,128]{0,1:T(8,128)(2,1)}, u32[]{:S(2)}) copy-start(bf16[512,128]{0,1:T(8,128)(2,1)} %copy-done.12) | copy-start | bytes 393220
  213.5 12.1 %copy-start.21 = (pred[256,512]{0,1:T(8,128)(4,1)S(1)}, pred[256,512]{0,1:T(8,128)(4,1)}, u32[]{:S(2)}) copy-start(pred[256,512]{0,1:T(8,128)(4,1)} %copy-done.20) | copy-start | bytes 393220
  213.5 12.1 %copy-start.23 = (bf16[256,4,64]{0,2,1:T(8,128)(2,1)S(1)}, bf16[256,4,64]{0,2,1:T(8,128)(2,1)}, u32[]{:S(2)}) copy-start(bf16[256,4,64]{0,2,1:T(8,128)(2,1)} %copy-done.22) | copy-start | bytes 393220
  213.5 12.1 %copy-start.25 = (bf16[512,128]{0,1:T(8,128)(2,1)S(1)}, bf16[512,128]{0,1:T(8,128)(2,1)}, u32[]{:S(2)}) copy-start(bf16[512,128]{0,1:T(8,128)(2,1)} %copy-done.24) | copy-start | bytes 393220
  232.8 2.5 copy-start.18
  233.7 8.2 %collective-permute-start.2 = (f32[256,256]{0,1:T(8,128)S(1)}, f32[256,256]{0,1:T(8,128)S(1)}, u32[]{:S(2)}, u32[]{:S(2)}) collective-permute-start(f32[256,256]{0,1:T(8,128)S(1)} %copy.116), channel_id=1, source_target_pairs={{0,4},{4,0},{1,5},{5,1},{2,6},{6,2},{3,7},{7,3},{8,12},{12,8},{9,1... | collective-permute-start | bytes 786440 | tf_op jit(solution)/shard_map/ppermute | solution.py:251
  235.6 5.0 %copy-start.11 = (bf16[2,64,2,256]{3,1,2,0:T(8,128)(2,1)S(1)}, bf16[2,64,2,256]{3,1,2,0:T(8,128)(2,1)}, u32[]{:S(2)}) copy-start(bf16[2,64,2,256]{3,1,2,0:T(8,128)(2,1)} %copy-done.10) | copy-start | bytes 393220
  235.6 61.8 %all-to-all-start.1 = ((bf16[4,128,1536]{2,1,0:T(8,128)(2,1)}), bf16[4,128,1536]{2,1,0:T(8,128)(2,1)}, u32[]{:S(2)}, u32[]{:S(2)}) async-start(bf16[4,128,1536]{2,1,0:T(8,128)(2,1)} %fusion.3), calls=%async_computation.1 | async-start | bytes 3145728 | tf_op jit(solution)/shard_map/all_to_all | solution.py:476
  240.5 1.5 copy-start.19
  241.9 7.5 %copy-start.9 = (bf16[256,1024]{1,0:T(8,128)(2,1)S(1)}, bf16[256,1024]{1,0:T(8,128)(2,1)}, u32[]{:S(2)}) copy-start(bf16[256,1024]{1,0:T(8,128)(2,1)} %param.14) | copy-start | bytes 1572868
  302.2 2.2 copy-start.16
  303.3 1.9 copy-start.17
